TPU v7x, 256 devices: a whole 4x4x8 slice. The times are simulated.
256 devices in a mesh: ctx: 32 (over x, y, core), tp: 8 (over z).
Axes of the slice: x: 4, y: 4, z: 8, core: 2. Of those that a mesh axis runs over, the one named last changes fastest.
Arguments:
- ctx_queries: bfloat16 [16384, 8192], P('ctx', 'tp'), may hold values from -100 to 100
- ctx_keyvals: bfloat16 [2, 16384, 1024], P(None, 'ctx', 'tp'), may hold values from -4 to 4
- block_map: int32 [64], replicated, may hold values from 0 to 63, as said below
- window_reach: int32 [2], replicated, may hold values from 16 to 32
- win_queries: bfloat16 [2, 256, 8192], P(None, None, 'tp'), may hold values from -100 to 100
- win_keyvals: bfloat16 [2, 2, 256, 1024], P(None, None, None, 'tp'), may hold values from -4 to 4
- out_weight: bfloat16 [8192, 8192], P('tp', 'ctx'), may hold values from -0.25 to 0.25
Outputs:
- context_attn: bfloat16 [16384, 8192], P('ctx', 'tp')
- window_proj: float32 [512, 8192], P('tp', 'ctx')
Inputs may be any that keep to these rules, and one draw needn't show every extreme that they name: `block_map`: each logical block of 0 to 63 appears exactly once; blocks c * 32 to (c + 1) * 32 - 1 make context c; of the row blocks 2 i and 2 i + 1 one holds a block of context 0 and the other a block of context 1.
All inputs are finite; a program needn't handle non-finite values.
Results may differ from a plain program's by a relative error of at most 0.0035.
Values may be sent and summed in bfloat16 or wider, within the bound.
No kernel may reach another device: no remote copies, remote signals or barrier semaphores. Data moves between devices by JAX's collectives and lax.ppermute only.
A program may use at most 192 MiB of HBM per device.

v0:
```python
import math

import jax
import jax.numpy as jnp
from jax import lax
from jax.sharding import PartitionSpec as P

HQ = 64
HK = 8
HD = 128


masked_score = -1e30


def spread(value, axis, source):
    kept = jnp.where(lax.axis_index(axis) == source, value, 0).astype(value.dtype)
    return lax.psum(kept, axis)


def partial_softmax(query_rows, key_rows, value_rows, count_mask):
    row_count = query_rows.shape[0]
    key_heads = key_rows.shape[1] // HD
    groups = HQ // HK
    query_split = query_rows.reshape(row_count, key_heads, groups, HD)
    key_split = key_rows.reshape(-1, key_heads, HD)
    value_split = value_rows.reshape(-1, key_heads, HD)
    scores = jnp.einsum(
        "rhgd,khd->rhgk", query_split, key_split, preferred_element_type=jnp.float32
    ) / math.sqrt(HD)
    live_mask = count_mask[:, None, None, :]
    scores = jnp.where(live_mask, scores, masked_score)
    row_top = jnp.max(scores, axis=-1)
    weights = jnp.where(live_mask, jnp.exp(scores - row_top[..., None]), 0.0)
    row_total = jnp.sum(weights, axis=-1)
    weights_low = weights.astype(jnp.bfloat16)
    weighted = jnp.einsum(
        "rhgk,khd->rhgd", weights_low, value_split, preferred_element_type=jnp.float32
    )
    return (
        row_top.reshape(row_count, -1),
        row_total.reshape(row_count, -1),
        weighted.reshape(row_count, -1),
    )


def combine_parts(former, latter):
    joined_top = jnp.maximum(former[0], latter[0])
    former_lift = jnp.exp(former[0] - joined_top)
    latter_lift = jnp.exp(latter[0] - joined_top)
    joined_total = former[1] * former_lift + latter[1] * latter_lift
    joined_sum = former[2] * jnp.repeat(former_lift, HD, axis=-1) + latter[2] * jnp.repeat(
        latter_lift, HD, axis=-1
    )
    return (joined_top, joined_total, joined_sum)


def finish_rows(parts):
    return parts[2] / jnp.repeat(parts[1], HD, axis=-1)


def anchor_slots(block_map, block_count):
    slot_ids = jnp.arange(block_map.shape[0], dtype=jnp.int32)
    firsts = jnp.arange(2, dtype=jnp.int32) * block_count
    hits = (block_map[None, :] == firsts[:, None]).astype(jnp.int32)
    return jnp.sum(hits * slot_ids[None, :], axis=1)


def lower_mask(length):
    return jnp.arange(length)[:, None] >= jnp.arange(length)[None, :]


def on_device(
    ctx_queries, ctx_keyvals, block_map, window_reach, win_queries, win_keyvals, out_weight
):
    block_len = ctx_queries.shape[0] // 2
    block_count = block_map.shape[0] // 2
    window_len = win_queries.shape[1]
    head_cols = win_queries.shape[2] // HD
    position = lax.axis_index("ctx")
    own_blocks = lax.dynamic_slice_in_dim(block_map, position * 2, 2)
    anchors = anchor_slots(block_map, block_count)
    gathered = []
    for context_id in range(2):
        holder = anchors[context_id]
        anchor_piece = lax.dynamic_slice_in_dim(ctx_keyvals, holder % 2 * block_len, block_len, 1)
        gathered.append(spread(anchor_piece, "ctx", holder // 2))
    anchor_all = jnp.stack(gathered, 0)
    causal = lower_mask(block_len)
    empty_part = (
        jnp.full((window_len, head_cols), masked_score, jnp.float32),
        jnp.zeros((window_len, head_cols), jnp.float32),
        jnp.zeros((window_len, head_cols * HD), jnp.float32),
    )
    window_parts = [empty_part, empty_part]
    block_outs = []
    for which_slot in range(2):
        block_id = own_blocks[which_slot]
        context_id = block_id // block_count
        anchor_kv = lax.dynamic_index_in_dim(anchor_all, context_id, 0, keepdims=False)
        own_kv = ctx_keyvals[:, which_slot * block_len : (which_slot + 1) * block_len]
        query_rows = ctx_queries[which_slot * block_len : (which_slot + 1) * block_len]
        key_rows = jnp.concatenate([anchor_kv[0], own_kv[0]], 0)
        value_rows = jnp.concatenate([anchor_kv[1], own_kv[1]], 0)
        anchor_seen = jnp.broadcast_to(block_id % block_count != 0, (block_len, block_len))
        block_parts = partial_softmax(
            query_rows, key_rows, value_rows, jnp.concatenate([anchor_seen, causal], 1)
        )
        block_outs.append(finish_rows(block_parts).astype(jnp.bfloat16))
        window_query = lax.dynamic_index_in_dim(win_queries, context_id, 0, keepdims=False)
        reach_limit = lax.dynamic_index_in_dim(window_reach, context_id, 0, keepdims=False)
        live_block = block_id % block_count < reach_limit
        slot_part = partial_softmax(
            window_query,
            own_kv[0],
            own_kv[1],
            jnp.broadcast_to(live_block, (window_len, block_len)),
        )
        for target in range(2):
            matches = context_id == target
            masked = tuple(
                (jnp.where(matches, taken, blank) for taken, blank in zip(slot_part, empty_part))
            )
            window_parts[target] = combine_parts(window_parts[target], masked)
    stacked_parts = tuple(
        (jnp.stack([window_parts[0][member], window_parts[1][member]]) for member in range(3))
    )
    window_causal = lower_mask(window_len)
    own_parts = [
        partial_softmax(
            win_queries[context_id],
            win_keyvals[context_id, 0],
            win_keyvals[context_id, 1],
            window_causal,
        )
        for context_id in range(2)
    ]
    own_stacked = tuple(
        (jnp.stack([own_parts[0][member], own_parts[1][member]]) for member in range(3))
    )
    global_top = lax.pmax(stacked_parts[0], "ctx")
    lift_factor = jnp.exp(stacked_parts[0] - global_top)
    summed = lax.psum(
        (stacked_parts[1] * lift_factor, stacked_parts[2] * jnp.repeat(lift_factor, HD, axis=-1)),
        "ctx",
    )
    merged = (global_top, summed[0], summed[1])
    final_parts = combine_parts(merged, own_stacked)
    window_attn = finish_rows(final_parts).astype(jnp.bfloat16).reshape(2 * window_len, -1)
    window_proj = lax.psum_scatter(
        jnp.dot(window_attn, out_weight, preferred_element_type=jnp.float32),
        "tp",
        scatter_dimension=0,
        tiled=True,
    )
    return (jnp.concatenate(block_outs, 0), window_proj)


def solution(mesh):
    return jax.shard_map(
        on_device,
        mesh=mesh,
        in_specs=(
            P("ctx", "tp"),
            P(None, "ctx", "tp"),
            P(),
            P(),
            P(None, None, "tp"),
            P(None, None, None, "tp"),
            P("tp", "ctx"),
        ),
        out_specs=(P("ctx", "tp"), P("tp", "ctx")),
        check_vma=False,
    )
```

profile of v0, /device:TPU:1, one launch (start us, length us, event | category | flops | bytes accessed | tf_op | source)
XLA Modules:
  0.0 399.0 jit_solution(9054087357862916269)
XLA Ops:
  7.2 0.9 fusion.128
  8.1 0.6 fusion.157
  13.9 1.7 select_bitcast_fusion
  15.8 0.7 dynamic_slice.32
  16.5 0.6 fusion.156
  22.3 1.3 fusion.155
  23.6 2.6 constant_dynamic-slice_fusion.1
  28.9 1.0 fusion.27
  29.9 0.6 broadcast_select_fusion.2
  30.6 2.0 broadcast_select_fusion.3
  32.6 0.6 fusion.122
  33.2 2.5 copy.131
  35.7 2.5 copy.141
  38.3 1.3 copy.138
  39.6 1.3 copy.144
  40.9 124.4 %pmax.7 = f32[2,256,8]{1,2,0:T(8,128)S(1)} all-reduce(f32[2,256,8]{1,2,0:T(8,128)S(1)} %pad_maximum_fusion.1), channel_id=1, replica_groups=mesh['ctx'=32,'tp'=8] {'ctx'}, use_global_device_ids=true, to_apply=%region_9.10 | all-reduce | flops 4096 | bytes 32768 | tf_op jit(solution)/shard_map/pmax | solution.py:141
  166.3 0.8 copy.139
  167.1 0.6 maximum_multiply_fusion.2
  167.8 1.2 broadcast_in_dim.185
  169.1 1.1 mul_broadcast_in_dim.51
  170.5 1.2 reshape.632
  172.1 1.1 mul_broadcast_in_dim.49
  173.6 1.2 reshape.627
  175.1 1.2 reshape.633
  176.6 1.2 reshape.634
  178.1 1.1 reshape.631
  179.6 1.1 reshape.629
  180.7 2.0 broadcast_in_dim.190
  182.7 1.7 reshape.635
  184.4 6.3 %multiply_add_fusion = (f32[1,256,1024]{2,1,0:T(8,128)S(1)}, f32[1,256,1024]{2,1,0:T(8,128)S(1)}) fusion(f32[1,256,1024]{2,1,0:T(8,128)} %copy.144, f32[1,256,1024]{2,1,0:T(8,128)} %reshape.634, f32[1,256,1024]{2,1,0:T(8,128)} %reshape.633, f32[1,256,1024]{2,1,0:T(8,128)} %mul_broadcast_in_dim.51, f32[1,256,1024]{2,1,0:T(8,128)} %copy.141, ...), kind=kLoop, calls=%fused_computation.64 | loop fusion | flops 2621440 | bytes 14680064 | tf_op jit(solution)/shard_map/add | solution.py:52
  190.7 1.7 maximum_multiply_fusion
  192.6 0.7 slice_bitcast_fusion.3
  194.4 1.7 fusion.41
  196.1 0.9 fusion.23
  197.0 0.5 fusion.25
  197.5 2.6 fusion.38
  200.4 1.0 copy.180
  201.4 1.3 copy.155
  202.8 1.3 copy.156
  204.1 124.5 %psum.31 = f32[2,256,8]{1,2,0:T(8,128)S(1)} all-reduce(f32[2,256,8]{1,2,0:T(8,128)S(1)} %copy-done.11), channel_id=1, replica_groups=mesh['ctx'=32,'tp'=8] {'ctx'}, use_global_device_ids=true, to_apply=%region_15.16 | all-reduce | flops 4096 | bytes 32768 | tf_op jit(solution)/shard_map/psum | solution.py:143
  328.7 0.8 copy.150
  329.6 0.8 copy.157
  330.4 1.5 broadcast_in_dim.194
  331.9 1.5 reshape.645
  333.5 1.5 broadcast_in_dim.193
  335.0 1.5 reshape.640
  336.5 0.6 broadcast_in_dim.196
  337.1 1.5 reshape.646
  338.8 0.9 constant_dynamic-update-slice_fusion.1
  339.7 0.9 constant_dynamic-update-slice_fusion
  340.7 1.9 fusion.1
  342.6 1.2 fusion.16
  343.8 0.7 copy-done.2
  344.5 1.3 copy.124
  345.8 0.8 fusion
  346.6 2.0 copy-done.1
  348.6 0.6 copy-done.3
  349.2 2.0 fusion.2
  351.3 4.7 %fusion.18 = bf16[2,256,1024]{2,1,0:T(8,128)(2,1)S(1)} fusion(f32[2,256,1024]{2,1,0:T(8,128)} %reshape.646, f32[2,256,1024]{2,1,0:T(8,128)S(1)} %copy-done.4, f32[1,256,1024]{2,1,0:T(8,128)} %copy.156, f32[1,256,1024]{2,1,0:T(8,128)} %copy.155, f32[2,256,1024]{2,1,0:T(8,128)} %all-reduce.6.cloned.1.call-done, f32[2,256,1024]{2,1,0:T(8,128)} %reshape.640), kind=kLoop, calls=%fused_computation.32 | loop fusion | flops 3145728 | bytes 11534336 | tf_op jit(solution)/shard_map/convert_element_type | solution.py:149
  355.9 1.3 fusion.158
  357.2 4.4 %fusion.14 = f32[128,256,8]{1,0,2:T(8,128)} fusion(f32[512,256,8]{1,0,2:T(8,128)} %copy-done.1, f32[256,8]{0,1:T(8,128)S(1)} %get-tuple-element.53, pred[256,512]{0,1:T(8,128)(4,1)S(1)} %get-tuple-element.31, bf16[256,128]{1,0:T(8,128)(2,1)S(1)} %copy-done.12, bf16[256,128]{1,0:T(8,128)(2,1)S(1)} %get-tuple-element.21), kind=kOutput, calls=%fused_computation.30 | convolution fusion | flops 273940480 | bytes 5513216 | tf_op jit(solution)/shard_map/rhgk,khd->rhgd/dot_general | solution.py:37
  361.6 1.6 copy.118
  364.9 1.0 pad_maximum_fusion
  365.9 26.6 %reduce-scatter.2.cloned.1.call-done = f32[64,256]{1,0:T(8,128)} async-done(((f32[512,256]{1,0:T(8,128)}), f32[64,256]{1,0:T(8,128)}) %reduce-scatter.2.cloned.1.call-update) | async-done | bytes 65552 | tf_op jit(solution)/shard_map/reduce_scatter | solution.py:150
  (77 shorter events, 8.1 us)
Async XLA Ops:
  7.2 348.8 %copy-start = (bf16[1024,256]{1,0:T(8,128)(2,1)S(1)}, bf16[1024,256]{1,0:T(8,128)(2,1)}, u32[]{:S(2)}) copy-start(bf16[1024,256]{1,0:T(8,128)(2,1)} %param.13) | copy-start | bytes 1572868
  7.2 331.6 %all-reduce.8.cloned.1.call-start = ((), (), s32[]{:S(2)}) async-start(), calls=%async_computation.3 | async-start | bytes 524288 | tf_op jit(solution)/shard_map/psum | solution.py:18
  15.7 335.5 %all-reduce.6.cloned.1.call-start = ((), (), s32[]{:S(2)}) async-start(), calls=%async_computation.1 | async-start | bytes 4194304 | tf_op jit(solution)/shard_map/psum | solution.py:143
  26.3 1.7 copy-start.7
  39.6 126.6 %copy-start.15 = (f32[256,8]{0,1:T(8,128)S(1)}, f32[256,8]{0,1:T(8,128)}, u32[]{:S(2)}) copy-start(f32[256,8]{0,1:T(8,128)} %get-tuple-element.43) | copy-start | bytes 24580
  39.6 126.7 %copy-start.14 = (f32[256,8]{0,1:T(8,128)S(1)}, f32[256,8]{0,1:T(8,128)}, u32[]{:S(2)}) copy-start(f32[256,8]{0,1:T(8,128)} %get-tuple-element.44) | copy-start | bytes 24580
  192.4 1.1 copy-start.6
  192.4 1.5 copy-start.16
  192.5 200.0 %reduce-scatter.2.cloned.1.call-start = ((), (), s32[]{:S(2)}) async-start(), calls=%async_computation.2 | async-start | bytes 589824 | tf_op jit(solution)/shard_map/reduce_scatter | solution.py:150
  197.5 2.6 copy-start.8
  200.2 1.2 copy-start.9
  201.4 1.3 copy-start.10
  201.4 2.6 copy-start.11
  340.6 1.9 copy-start.13
  342.5 2.0 copy-start.2
  345.8 3.3 copy-start.3
  346.6 2.0 copy-start.1
  349.2 2.1 copy-start.4
  355.9 1.3 copy-start.12
  361.6 2.3 copy-start.5
Sparse Core Ops, SparseCore 0:
  15.8 115.1 all-reduce.7
  192.6 120.3 all-reduce.5
  357.3 35.1 reduce-scatter.1
where the time goes:
time: 404 us; the launch traced here: 399 us
  blocking collectives  249 us (62%)
  local copies, waits for them, and re-layouts  56.8 us (14%)
  waiting for transfers between devices  26.7 us (7%)
  between operations  26 us (6%)
  other arithmetic  21.9 us (5%)
  matrix products  18.7 us (5%)
    psum x1, blocking collectives, on_device(): lax.psum((stacked_parts[1] * lift_factor, stacked_parts[2] * jnp.repeat(l...  124 us
    pmax x1, blocking collectives, on_device(): global_top = lax.pmax(stacked_parts[0], 'ctx')  124 us
    reduce_scatter x1, waiting for transfers between devices, on_device(): lax.psum_scatter(jnp.dot(window_attn, out_weight, preferred_element_type=...  26.6 us
    dot_general x6, matrix products, partial_softmax(): jnp.einsum('rhgk,khd->rhgd', weights_low, value_split, preferred_element_...  12.5 us
  transfers between devices with their start and end apart: 3, of which 1 were waited for; matrix products, arithmetic and copies ran while one was open for 21% of the time, Pallas kernels for 0%

commit v1 on v0

v1 whole, which is shorter than its diff:
```python
import math

import jax
import jax.numpy as jnp
from jax import lax
from jax.experimental import pallas as pl
from jax.experimental.pallas import tpu as pltpu
from jax.sharding import PartitionSpec as P

HD = 128
HEADS = 8
BLK = 256
NB = 32
CHIPS = 16
HALF = 128
STAT = 16
PIECE = 32
SCALE = 1.0 / math.sqrt(HD)
masked_score = -1e30

SEND_ROWS = HALF + STAT + PIECE
SHARE_ROWS = HALF + PIECE

same_core = [[chip * 2 + core for chip in range(CHIPS)] for core in range(2)]
core_swap = [(device, device ^ 1) for device in range(2 * CHIPS)]

smem = pl.BlockSpec(memory_space=pltpu.SMEM)
vmem = pl.BlockSpec(memory_space=pltpu.VMEM)


def params():
    return pltpu.CompilerParams(vmem_limit_bytes=40 * 2**20)


def cost(flops, exps, size):
    return pl.CostEstimate(flops=flops, transcendentals=exps, bytes_accessed=size)


def split_three(value):
    high = value.astype(jnp.bfloat16)
    rest = value - high.astype(jnp.float32)
    middle = rest.astype(jnp.bfloat16)
    low = (rest - middle.astype(jnp.float32)).astype(jnp.bfloat16)
    return high, middle, low


def dot_nt(left, right):
    return lax.dot_general(
        left, right, (((1,), (1,)), ((), ())), preferred_element_type=jnp.float32
    )


def column_softmax(raw):
    top = jnp.max(raw, axis=0, keepdims=True)
    weights = jnp.exp((raw - top) * SCALE)
    return top * SCALE, jnp.sum(weights, axis=0, keepdims=True), weights


def window_kernel(map_ref, reach_ref, query_ref, own_ref, other_ref, send_ref):
    position = lax.axis_index("ctx")
    core = position % 2
    partner = position + 1 - 2 * core
    reach = reach_ref[core]
    blocks = []
    for ref, device in ((own_ref, position), (other_ref, partner)):
        slot = jnp.where(map_ref[2 * device] // NB == core, 0, 1)
        place = map_ref[2 * device + slot] - NB * core
        rows = pl.ds(pl.multiple_of(slot * BLK, BLK), BLK)
        keys = ref[0, rows, :]
        values = ref[1, rows, :]
        blocks.append((place < reach, place, keys, values, values.T))
    for head in range(HEADS):
        query = query_ref[core, :, head * HD : (head + 1) * HD]
        parts = []
        for live, _, keys, _, values_t in blocks:
            top, total, weights = column_softmax(dot_nt(keys, query))
            weighted = jnp.dot(
                values_t, weights.astype(jnp.bfloat16), preferred_element_type=jnp.float32
            )
            parts.append((jnp.where(live, top, masked_score), total, weighted, live))
        joined = jnp.maximum(parts[0][0], parts[1][0])
        lifts = [jnp.where(part[3], jnp.exp(part[0] - joined), 0.0) for part in parts]
        total = parts[0][1] * lifts[0] + parts[1][1] * lifts[1]
        some = total > 0.0
        inverse = jnp.where(some, 1.0 / jnp.where(some, total, 1.0), 0.0)
        level = jnp.where(some, joined + jnp.log(jnp.where(some, total, 1.0)), masked_score)
        mean = parts[0][2] * (lifts[0] * inverse) + parts[1][2] * (lifts[1] * inverse)
        mean = mean.astype(jnp.bfloat16)
        high, middle, low = split_three(level)
        row = lax.broadcasted_iota(jnp.int32, (STAT, BLK), 0)
        stats = jnp.where(
            row == 0,
            high.astype(jnp.float32),
            jnp.where(
                row == 1,
                middle.astype(jnp.float32),
                jnp.where(row == 2, low.astype(jnp.float32), 0.0),
            ),
        ).astype(jnp.bfloat16)
        for half in range(2):
            lanes = slice(half * HALF, (half + 1) * HALF)
            send_ref[2 * head + half, :HALF, :] = mean[:, lanes]
            send_ref[2 * head + half, HALF : HALF + STAT, :] = stats[:, lanes]
    first = blocks[0][1] == 0
    for member in range(2):
        block = jnp.where(first, blocks[0][2 + member], blocks[1][2 + member])
        send_ref[8 * member : 8 * member + 8, HALF + STAT :, :] = block.reshape(8, PIECE, HD)


def own_kernel(query_ref, keyval_ref, mean_ref, level_ref):
    position = lax.axis_index("ctx")
    core = position % 2
    chip = position // 2
    half = chip % 2
    rows = pl.ds(pl.multiple_of(half * HALF, HALF), HALF)
    lanes = pl.ds(pl.multiple_of(chip // 2 * HD, HD), HD)
    query = query_ref[core, rows, lanes]
    raw = dot_nt(keyval_ref[core, 0], query)
    key = lax.broadcasted_iota(jnp.int32, raw.shape, 0)
    row = lax.broadcasted_iota(jnp.int32, raw.shape, 1) + half * HALF
    live = key <= row
    raw = jnp.where(live, raw, masked_score)
    top = jnp.max(raw, axis=0, keepdims=True)
    weights = jnp.where(live, jnp.exp((raw - top) * SCALE), 0.0)
    total = jnp.sum(weights, axis=0, keepdims=True)
    weighted = jnp.dot(
        keyval_ref[core, 1].T, weights.astype(jnp.bfloat16), preferred_element_type=jnp.float32
    )
    mean_ref[...] = weighted / total
    level_ref[...] = jnp.broadcast_to(top * SCALE + jnp.log(total), level_ref.shape)


def combine_kernel(map_ref, got_ref, mean_ref, level_ref, share_ref):
    core = lax.axis_index("ctx") % 2

    def look(slot, found):
        return jnp.where(map_ref[slot] == core * NB, slot, found)

    holder = lax.fori_loop(0, 2 * NB, look, jnp.int32(0)) // 4
    levels = [level_ref[0:1, :]]
    for source in range(CHIPS):
        stats = got_ref[source, HALF : HALF + STAT, :].astype(jnp.float32)
        levels.append(stats[0:1] + stats[1:2] + stats[2:3])
    top = levels[0]
    for level in levels[1:]:
        top = jnp.maximum(top, level)
    lift = jnp.exp(levels[0] - top)
    total = lift
    joined = mean_ref[...] * lift
    for source in range(CHIPS):
        lift = jnp.exp(levels[source + 1] - top)
        total = total + lift
        joined = joined + got_ref[source, :HALF, :].astype(jnp.float32) * lift
    result = (joined / total).T.astype(jnp.bfloat16)
    piece = got_ref[holder, HALF + STAT :, :]
    for target in range(CHIPS):
        share_ref[target, :HALF, :] = result
        share_ref[target, HALF:, :] = piece


def project_kernel(own_ref, other_ref, weight_ref, out_ref):
    core = lax.axis_index("ctx") % 2
    for ref, context in ((own_ref, core), (other_ref, 1 - core)):
        for half in range(2):
            rows = jnp.concatenate(
                [ref[2 * head + half, :HALF, :] for head in range(HEADS)], axis=1
            )
            result = jnp.dot(rows, weight_ref[...], preferred_element_type=jnp.float32)
            out_ref[pl.ds(context * 4 + half * 2, 2)] = result.reshape(2, 64, BLK)


STEP_HEADS = 4


def block_kernel(map_ref, query_ref, keyval_ref, own_ref, other_ref, out_ref):
    position = lax.axis_index("ctx")
    core = position % 2
    slot = pl.program_id(0)
    block = map_ref[2 * position + slot]
    mine = block // NB == core
    seen = block % NB != 0

    def anchor(member):
        taken = slice(8 * member, 8 * member + 8)
        own = own_ref[taken, HALF:, :].reshape(BLK, HD)
        other = other_ref[taken, HALF:, :].reshape(BLK, HD)
        return jnp.where(mine, own, other)

    keys = jnp.concatenate([anchor(0), keyval_ref[0]], axis=0)
    values = jnp.concatenate([anchor(1), keyval_ref[1]], axis=0)
    key = lax.broadcasted_iota(jnp.int32, (BLK, 2 * BLK), 1)
    row = lax.broadcasted_iota(jnp.int32, (BLK, 2 * BLK), 0) + BLK
    first_key = jnp.where(seen, 0, BLK)
    live = (key <= row) & (key >= first_key)
    for head in range(STEP_HEADS):
        lanes = slice(head * HD, (head + 1) * HD)
        raw = jnp.where(live, dot_nt(query_ref[:, lanes], keys), masked_score)
        top = jnp.max(raw, axis=1, keepdims=True)
        weights = jnp.where(live, jnp.exp((raw - top) * SCALE), 0.0)
        total = jnp.sum(weights, axis=1, keepdims=True)
        weighted = jnp.dot(
            weights.astype(jnp.bfloat16), values, preferred_element_type=jnp.float32
        )
        out_ref[:, lanes] = (weighted / total).astype(jnp.bfloat16)


def shaped(shape, dtype):
    return jax.ShapeDtypeStruct(shape, dtype)


def on_device(
    ctx_queries, ctx_keyvals, block_map, window_reach, win_queries, win_keyvals, out_weight
):
    other_keyvals = lax.ppermute(ctx_keyvals, "ctx", core_swap)
    send = pl.pallas_call(
        window_kernel,
        out_shape=shaped((CHIPS, SEND_ROWS, HD), jnp.bfloat16),
        in_specs=[smem, smem, vmem, vmem, vmem],
        out_specs=vmem,
        compiler_params=params(),
        cost_estimate=cost(2**29, 2**20, 2**21),
        name="window_parts",
    )(block_map, window_reach, win_queries, ctx_keyvals, other_keyvals)
    got = lax.all_to_all(send, "ctx", 0, 0, axis_index_groups=same_core, tiled=True)
    own_mean, own_level = pl.pallas_call(
        own_kernel,
        out_shape=(shaped((HD, HALF), jnp.float32), shaped((8, HALF), jnp.float32)),
        in_specs=[vmem, vmem],
        out_specs=(vmem, vmem),
        compiler_params=params(),
        cost_estimate=cost(2**24, 2**15, 2**20),
        name="window_own",
    )(win_queries, win_keyvals)
    share = pl.pallas_call(
        combine_kernel,
        out_shape=shaped((CHIPS, SHARE_ROWS, HD), jnp.bfloat16),
        in_specs=[smem, vmem, vmem, vmem],
        out_specs=vmem,
        compiler_params=params(),
        cost_estimate=cost(2**20, 2**12, 2**20),
        name="window_join",
    )(block_map, got, own_mean, own_level)
    rows_own = lax.all_to_all(share, "ctx", 0, 0, axis_index_groups=same_core, tiled=True)
    rows_other = lax.ppermute(rows_own, "ctx", core_swap)
    shares = pl.pallas_call(
        project_kernel,
        out_shape=shaped((8, 64, BLK), jnp.float32),
        in_specs=[vmem, vmem, vmem],
        out_specs=vmem,
        compiler_params=params(),
        cost_estimate=cost(2**28, 0, 2**21),
        name="project",
    )(rows_own, rows_other, out_weight)
    summands = lax.all_to_all(shares, "tp", 0, 0, tiled=True)
    context_attn = pl.pallas_call(
        block_kernel,
        out_shape=shaped((2 * BLK, HEADS * HD), jnp.bfloat16),
        grid=(2, HEADS // STEP_HEADS),
        in_specs=[
            smem,
            pl.BlockSpec((BLK, STEP_HEADS * HD), lambda slot, step: (slot, step)),
            pl.BlockSpec((2, BLK, HD), lambda slot, step: (0, slot, 0)),
            pl.BlockSpec((CHIPS, SHARE_ROWS, HD), lambda slot, step: (0, 0, 0)),
            pl.BlockSpec((CHIPS, SHARE_ROWS, HD), lambda slot, step: (0, 0, 0)),
        ],
        out_specs=pl.BlockSpec((BLK, STEP_HEADS * HD), lambda slot, step: (slot, step)),
        compiler_params=params(),
        cost_estimate=cost(2**30, 2**21, 2**22),
        name="block_attention",
    )(block_map, ctx_queries, ctx_keyvals, rows_own, rows_other)
    window_proj = jnp.sum(summands, axis=0)
    return (context_attn, window_proj)


def solution(mesh):
    return jax.shard_map(
        on_device,
        mesh=mesh,
        in_specs=(
            P("ctx", "tp"),
            P(None, "ctx", "tp"),
            P(),
            P(),
            P(None, None, "tp"),
            P(None, None, None, "tp"),
            P("tp", "ctx"),
        ),
        out_specs=(P("ctx", "tp"), P("tp", "ctx")),
        check_vma=False,
    )
```

time: 404 us -> 82.6 us (0.20); the launches traced: 399 us -> 82.2 us
  blocking collectives: 249 us -> 14.7 us
  local copies, waits for them, and re-layouts: 56.8 us -> 4.16 us
  between operations: 26 us -> 0.7 us
  other arithmetic: 21.9 us -> 0.66 us
  starting transfers between devices: 0.12 us -> 19.9 us
  matrix products: 18.7 us -> 0 us
  Pallas kernels: 0 us -> 16.4 us
    psum x1 -> x0, blocking collectives: 124 us -> none  [on_device(): lax.psum((stacked_parts[1] * lift_factor, stacked_parts[2] * jnp.repeat(l...]
    pmax x1 -> x0, blocking collectives: 124 us -> none  [on_device(): global_top = lax.pmax(stacked_parts[0], 'ctx')]
    reduce_scatter x1 -> x0, waiting for transfers between devices: 26.6 us -> none  [on_device(): lax.psum_scatter(jnp.dot(window_attn, out_weight, preferred_element_type=...]
    all_to_all x0 -> x2, waiting for transfers between devices: none -> 22.5 us  [the longest x1 11.6 us: on_device(): lax.all_to_all(send, 'ctx', 0, 0, axis_index_groups=same_core, tiled=True)]
    dot_general x13 -> x0, matrix products: 18.7 us -> none  [the longest x6 12.5 us: partial_softmax(): jnp.einsum('rhgk,khd->rhgd', weights_low, value_split, preferred_element_...]
    pallas_call x0 -> x5, Pallas kernels: none -> 16.4 us  [the longest x1 6.99 us: on_device(): pl.pallas_call(block_kernel, out_shape=shaped((2 * BLK, HEADS * HD), jnp....]
    reshape x12 -> x0, local copies, waits for them, and re-layouts: 16.3 us -> none  [the longest x5 6.3 us: combine_parts(): jnp.repeat(latter_lift, HD, axis=-1)]
    all_to_all x0 -> x1, blocking collectives: none -> 14.7 us  [on_device(): lax.all_to_all(share, 'ctx', 0, 0, axis_index_groups=same_core, tiled=True)]
  transfers between devices with their start and end apart: 3 -> 4, of which waited for: 1 -> 4; matrix products, arithmetic and copies ran while one was open for 21% -> 0% of each run, Pallas kernels for 0% -> 9%
where the time goes in v1:
time: 82.6 us; the launch traced here: 82.2 us
  waiting for transfers between devices  25.6 us (31%)
  starting transfers between devices  19.9 us (24%)
  Pallas kernels  16.4 us (20%)
  blocking collectives  14.7 us (18%)
  local copies, waits for them, and re-layouts  4.16 us (5%)
    all_to_all x1, blocking collectives, on_device(): lax.all_to_all(share, 'ctx', 0, 0, axis_index_groups=same_core, tiled=True)  14.7 us
    all_to_all x1, waiting for transfers between devices, on_device(): lax.all_to_all(send, 'ctx', 0, 0, axis_index_groups=same_core, tiled=True)  11.6 us
    all_to_all x1, waiting for transfers between devices, on_device(): summands = lax.all_to_all(shares, 'tp', 0, 0, tiled=True)  10.9 us
    all_to_all x1, starting transfers between devices, on_device(): summands = lax.all_to_all(shares, 'tp', 0, 0, tiled=True)  8.31 us
    pallas_call x1, Pallas kernels, on_device(): pl.pallas_call(block_kernel, out_shape=shaped((2 * BLK, HEADS * HD), jnp....  6.99 us
    pallas_call x1, Pallas kernels, on_device(): pl.pallas_call(window_kernel, out_shape=shaped((CHIPS, SEND_ROWS, HD), jn...  6.36 us
    all_to_all x1, starting transfers between devices, on_device(): lax.all_to_all(send, 'ctx', 0, 0, axis_index_groups=same_core, tiled=True)  5.15 us
    unnamed x20, local copies, waits for them, and re-layouts  4.16 us
  transfers between devices with their start and end apart: 4, of which 4 were waited for; matrix products, arithmetic and copies ran while one was open for 0% of the time, Pallas kernels for 9%

profile of v1, /device:TPU:1, one launch (start us, length us, event | category | flops | bytes accessed | tf_op | source)
XLA Modules:
  0.0 82.2 jit_solution(14085097377147767036)
XLA Ops:
  0.6 3.3 %collective-permute-start = (bf16[2,512,128]{2,1,0:T(8,128)(2,1)}, bf16[2,512,128]{2,1,0:T(8,128)(2,1)S(1)}, u32[]{:S(2)}, u32[]{:S(2)}) collective-permute-start(bf16[2,512,128]{2,1,0:T(8,128)(2,1)} %keyval_ref.3), channel_id=1, source_target_pairs={{0,8},{8,0},{16,24},{24,16},{32,40},{40,32},{48,56},{56,48},{64,72... | collective-permute-start | bytes 786440 | tf_op jit(solution)/shard_map/ppermute | solution.py:214
  4.0 1.4 %collective-permute-done.other_ref = bf16[2,512,128]{2,1,0:T(8,128)(2,1)S(1)} collective-permute-done((bf16[2,512,128]{2,1,0:T(8,128)(2,1)}, bf16[2,512,128]{2,1,0:T(8,128)(2,1)S(1)}, u32[]{:S(2)}, u32[]{:S(2)}) %collective-permute-start) | collective-permute-done | bytes 262176 | tf_op jit(solution)/shard_map/ppermute | solution.py:214
  5.3 0.0 copy-start
  5.3 1.2 %copy-done = bf16[2,256,1024]{2,1,0:T(8,128)(2,1)S(1)} copy-done((bf16[2,256,1024]{2,1,0:T(8,128)(2,1)S(1)}, bf16[2,256,1024]{2,1,0:T(8,128)(2,1)}, u32[]{:S(2)}) %copy-start) | copy-done | bytes 1048600
  6.6 0.0 copy-start.4
  6.6 0.9 %copy-done.4 = bf16[2,512,128]{2,1,0:T(8,128)(2,1)S(1)} copy-done((bf16[2,512,128]{2,1,0:T(8,128)(2,1)S(1)}, bf16[2,512,128]{2,1,0:T(8,128)(2,1)}, u32[]{:S(2)}) %copy-start.4) | copy-done | bytes 262168
  7.5 0.0 copy-start.6
  7.5 0.7 copy-done.6
  8.2 0.0 copy-start.8
  8.2 0.7 copy-done.8
  8.8 6.4 %window_parts.1 = bf16[16,176,128]{2,1,0:T(8,128)(2,1)} custom-call(s32[64]{0:T(128)S(1)} %copy-done.6, s32[2]{0:T(128)S(1)} %copy-done.8, bf16[2,256,1024]{2,1,0:T(8,128)(2,1)S(1)} %copy-done, bf16[2,512,128]{2,1,0:T(8,128)(2,1)S(1)} %copy-done.4, bf16[2,512,128]{2,1,0:T(8,128)(2,1)S(1)} %collective-permute-done.other_ref), custom_call_target="tpu_custom_call" | custom-call | flops 536870912 | bytes 2097152 | tf_op jit(solution)/shard_map/window_parts/pallas_call | solution.py:215
  15.2 0.0 copy-start.1
  15.2 0.0 copy-start.3
  15.2 5.2 %all-to-all-start = ((bf16[16,176,128]{2,1,0:T(8,128)(2,1)}), bf16[16,176,128]{2,1,0:T(8,128)(2,1)S(1)}, u32[]{:S(2)}, u32[]{:S(2)}) async-start(bf16[16,176,128]{2,1,0:T(8,128)(2,1)} %window_parts.1), calls=%async_computation | async-start | bytes 1441792 | tf_op jit(solution)/shard_map/all_to_all | solution.py:224
  20.3 0.0 copy-done.1
  20.4 0.0 copy-done.3
  20.4 0.4 window_own.1
  20.8 11.6 %all-to-all-done.got_ref = bf16[16,176,128]{2,1,0:T(8,128)(2,1)S(1)} async-done(((bf16[16,176,128]{2,1,0:T(8,128)(2,1)}), bf16[16,176,128]{2,1,0:T(8,128)(2,1)S(1)}, u32[]{:S(2)}, u32[]{:S(2)}) %all-to-all-start) | async-done | bytes 720928 | tf_op jit(solution)/shard_map/all_to_all | solution.py:224
  32.4 0.0 copy-start.7
  32.4 0.7 copy-done.7
  33.0 1.4 %window_join.1 = bf16[16,160,128]{2,1,0:T(8,128)(2,1)S(1)} custom-call(s32[64]{0:T(128)S(1)} %copy-done.7, bf16[16,176,128]{2,1,0:T(8,128)(2,1)S(1)} %all-to-all-done.got_ref, f32[128,128]{1,0:T(8,128)S(1)} %get-tuple-element.4.mean_ref, f32[8,128]{1,0:T(8,128)S(1)} %get-tuple-element.5.level_ref), custom_call_target="tpu_custom_call" | custom-call | flops 1048576 | bytes 1048576 | tf_op jit(solution)/shard_map/window_join/pallas_call | solution.py:234
  34.5 0.0 copy-start.2
  34.5 14.7 %all_to_all.15.own_ref = bf16[16,160,128]{2,1,0:T(8,128)(2,1)S(1)} all-to-all(bf16[16,160,128]{2,1,0:T(8,128)(2,1)S(1)} %window_join.1), channel_id=1, replica_groups={{0,16,32,48,64,80,96,112,128,144,160,176,192,208,224,240},{8,24,40,56,7..., dimensions={0} | all-to-all | bytes 1310720 | tf_op jit(solution)/shard_map/all_to_all | solution.py:243
  49.1 3.2 %collective-permute-start.1 = (bf16[16,160,128]{2,1,0:T(8,128)(2,1)S(1)}, bf16[16,160,128]{2,1,0:T(8,128)(2,1)S(1)}, u32[]{:S(2)}, u32[]{:S(2)}) collective-permute-start(bf16[16,160,128]{2,1,0:T(8,128)(2,1)S(1)} %all_to_all.15.own_ref), channel_id=1, source_target_pairs={{0,8},{8,0},{16,24},{24,16},{32,40},{40,32},{48,56},{56,48},{64,72... | collective-permute-start | bytes 1966088 | tf_op jit(solution)/shard_map/ppermute | solution.py:244
  52.3 1.7 %collective-permute-done.1.other_ref = bf16[16,160,128]{2,1,0:T(8,128)(2,1)S(1)} collective-permute-done((bf16[16,160,128]{2,1,0:T(8,128)(2,1)S(1)}, bf16[16,160,128]{2,1,0:T(8,128)(2,1)S(1)}, u32[]{:S(2)}, u32[]{:S(2)}) %collective-permute-start.1) | collective-permute-done | bytes 655392 | tf_op jit(solution)/shard_map/ppermute | solution.py:244
  54.0 0.0 copy-done.2
  54.0 0.0 copy-start.9
  54.0 1.2 %project.1 = f32[8,64,256]{2,1,0:T(8,128)} custom-call(bf16[16,160,128]{2,1,0:T(8,128)(2,1)S(1)} %all_to_all.15.own_ref, bf16[16,160,128]{2,1,0:T(8,128)(2,1)S(1)} %collective-permute-done.1.other_ref, bf16[1024,256]{1,0:T(8,128)(2,1)S(1)} %copy-done.2), custom_call_target="tpu_custom_call" | custom-call | flops 268435456 | bytes 2097152 | tf_op jit(solution)/shard_map/project/pallas_call | solution.py:245
  55.3 0.0 copy-start.5
  55.3 8.3 %all-to-all-start.2 = ((f32[8,64,256]{2,1,0:T(8,128)}), f32[8,64,256]{2,1,0:T(8,128)S(1)}, u32[]{:S(2)}, u32[]{:S(2)}) async-start(f32[8,64,256]{2,1,0:T(8,128)} %project.1), calls=%async_computation.2 | async-start | bytes 1048576 | tf_op jit(solution)/shard_map/all_to_all | solution.py:254
  63.6 0.0 copy-done.9
  63.6 0.0 copy-done.5
  63.6 7.0 %block_attention.1 = bf16[512,1024]{1,0:T(8,128)(2,1)} custom-call(s32[64]{0:T(128)S(1)} %copy-done.7, bf16[512,1024]{1,0:T(8,128)(2,1)S(1)} %copy-done.9, bf16[2,512,128]{2,1,0:T(8,128)(2,1)S(1)} %copy-done.5, bf16[16,160,128]{2,1,0:T(8,128)(2,1)S(1)} %all_to_all.15.own_ref, bf16[16,160,128]{2,1,0:T(8,128)(2,1)S(1)} %collective-permute-done.1.other_ref), custom_call_target="tpu_custom_call" | custom-call | flops 1073741824 | bytes 4194304 | tf_op jit(solution)/shard_map/block_attention/pallas_call | solution.py:255
  70.6 10.9 %all-to-all-done.2 = f32[8,64,256]{2,1,0:T(8,128)S(1)} async-done(((f32[8,64,256]{2,1,0:T(8,128)}), f32[8,64,256]{2,1,0:T(8,128)S(1)}, u32[]{:S(2)}, u32[]{:S(2)}) %all-to-all-start.2) | async-done | bytes 524320 | tf_op jit(solution)/shard_map/all_to_all | solution.py:254
  81.5 0.7 reduce_sum.9
Async XLA Ops:
  0.6 4.7 %collective-permute-start = (bf16[2,512,128]{2,1,0:T(8,128)(2,1)}, bf16[2,512,128]{2,1,0:T(8,128)(2,1)S(1)}, u32[]{:S(2)}, u32[]{:S(2)}) collective-permute-start(bf16[2,512,128]{2,1,0:T(8,128)(2,1)} %keyval_ref.3), channel_id=1, source_target_pairs={{0,8},{8,0},{16,24},{24,16},{32,40},{40,32},{48,56},{56,48},{64,72... | collective-permute-start | bytes 786440 | tf_op jit(solution)/shard_map/ppermute | solution.py:214
  5.3 1.2 %copy-start = (bf16[2,256,1024]{2,1,0:T(8,128)(2,1)S(1)}, bf16[2,256,1024]{2,1,0:T(8,128)(2,1)}, u32[]{:S(2)}) copy-start(bf16[2,256,1024]{2,1,0:T(8,128)(2,1)} %query_ref.4) | copy-start | bytes 3145732
  6.6 0.9 %copy-start.4 = (bf16[2,512,128]{2,1,0:T(8,128)(2,1)S(1)}, bf16[2,512,128]{2,1,0:T(8,128)(2,1)}, u32[]{:S(2)}) copy-start(bf16[2,512,128]{2,1,0:T(8,128)(2,1)} %keyval_ref.3) | copy-start | bytes 786436
  7.5 0.7 copy-start.6
  8.2 0.7 copy-start.8
  15.2 5.2 %copy-start.1 = (bf16[2,256,1024]{2,1,0:T(8,128)(2,1)S(1)}, bf16[2,256,1024]{2,1,0:T(8,128)(2,1)}, u32[]{:S(2)}) copy-start(bf16[2,256,1024]{2,1,0:T(8,128)(2,1)} %query_ref.4) | copy-start | bytes 3145732
  15.2 5.2 %copy-start.3 = (bf16[2,2,256,128]{3,2,1,0:T(8,128)(2,1)S(1)}, bf16[2,2,256,128]{3,2,1,0:T(8,128)(2,1)}, u32[]{:S(2)}) copy-start(bf16[2,2,256,128]{3,2,1,0:T(8,128)(2,1)} %keyval_ref.2) | copy-start | bytes 786436
  15.2 17.2 %all-to-all-start = ((bf16[16,176,128]{2,1,0:T(8,128)(2,1)}), bf16[16,176,128]{2,1,0:T(8,128)(2,1)S(1)}, u32[]{:S(2)}, u32[]{:S(2)}) async-start(bf16[16,176,128]{2,1,0:T(8,128)(2,1)} %window_parts.1), calls=%async_computation | async-start | bytes 1441792 | tf_op jit(solution)/shard_map/all_to_all | solution.py:224
  32.4 0.7 copy-start.7
  34.5 19.6 %copy-start.2 = (bf16[1024,256]{1,0:T(8,128)(2,1)S(1)}, bf16[1024,256]{1,0:T(8,128)(2,1)}, u32[]{:S(2)}) copy-start(bf16[1024,256]{1,0:T(8,128)(2,1)} %weight_ref.1) | copy-start | bytes 1572868
  49.1 4.9 %collective-permute-start.1 = (bf16[16,160,128]{2,1,0:T(8,128)(2,1)S(1)}, bf16[16,160,128]{2,1,0:T(8,128)(2,1)S(1)}, u32[]{:S(2)}, u32[]{:S(2)}) collective-permute-start(bf16[16,160,128]{2,1,0:T(8,128)(2,1)S(1)} %all_to_all.15.own_ref), channel_id=1, source_target_pairs={{0,8},{8,0},{16,24},{24,16},{32,40},{40,32},{48,56},{56,48},{64,72... | collective-permute-start | bytes 1966088 | tf_op jit(solution)/shard_map/ppermute | solution.py:244
  54.0 9.6 %copy-start.9 = (bf16[512,1024]{1,0:T(8,128)(2,1)S(1)}, bf16[512,1024]{1,0:T(8,128)(2,1)}, u32[]{:S(2)}) copy-start(bf16[512,1024]{1,0:T(8,128)(2,1)} %query_ref.5) | copy-start | bytes 3145732
  55.3 8.3 %copy-start.5 = (bf16[2,512,128]{2,1,0:T(8,128)(2,1)S(1)}, bf16[2,512,128]{2,1,0:T(8,128)(2,1)}, u32[]{:S(2)}) copy-start(bf16[2,512,128]{2,1,0:T(8,128)(2,1)} %keyval_ref.3) | copy-start | bytes 786436
  55.3 26.3 %all-to-all-start.2 = ((f32[8,64,256]{2,1,0:T(8,128)}), f32[8,64,256]{2,1,0:T(8,128)S(1)}, u32[]{:S(2)}, u32[]{:S(2)}) async-start(f32[8,64,256]{2,1,0:T(8,128)} %project.1), calls=%async_computation.2 | async-start | bytes 1048576 | tf_op jit(solution)/shard_map/all_to_all | solution.py:254

commit v2 on v1

v2 whole, which is shorter than its diff:
```python
import math

import jax
import jax.numpy as jnp
from jax import lax
from jax.experimental import pallas as pl
from jax.experimental.pallas import tpu as pltpu
from jax.sharding import PartitionSpec as P

HD = 128
HEADS = 8
BLK = 256
NB = 32
CHIPS = 16
HALF = 128
STAT = 16
PIECE = 32
SCALE = 1.0 / math.sqrt(HD)
SCALE2 = SCALE * math.log2(math.e)
masked_score = -1e30

SEND_ROWS = HALF + STAT + PIECE
SHARE_ROWS = HALF + PIECE

same_core = [[chip * 2 + core for chip in range(CHIPS)] for core in range(2)]
core_swap = [(device, device ^ 1) for device in range(2 * CHIPS)]

smem = pl.BlockSpec(memory_space=pltpu.SMEM)
vmem = pl.BlockSpec(memory_space=pltpu.VMEM)
hbm = pl.BlockSpec(memory_space=pltpu.HBM)


def params(room=40):
    return pltpu.CompilerParams(vmem_limit_bytes=room * 2**20)


def cost(flops, exps, size):
    return pl.CostEstimate(flops=flops, transcendentals=exps, bytes_accessed=size)


def split_three(value):
    high = value.astype(jnp.bfloat16)
    rest = value - high.astype(jnp.float32)
    middle = rest.astype(jnp.bfloat16)
    low = (rest - middle.astype(jnp.float32)).astype(jnp.bfloat16)
    return high, middle, low


def dot_nt(left, right):
    return lax.dot_general(
        left, right, (((1,), (1,)), ((), ())), preferred_element_type=jnp.float32
    )


def row_softmax(raw):
    top = jnp.max(raw, axis=1, keepdims=True)
    weights = jnp.exp2((raw - top) * SCALE2)
    return top * SCALE, jnp.sum(weights, axis=1, keepdims=True), weights


def weigh(weights, values):
    return jnp.dot(weights.astype(jnp.bfloat16), values, preferred_element_type=jnp.float32)


def find_block(map_ref, device, core):
    slot = jnp.where(map_ref[2 * device] // NB == core, 0, 1)
    place = map_ref[2 * device + slot] - NB * core
    return place, pl.ds(pl.multiple_of(slot * BLK, BLK), BLK)


def block_parts(query_ref, keys, values, sum_ref):
    lane = lax.broadcasted_iota(jnp.int32, (BLK, HD), 1)
    tops = jnp.zeros((BLK, HD), jnp.float32)
    totals = jnp.zeros((BLK, HD), jnp.float32)
    for head in range(HEADS):
        lanes = slice(head * HD, (head + 1) * HD)
        top, total, weights = row_softmax(dot_nt(query_ref[:, lanes], keys))
        sum_ref[:, lanes] = weigh(weights, values)
        tops = jnp.where(lane == head, top, tops)
        totals = jnp.where(lane == head, total, totals)
    return tops, totals


def first_kernel(
    map_hbm,
    reach_hbm,
    query_hbm,
    keyval_hbm,
    window_hbm,
    query_ref,
    sum_ref,
    top_ref,
    total_ref,
    mean_ref,
    level_ref,
    info_ref,
    keyval_ref,
    window_ref,
    map_ref,
    reach_ref,
    done,
):
    position = lax.axis_index("ctx")
    core = position % 2
    chip = position // 2
    copies = [
        pltpu.make_async_copy(source, target, done.at[number])
        for number, (source, target) in enumerate(
            (
                (map_hbm, map_ref),
                (reach_hbm, reach_ref),
                (keyval_hbm, keyval_ref),
                (query_hbm.at[core], query_ref),
                (window_hbm.at[core], window_ref),
            )
        )
    ]
    for copy in copies:
        copy.start()
    for copy in copies:
        copy.wait()
    partner = position + 1 - 2 * core
    reach = reach_ref[core]
    place, rows = find_block(map_ref, position, core)
    other_place, _ = find_block(map_ref, partner, core)
    holder = jnp.int32(0)
    for slot in range(2 * NB):
        holder = jnp.where(map_ref[slot] == core * NB, slot // 4, holder)
    info_ref[0] = holder
    info_ref[1] = jnp.where(place < reach, 1, 0)
    info_ref[2] = jnp.where(other_place < reach, 1, 0)
    info_ref[3] = place
    info_ref[4] = jnp.where(map_ref[2 * partner] // NB == core, 0, 1)
    info_ref[5] = jnp.where(map_ref[2 * position] // NB == core, 0, 1)
    info_ref[6] = map_ref[2 * position]
    info_ref[7] = map_ref[2 * position + 1]
    top_ref[...], total_ref[...] = block_parts(
        query_ref, keyval_ref[0, rows, :], keyval_ref[1, rows, :], sum_ref
    )
    half = chip % 2
    query_rows = pl.ds(pl.multiple_of(half * HALF, HALF), HALF)
    query_lanes = pl.ds(pl.multiple_of(chip // 2 * HD, HD), HD)
    raw = dot_nt(query_ref[query_rows, query_lanes], window_ref[0])
    key = lax.broadcasted_iota(jnp.int32, raw.shape, 1)
    row = lax.broadcasted_iota(jnp.int32, raw.shape, 0) + half * HALF
    live = key <= row
    raw = jnp.where(live, raw, masked_score)
    top, _, weights = row_softmax(raw)
    weights = jnp.where(live, weights, 0.0)
    total = jnp.sum(weights, axis=1, keepdims=True)
    mean_ref[...] = weigh(weights, window_ref[1]) / total
    level = jnp.broadcast_to(top + jnp.log(total), (HALF, HALF)).T
    level_ref[...] = level[:8]


def second_kernel(
    info_ref,
    query_ref,
    sum_ref,
    top_ref,
    total_ref,
    own_ref,
    other_ref,
    send_ref,
    second_ref,
):
    own_rows = pl.ds(pl.multiple_of(info_ref[5] * BLK, BLK), BLK)
    other_rows = pl.ds(pl.multiple_of(info_ref[4] * BLK, BLK), BLK)
    first = info_ref[3] == 0
    for member in range(2):
        block = jnp.where(first, own_ref[member, own_rows, :], other_ref[member, other_rows, :])
        send_ref[8 * member : 8 * member + 8, HALF + STAT :, :] = block.reshape(8, PIECE, HD)
    tops, totals = block_parts(
        query_ref, other_ref[0, other_rows, :], other_ref[1, other_rows, :], second_ref
    )
    lives = (info_ref[1] == 1, info_ref[2] == 1)
    tops = [
        jnp.where(live, top, masked_score) for live, top in zip(lives, (top_ref[...], tops))
    ]
    joined = jnp.maximum(tops[0], tops[1])
    lifts = [jnp.where(live, jnp.exp(top - joined), 0.0) for live, top in zip(lives, tops)]
    total = total_ref[...] * lifts[0] + totals * lifts[1]
    some = total > 0.0
    safe = jnp.where(some, total, 1.0)
    inverse = jnp.where(some, 1.0 / safe, 0.0)
    lifts = [lift * inverse for lift in lifts]
    level = jnp.where(some, joined + jnp.log(safe), masked_score).T[:HEADS]
    pieces = [piece.astype(jnp.float32) for piece in split_three(level)]
    row = lax.broadcasted_iota(jnp.int32, (STAT, BLK), 0)
    for head in range(HEADS):
        lanes = slice(head * HD, (head + 1) * HD)
        mean = (
            sum_ref[:, lanes] * lifts[0][:, head : head + 1]
            + second_ref[:, lanes] * lifts[1][:, head : head + 1]
        ).astype(jnp.bfloat16)
        stats = jnp.zeros((STAT, BLK), jnp.float32)
        for number, piece in enumerate(pieces):
            stats = jnp.where(row == number, piece[head : head + 1], stats)
        stats = stats.astype(jnp.bfloat16)
        for half in range(2):
            rows = slice(half * HALF, (half + 1) * HALF)
            send_ref[2 * head + half, :HALF, :] = mean[rows]
            send_ref[2 * head + half, HALF : HALF + STAT, :] = stats[:, rows]


def combine_kernel(info_ref, got_ref, mean_ref, level_ref, share_ref):
    levels = []
    for source in range(CHIPS):
        stats = got_ref[source, HALF : HALF + STAT, :].astype(jnp.float32)
        levels.append(stats[0:1] + stats[1:2] + stats[2:3])
    levels.append(level_ref[0:1, :])
    levels = jnp.concatenate(levels, axis=0)
    lifts = jnp.exp(levels - jnp.max(levels, axis=0, keepdims=True))
    lifts = lifts / jnp.sum(lifts, axis=0, keepdims=True)
    blank = jnp.zeros((HALF - CHIPS - 1, HALF), jnp.float32)
    lifts = jnp.concatenate([lifts, blank], axis=0).T
    joined = mean_ref[...] * lifts[:, CHIPS : CHIPS + 1]
    for source in range(CHIPS):
        part = got_ref[source, :HALF, :].astype(jnp.float32)
        joined = joined + part * lifts[:, source : source + 1]
    result = joined.astype(jnp.bfloat16)
    piece = got_ref[info_ref[0], HALF + STAT :, :]
    for target in range(CHIPS):
        share_ref[target, :HALF, :] = result
        share_ref[target, HALF:, :] = piece


def project_kernel(own_ref, other_ref, weight_ref, out_ref):
    core = lax.axis_index("ctx") % 2
    rows = jnp.concatenate(
        [
            jnp.concatenate([ref[2 * head + half, :HALF, :] for head in range(HEADS)], axis=1)
            for ref in (own_ref, other_ref)
            for half in range(2)
        ],
        axis=0,
    )
    result = jnp.dot(rows, weight_ref[...], preferred_element_type=jnp.float32)
    result = result.reshape(8, 64, BLK).astype(out_ref.dtype)
    out_ref[pl.ds(core * 4, 4)] = result[:4]
    out_ref[pl.ds(4 - core * 4, 4)] = result[4:]


STEP_HEADS = 4


def block_kernel(info_ref, query_ref, keyval_ref, own_ref, other_ref, out_ref):
    core = lax.axis_index("ctx") % 2
    block = info_ref[6 + pl.program_id(0)]
    mine = block // NB == core
    seen = block % NB != 0

    def anchor(member):
        taken = slice(8 * member, 8 * member + 8)
        own = own_ref[taken, HALF:, :].reshape(BLK, HD)
        other = other_ref[taken, HALF:, :].reshape(BLK, HD)
        return jnp.where(mine, own, other)

    keys = jnp.concatenate([anchor(0), keyval_ref[0]], axis=0)
    values = jnp.concatenate([anchor(1), keyval_ref[1]], axis=0)
    key = lax.broadcasted_iota(jnp.int32, (BLK, 2 * BLK), 1)
    row = lax.broadcasted_iota(jnp.int32, (BLK, 2 * BLK), 0) + BLK
    first_key = jnp.where(seen, 0, BLK)
    live = (key <= row) & (key >= first_key)
    for head in range(STEP_HEADS):
        lanes = slice(head * HD, (head + 1) * HD)
        raw = jnp.where(live, dot_nt(query_ref[:, lanes], keys), masked_score)
        _, total, weights = row_softmax(raw)
        out_ref[:, lanes] = (weigh(weights, values) / total).astype(jnp.bfloat16)


def far(array):
    return pltpu.with_memory_space_constraint(array, pltpu.HBM)


def shaped(shape, dtype):
    return jax.ShapeDtypeStruct(shape, dtype)


def on_device(
    ctx_queries, ctx_keyvals, block_map, window_reach, win_queries, win_keyvals, out_weight
):
    other_keyvals = lax.ppermute(ctx_keyvals, "ctx", core_swap)
    queries, sums, tops, totals, own_mean, own_level, info = pl.pallas_call(
        first_kernel,
        out_shape=(
            shaped((BLK, HEADS * HD), jnp.bfloat16),
            shaped((BLK, HEADS * HD), jnp.float32),
            shaped((BLK, HD), jnp.float32),
            shaped((BLK, HD), jnp.float32),
            shaped((HALF, HD), jnp.float32),
            shaped((8, HALF), jnp.float32),
            shaped((8,), jnp.int32),
        ),
        in_specs=[hbm] * 5,
        out_specs=(vmem,) * 6 + (smem,),
        scratch_shapes=[
            pltpu.VMEM((2, 2 * BLK, HD), jnp.bfloat16),
            pltpu.VMEM((2, BLK, HD), jnp.bfloat16),
            pltpu.SMEM((2 * NB,), jnp.int32),
            pltpu.SMEM((2,), jnp.int32),
            pltpu.SemaphoreType.DMA((5,)),
        ],
        compiler_params=params(),
        cost_estimate=cost(2**28, 2**19, 2**21),
        name="window_first",
    )(
        *(far(array) for array in (block_map, window_reach, win_queries, ctx_keyvals, win_keyvals))
    )
    send = pl.pallas_call(
        second_kernel,
        out_shape=shaped((CHIPS, SEND_ROWS, HD), jnp.bfloat16),
        in_specs=[smem] + [vmem] * 6,
        out_specs=vmem,
        scratch_shapes=[pltpu.VMEM((BLK, HEADS * HD), jnp.float32)],
        compiler_params=params(),
        cost_estimate=cost(2**28, 2**19, 2**21),
        name="window_second",
    )(info, queries, sums, tops, totals, ctx_keyvals, other_keyvals)
    got = lax.all_to_all(send, "ctx", 0, 0, axis_index_groups=same_core, tiled=True)
    share = pl.pallas_call(
        combine_kernel,
        out_shape=shaped((CHIPS, SHARE_ROWS, HD), jnp.bfloat16),
        in_specs=[smem, vmem, vmem, vmem],
        out_specs=vmem,
        compiler_params=params(),
        cost_estimate=cost(2**20, 2**12, 2**20),
        name="window_join",
    )(info, got, own_mean, own_level)
    rows_own = lax.all_to_all(share, "ctx", 0, 0, axis_index_groups=same_core, tiled=True)
    rows_other = lax.ppermute(rows_own, "ctx", core_swap)
    shares = pl.pallas_call(
        project_kernel,
        out_shape=shaped((8, 64, BLK), jnp.bfloat16),
        in_specs=[vmem, vmem, vmem],
        out_specs=vmem,
        compiler_params=params(),
        cost_estimate=cost(2**28, 0, 2**21),
        name="project",
    )(rows_own, rows_other, out_weight)
    summands = lax.all_to_all(shares, "tp", 0, 0, tiled=True)
    context_attn = pl.pallas_call(
        block_kernel,
        out_shape=shaped((2 * BLK, HEADS * HD), jnp.bfloat16),
        grid=(2, HEADS // STEP_HEADS),
        in_specs=[
            smem,
            pl.BlockSpec((BLK, STEP_HEADS * HD), lambda slot, step: (slot, step)),
            pl.BlockSpec((2, BLK, HD), lambda slot, step: (0, slot, 0)),
            pl.BlockSpec((CHIPS, SHARE_ROWS, HD), lambda slot, step: (0, 0, 0)),
            pl.BlockSpec((CHIPS, SHARE_ROWS, HD), lambda slot, step: (0, 0, 0)),
        ],
        out_specs=pl.BlockSpec((BLK, STEP_HEADS * HD), lambda slot, step: (slot, step)),
        compiler_params=params(),
        cost_estimate=cost(2**30, 2**21, 2**22),
        name="block_attention",
    )(info, ctx_queries, ctx_keyvals, rows_own, rows_other)
    window_proj = jnp.sum(summands.astype(jnp.float32), axis=0)
    return (context_attn, window_proj)


def solution(mesh):
    return jax.shard_map(
        on_device,
        mesh=mesh,
        in_specs=(
            P("ctx", "tp"),
            P(None, "ctx", "tp"),
            P(),
            P(),
            P(None, None, "tp"),
            P(None, None, None, "tp"),
            P("tp", "ctx"),
        ),
        out_specs=(P("ctx", "tp"), P("tp", "ctx")),
        check_vma=False,
    )
```

time: 82.6 us -> 68.6 us (0.83)
  waiting for transfers between devices: 25.6 us -> 5.82 us
  blocking collectives: 14.7 us -> 32.4 us
  starting transfers between devices: 19.9 us -> 14.1 us
  local copies, waits for them, and re-layouts: 4.16 us -> 0.01 us
  Pallas kernels: 16.4 us -> 14.6 us
    all_to_all x0 -> x1, blocking collectives: none -> 17.8 us  [on_device(): lax.all_to_all(send, 'ctx', 0, 0, axis_index_groups=same_core, tiled=True)]
    all_to_all x1 -> x0, waiting for transfers between devices: 11.6 us -> none  [on_device(): lax.all_to_all(send, 'ctx', 0, 0, axis_index_groups=same_core, tiled=True)]
    all_to_all x1, waiting for transfers between devices: 10.9 us -> 4.09 us  [on_device(): summands = lax.all_to_all(shares, 'tp', 0, 0, tiled=True)]
    all_to_all x1 -> x0, starting transfers between devices: 5.15 us -> none  [on_device(): lax.all_to_all(send, 'ctx', 0, 0, axis_index_groups=same_core, tiled=True)]
    unnamed x20 -> x6, local copies, waits for them, and re-layouts: 4.16 us -> 0.01 us
    pallas_call x3, Pallas kernels: 8.01 us -> 6.49 us  [the longest x1 2.97 us: on_device(): pl.pallas_call(first_kernel, out_shape=(shaped((BLK, HEADS * HD), jnp.bfl...]
    ppermute x1, waiting for transfers between devices: 1.37 us -> 0.01 us  [on_device(): other_keyvals = lax.ppermute(ctx_keyvals, 'ctx', core_swap)]
  transfers between devices with their start and end apart: 4 -> 3, of which waited for: 4 -> 2; matrix products, arithmetic and copies ran while one was open for 0% -> 0% of each run, Pallas kernels for 9% -> 15%
where the time goes in v2:
time: 68.6 us; the launch traced here: 68.3 us
  blocking collectives  32.4 us (47%)
  Pallas kernels  14.6 us (21%)
  starting transfers between devices  14.1 us (21%)
  waiting for transfers between devices  5.82 us (8%)
  between operations  0.69 us (1%)
    all_to_all x1, blocking collectives, on_device(): lax.all_to_all(send, 'ctx', 0, 0, axis_index_groups=same_core, tiled=True)  17.8 us
    all_to_all x1, blocking collectives, on_device(): lax.all_to_all(share, 'ctx', 0, 0, axis_index_groups=same_core, tiled=True)  14.7 us
    all_to_all x1, starting transfers between devices, on_device(): summands = lax.all_to_all(shares, 'tp', 0, 0, tiled=True)  8.18 us
    pallas_call x1, Pallas kernels, on_device(): pl.pallas_call(block_kernel, out_shape=shaped((2 * BLK, HEADS * HD), jnp....  6.95 us
    all_to_all x1, waiting for transfers between devices, on_device(): summands = lax.all_to_all(shares, 'tp', 0, 0, tiled=True)  4.09 us
    ppermute x1, starting transfers between devices, on_device(): other_keyvals = lax.ppermute(ctx_keyvals, 'ctx', core_swap)  3.33 us
    pallas_call x1, Pallas kernels, on_device(): pl.pallas_call(first_kernel, out_shape=(shaped((BLK, HEADS * HD), jnp.bfl...  2.97 us
    ppermute x1, starting transfers between devices, on_device(): rows_other = lax.ppermute(rows_own, 'ctx', core_swap)  2.61 us
  transfers between devices with their start and end apart: 3, of which 2 were waited for; matrix products, arithmetic and copies ran while one was open for 0% of the time, Pallas kernels for 15%

profile of v2, /device:TPU:1, one launch (start us, length us, event | category | flops | bytes accessed | tf_op | source)
XLA Modules:
  0.0 68.3 jit_solution(11686717418526953184)
XLA Ops:
  0.6 0.0 copy-start
  0.6 3.3 %collective-permute-start = (bf16[2,512,128]{2,1,0:T(8,128)(2,1)}, bf16[2,512,128]{2,1,0:T(8,128)(2,1)S(1)}, u32[]{:S(2)}, u32[]{:S(2)}) collective-permute-start(bf16[2,512,128]{2,1,0:T(8,128)(2,1)} %keyval_ref.1), channel_id=1, source_target_pairs={{0,8},{8,0},{16,24},{24,16},{32,40},{40,32},{48,56},{56,48},{64,72... | collective-permute-start | bytes 786440 | tf_op jit(solution)/shard_map/ppermute | solution.py:283
  4.0 3.0 %window_first.1 = (bf16[256,1024]{1,0:T(8,128)(2,1)S(1)}, f32[256,1024]{1,0:T(8,128)S(1)}, f32[256,128]{1,0:T(8,128)S(1)}, f32[256,128]{1,0:T(8,128)S(1)}, f32[1...) custom-call(s32[64]{0:T(128)} %map_hbm.1, s32[2]{0:T(128)} %reach_hbm.1, bf16[2,256,1024]{2,1,0:T(8,128)(2,1)} %query_hbm.1, ...), custom_call_target="tpu_custom_call" | custom-call | flops 268435456 | bytes 2097152 | tf_op jit(solution)/shard_map/window_first/pallas_call | solution.py:284
  7.0 0.0 collective-permute-done.other_ref
  7.0 0.0 copy-done
  7.0 2.4 %window_second.1 = bf16[16,176,128]{2,1,0:T(8,128)(2,1)S(1)} custom-call(s32[8]{0:T(128)S(1)} %get-tuple-element.9.info_ref, bf16[256,1024]{1,0:T(8,128)(2,1)S(1)} %get-tuple-element.10.query_ref, f32[256,1024]{1,0:T(8,128)S(1)} %get-tuple-element.11.sum_ref, f32[256,128]{1,0:T(8,128)S(1)} %get-tuple-element.12.top_ref, ...), custom_call_target="tpu_custom_call" | custom-call | flops 268435456 | bytes 2097152 | tf_op jit(solution)/shard_map/window_second/pallas_call | solution.py:310
  9.4 17.8 %all_to_all.15.got_ref = bf16[16,176,128]{2,1,0:T(8,128)(2,1)S(1)} all-to-all(bf16[16,176,128]{2,1,0:T(8,128)(2,1)S(1)} %window_second.1), channel_id=1, replica_groups={{0,16,32,48,64,80,96,112,128,144,160,176,192,208,224,240},{8,24,40,56,7..., dimensions={0} | all-to-all | bytes 1441792 | tf_op jit(solution)/shard_map/all_to_all | solution.py:320
  27.1 1.1 %window_join.1 = bf16[16,160,128]{2,1,0:T(8,128)(2,1)S(1)} custom-call(s32[8]{0:T(128)S(1)} %get-tuple-element.9.info_ref, bf16[16,176,128]{2,1,0:T(8,128)(2,1)S(1)} %all_to_all.15.got_ref, f32[128,128]{1,0:T(8,128)S(1)} %get-tuple-element.14.mean_ref, f32[8,128]{1,0:T(8,128)S(1)} %get-tuple-element.15.level_ref), custom_call_target="tpu_custom_call" | custom-call | flops 1048576 | bytes 1048576 | tf_op jit(solution)/shard_map/window_join/pallas_call | solution.py:321
  28.3 0.0 copy-start.1
  28.3 14.7 %all_to_all.16.own_ref = bf16[16,160,128]{2,1,0:T(8,128)(2,1)S(1)} all-to-all(bf16[16,160,128]{2,1,0:T(8,128)(2,1)S(1)} %window_join.1), channel_id=1, replica_groups={{0,16,32,48,64,80,96,112,128,144,160,176,192,208,224,240},{8,24,40,56,7..., dimensions={0} | all-to-all | bytes 1310720 | tf_op jit(solution)/shard_map/all_to_all | solution.py:330
  43.0 0.0 copy-start.2
  43.0 2.6 %collective-permute-start.1 = (bf16[16,160,128]{2,1,0:T(8,128)(2,1)S(1)}, bf16[16,160,128]{2,1,0:T(8,128)(2,1)S(1)}, u32[]{:S(2)}, u32[]{:S(2)}) collective-permute-start(bf16[16,160,128]{2,1,0:T(8,128)(2,1)S(1)} %all_to_all.16.own_ref), channel_id=1, source_target_pairs={{0,8},{8,0},{16,24},{24,16},{32,40},{40,32},{48,56},{56,48},{64,72... | collective-permute-start | bytes 1966088 | tf_op jit(solution)/shard_map/ppermute | solution.py:331
  45.6 1.7 %collective-permute-done.1.other_ref = bf16[16,160,128]{2,1,0:T(8,128)(2,1)S(1)} collective-permute-done((bf16[16,160,128]{2,1,0:T(8,128)(2,1)S(1)}, bf16[16,160,128]{2,1,0:T(8,128)(2,1)S(1)}, u32[]{:S(2)}, u32[]{:S(2)}) %collective-permute-start.1) | collective-permute-done | bytes 655392 | tf_op jit(solution)/shard_map/ppermute | solution.py:331
  47.3 0.0 copy-done.1
  47.3 1.1 %project.1 = bf16[8,64,256]{2,1,0:T(8,128)(2,1)} custom-call(bf16[16,160,128]{2,1,0:T(8,128)(2,1)S(1)} %all_to_all.16.own_ref, bf16[16,160,128]{2,1,0:T(8,128)(2,1)S(1)} %collective-permute-done.1.other_ref, bf16[1024,256]{1,0:T(8,128)(2,1)S(1)} %copy-done.1), custom_call_target="tpu_custom_call" | custom-call | flops 268435456 | bytes 2097152 | tf_op jit(solution)/shard_map/project/pallas_call | solution.py:332
  48.4 8.2 %all-to-all-start.2 = ((bf16[8,64,256]{2,1,0:T(8,128)(2,1)}), bf16[8,64,256]{2,1,0:T(8,128)(2,1)S(1)}, u32[]{:S(2)}, u32[]{:S(2)}) async-start(bf16[8,64,256]{2,1,0:T(8,128)(2,1)} %project.1), calls=%async_computation.2 | async-start | bytes 524288 | tf_op jit(solution)/shard_map/all_to_all | solution.py:341
  56.6 0.0 copy-done.2
  56.6 6.9 %block_attention.1 = bf16[512,1024]{1,0:T(8,128)(2,1)} custom-call(s32[8]{0:T(128)S(1)} %get-tuple-element.9.info_ref, bf16[512,1024]{1,0:T(8,128)(2,1)S(1)} %copy-done.2, bf16[2,512,128]{2,1,0:T(8,128)(2,1)S(1)} %copy-done, bf16[16,160,128]{2,1,0:T(8,128)(2,1)S(1)} %all_to_all.16.own_ref, bf16[16,160,128]{2,1,0:T(8,128)(2,1)S(1)} %collective-permute-done.1.other_ref), custom_call_target="tpu_custom_call" | custom-call | flops 1073741824 | bytes 4194304 | tf_op jit(solution)/shard_map/block_attention/pallas_call | solution.py:342
  63.6 4.1 %all-to-all-done.2 = bf16[8,64,256]{2,1,0:T(8,128)(2,1)S(1)} async-done(((bf16[8,64,256]{2,1,0:T(8,128)(2,1)}), bf16[8,64,256]{2,1,0:T(8,128)(2,1)S(1)}, u32[]{:S(2)}, u32[]{:S(2)}) %all-to-all-start.2) | async-done | bytes 262176 | tf_op jit(solution)/shard_map/all_to_all | solution.py:341
  67.7 0.7 convert_reduce_fusion
Async XLA Ops:
  0.6 6.3 %copy-start = (bf16[2,512,128]{2,1,0:T(8,128)(2,1)S(1)}, bf16[2,512,128]{2,1,0:T(8,128)(2,1)}, u32[]{:S(2)}) copy-start(bf16[2,512,128]{2,1,0:T(8,128)(2,1)} %keyval_ref.1) | copy-start | bytes 786436
  0.6 6.3 %collective-permute-start = (bf16[2,512,128]{2,1,0:T(8,128)(2,1)}, bf16[2,512,128]{2,1,0:T(8,128)(2,1)S(1)}, u32[]{:S(2)}, u32[]{:S(2)}) collective-permute-start(bf16[2,512,128]{2,1,0:T(8,128)(2,1)} %keyval_ref.1), channel_id=1, source_target_pairs={{0,8},{8,0},{16,24},{24,16},{32,40},{40,32},{48,56},{56,48},{64,72... | collective-permute-start | bytes 786440 | tf_op jit(solution)/shard_map/ppermute | solution.py:283
  28.3 19.0 %copy-start.1 = (bf16[1024,256]{1,0:T(8,128)(2,1)S(1)}, bf16[1024,256]{1,0:T(8,128)(2,1)}, u32[]{:S(2)}) copy-start(bf16[1024,256]{1,0:T(8,128)(2,1)} %weight_ref.1) | copy-start | bytes 1572868
  43.0 13.7 %copy-start.2 = (bf16[512,1024]{1,0:T(8,128)(2,1)S(1)}, bf16[512,1024]{1,0:T(8,128)(2,1)}, u32[]{:S(2)}) copy-start(bf16[512,1024]{1,0:T(8,128)(2,1)} %query_ref.1) | copy-start | bytes 3145732
  43.0 4.3 %collective-permute-start.1 = (bf16[16,160,128]{2,1,0:T(8,128)(2,1)S(1)}, bf16[16,160,128]{2,1,0:T(8,128)(2,1)S(1)}, u32[]{:S(2)}, u32[]{:S(2)}) collective-permute-start(bf16[16,160,128]{2,1,0:T(8,128)(2,1)S(1)} %all_to_all.16.own_ref), channel_id=1, source_target_pairs={{0,8},{8,0},{16,24},{24,16},{32,40},{40,32},{48,56},{56,48},{64,72... | collective-permute-start | bytes 1966088 | tf_op jit(solution)/shard_map/ppermute | solution.py:331
  48.4 19.2 %all-to-all-start.2 = ((bf16[8,64,256]{2,1,0:T(8,128)(2,1)}), bf16[8,64,256]{2,1,0:T(8,128)(2,1)S(1)}, u32[]{:S(2)}, u32[]{:S(2)}) async-start(bf16[8,64,256]{2,1,0:T(8,128)(2,1)} %project.1), calls=%async_computation.2 | async-start | bytes 524288 | tf_op jit(solution)/shard_map/all_to_all | solution.py:341

commit v3 on v2

v3 whole, which is shorter than its diff:
```python
import math

import jax
import jax.numpy as jnp
from jax import lax
from jax.experimental import pallas as pl
from jax.experimental.pallas import tpu as pltpu
from jax.sharding import PartitionSpec as P

HD = 128
HEADS = 8
BLK = 256
NB = 32
CHIPS = 16
HALF = 128
STAT = 16
PIECE = 32
SCALE = 1.0 / math.sqrt(HD)
SCALE2 = SCALE * math.log2(math.e)
AHEAD = 2
masked_score = -1e30

SEND_ROWS = HALF + STAT + PIECE
SHARE_ROWS = HALF + PIECE

same_core = [[chip * 2 + core for chip in range(CHIPS)] for core in range(2)]
core_swap = [(device, device ^ 1) for device in range(2 * CHIPS)]

smem = pl.BlockSpec(memory_space=pltpu.SMEM)
vmem = pl.BlockSpec(memory_space=pltpu.VMEM)
hbm = pl.BlockSpec(memory_space=pltpu.HBM)


def params(room=40):
    return pltpu.CompilerParams(vmem_limit_bytes=room * 2**20)


def cost(flops, exps, size):
    return pl.CostEstimate(flops=flops, transcendentals=exps, bytes_accessed=size)


def split_three(value):
    high = value.astype(jnp.bfloat16)
    rest = value - high.astype(jnp.float32)
    middle = rest.astype(jnp.bfloat16)
    low = (rest - middle.astype(jnp.float32)).astype(jnp.bfloat16)
    return high, middle, low


def dot_nt(left, right):
    return lax.dot_general(
        left, right, (((1,), (1,)), ((), ())), preferred_element_type=jnp.float32
    )


def row_softmax(raw):
    top = jnp.max(raw, axis=1, keepdims=True)
    weights = jnp.exp2((raw - top) * SCALE2)
    return top, jnp.sum(weights, axis=1, keepdims=True), weights


def weigh(weights, values):
    return jnp.dot(weights.astype(jnp.bfloat16), values, preferred_element_type=jnp.float32)


def each_head(query_ref, keys):
    ready = []
    for head in range(HEADS + AHEAD):
        if head < HEADS:
            ready.append(dot_nt(query_ref[:, head * HD : (head + 1) * HD], keys))
        if head >= AHEAD:
            yield head - AHEAD, ready.pop(0)


def find_block(map_ref, device, core):
    slot = jnp.where(map_ref[2 * device] // NB == core, 0, 1)
    return slot, map_ref[2 * device + slot] - NB * core


def fetch_kernel(
    map_hbm,
    reach_hbm,
    query_hbm,
    keyval_hbm,
    window_hbm,
    query_ref,
    keyval_ref,
    mean_ref,
    level_ref,
    info_ref,
    window_ref,
    map_ref,
    reach_ref,
    done,
):
    position = lax.axis_index("ctx")
    core = position % 2
    chip = position // 2
    copies = [
        pltpu.make_async_copy(source, target, done.at[number])
        for number, (source, target) in enumerate(
            (
                (map_hbm, map_ref),
                (reach_hbm, reach_ref),
                (query_hbm.at[core], query_ref),
                (window_hbm.at[core], window_ref),
                (keyval_hbm, keyval_ref),
            )
        )
    ]
    for copy in copies:
        copy.start()
    for copy in copies[:2]:
        copy.wait()
    partner = position + 1 - 2 * core
    slot, place = find_block(map_ref, position, core)
    other_slot, other_place = find_block(map_ref, partner, core)
    holder = jnp.int32(0)
    for number in range(2 * NB):
        holder = jnp.where(map_ref[number] == core * NB, number // 4, holder)
    info_ref[0] = holder
    info_ref[1] = jnp.where(place < reach_ref[core], 1, 0)
    info_ref[2] = jnp.where(other_place < reach_ref[core], 1, 0)
    info_ref[3] = place
    info_ref[4] = other_slot
    info_ref[5] = slot
    info_ref[6] = map_ref[2 * position]
    info_ref[7] = map_ref[2 * position + 1]
    for copy in copies[2:]:
        copy.wait()
    half = chip % 2
    query_rows = pl.ds(pl.multiple_of(half * HALF, HALF), HALF)
    query_lanes = pl.ds(pl.multiple_of(chip // 2 * HD, HD), HD)
    raw = dot_nt(query_ref[query_rows, query_lanes], window_ref[0])
    key = lax.broadcasted_iota(jnp.int32, raw.shape, 1)
    row = lax.broadcasted_iota(jnp.int32, raw.shape, 0) + half * HALF
    raw = jnp.where(key <= row, raw, masked_score)
    top, total, weights = row_softmax(raw)
    mean_ref[...] = weigh(weights, window_ref[1]) / total
    level = jnp.broadcast_to(top * SCALE + jnp.log(total), (HALF, HALF)).T
    level_ref[...] = level[:8]


def window_kernel(info_ref, query_ref, own_ref, other_ref, send_ref, sum_ref):
    own_rows = pl.ds(pl.multiple_of(info_ref[5] * BLK, BLK), BLK)
    other_rows = pl.ds(pl.multiple_of(info_ref[4] * BLK, BLK), BLK)
    keys = jnp.concatenate([own_ref[0, own_rows, :], other_ref[0, other_rows, :]], axis=0)
    values = (own_ref[1, own_rows, :], other_ref[1, other_rows, :])
    lane = lax.broadcasted_iota(jnp.int32, (BLK, HD), 1)
    columns = jnp.zeros((BLK, HD), jnp.float32)
    for head, raw in each_head(query_ref, keys):
        for part in range(2):
            top, total, weights = row_softmax(raw[:, part * BLK : (part + 1) * BLK])
            sum_ref[part, :, head * HD : (head + 1) * HD] = weigh(weights, values[part])
            columns = jnp.where(lane == part * HEADS + head, top, columns)
            columns = jnp.where(lane == (2 + part) * HEADS + head, total, columns)
    table = columns.T
    table = [table[number * HEADS : (number + 1) * HEADS] for number in range(4)]
    lives = [info_ref[1 + part] == 1 for part in range(2)]
    tops = [
        jnp.where(live, top * SCALE, masked_score) for live, top in zip(lives, table[:2])
    ]
    joined = jnp.maximum(tops[0], tops[1])
    lifts = [jnp.where(live, jnp.exp(top - joined), 0.0) for live, top in zip(lives, tops)]
    total = table[2] * lifts[0] + table[3] * lifts[1]
    some = total > 0.0
    safe = jnp.where(some, total, 1.0)
    inverse = jnp.where(some, 1.0 / safe, 0.0)
    level = jnp.where(some, joined + jnp.log(safe), masked_score)
    blank = jnp.zeros((HD - 2 * HEADS, BLK), jnp.float32)
    lifts = jnp.concatenate([lifts[0] * inverse, lifts[1] * inverse, blank], axis=0).T
    pieces = [piece.astype(jnp.float32) for piece in split_three(level)]
    row = lax.broadcasted_iota(jnp.int32, (STAT, BLK), 0)
    for head in range(HEADS):
        lanes = slice(head * HD, (head + 1) * HD)
        mean = (
            sum_ref[0, :, lanes] * lifts[:, head : head + 1]
            + sum_ref[1, :, lanes] * lifts[:, HEADS + head : HEADS + head + 1]
        ).astype(jnp.bfloat16)
        stats = jnp.zeros((STAT, BLK), jnp.float32)
        for number, piece in enumerate(pieces):
            stats = jnp.where(row == number, piece[head : head + 1], stats)
        stats = stats.astype(jnp.bfloat16)
        for half in range(2):
            rows = slice(half * HALF, (half + 1) * HALF)
            send_ref[2 * head + half, :HALF, :] = mean[rows]
            send_ref[2 * head + half, HALF : HALF + STAT, :] = stats[:, rows]
    first = info_ref[3] == 0
    for member in range(2):
        block = jnp.where(first, own_ref[member, own_rows, :], other_ref[member, other_rows, :])
        send_ref[8 * member : 8 * member + 8, HALF + STAT :, :] = block.reshape(8, PIECE, HD)


def combine_kernel(info_ref, got_ref, mean_ref, level_ref, share_ref):
    levels = []
    for source in range(CHIPS):
        stats = got_ref[source, HALF : HALF + STAT, :].astype(jnp.float32)
        levels.append(stats[0:1] + stats[1:2] + stats[2:3])
    levels.append(level_ref[0:1, :])
    levels = jnp.concatenate(levels, axis=0)
    lifts = jnp.exp(levels - jnp.max(levels, axis=0, keepdims=True))
    lifts = lifts / jnp.sum(lifts, axis=0, keepdims=True)
    blank = jnp.zeros((HALF - CHIPS - 1, HALF), jnp.float32)
    lifts = jnp.concatenate([lifts, blank], axis=0).T
    joined = mean_ref[...] * lifts[:, CHIPS : CHIPS + 1]
    for source in range(CHIPS):
        part = got_ref[source, :HALF, :].astype(jnp.float32)
        joined = joined + part * lifts[:, source : source + 1]
    result = joined.astype(jnp.bfloat16)
    piece = got_ref[info_ref[0], HALF + STAT :, :]
    for target in range(CHIPS):
        share_ref[target, :HALF, :] = result
        share_ref[target, HALF:, :] = piece


def project_kernel(own_ref, other_ref, weight_ref, out_ref):
    core = lax.axis_index("ctx") % 2
    rows = jnp.concatenate(
        [
            jnp.concatenate([ref[2 * head + half, :HALF, :] for head in range(HEADS)], axis=1)
            for ref in (own_ref, other_ref)
            for half in range(2)
        ],
        axis=0,
    )
    result = jnp.dot(rows, weight_ref[...], preferred_element_type=jnp.float32)
    result = result.reshape(8, 64, BLK).astype(out_ref.dtype)
    out_ref[pl.ds(core * 4, 4)] = result[:4]
    out_ref[pl.ds(4 - core * 4, 4)] = result[4:]


def block_kernel(info_ref, query_ref, keyval_ref, own_ref, other_ref, out_ref):
    core = lax.axis_index("ctx") % 2
    block = info_ref[6 + pl.program_id(0)]
    mine = block // NB == core
    bias = jnp.where(block % NB != 0, 0.0, masked_score)

    def anchor(member):
        taken = slice(8 * member, 8 * member + 8)
        own = own_ref[taken, HALF:, :].reshape(BLK, HD)
        other = other_ref[taken, HALF:, :].reshape(BLK, HD)
        return jnp.where(mine, own, other)

    keys = jnp.concatenate([anchor(0), keyval_ref[0]], axis=0)
    values = jnp.concatenate([anchor(1), keyval_ref[1]], axis=0)
    key = lax.broadcasted_iota(jnp.int32, (BLK, BLK), 1)
    row = lax.broadcasted_iota(jnp.int32, (BLK, BLK), 0)
    live = key <= row
    for head, raw in each_head(query_ref, keys):
        raw = jnp.concatenate(
            [raw[:, :BLK] + bias, jnp.where(live, raw[:, BLK:], masked_score)], axis=1
        )
        _, total, weights = row_softmax(raw)
        result = weigh(weights, values) / total
        out_ref[:, head * HD : (head + 1) * HD] = result.astype(jnp.bfloat16)


def far(array):
    return pltpu.with_memory_space_constraint(array, pltpu.HBM)


def shaped(shape, dtype):
    return jax.ShapeDtypeStruct(shape, dtype)


def on_device(
    ctx_queries, ctx_keyvals, block_map, window_reach, win_queries, win_keyvals, out_weight
):
    other_keyvals = lax.ppermute(ctx_keyvals, "ctx", core_swap)
    queries, keyvals, own_mean, own_level, info = pl.pallas_call(
        fetch_kernel,
        out_shape=(
            shaped((BLK, HEADS * HD), jnp.bfloat16),
            shaped((2, 2 * BLK, HD), jnp.bfloat16),
            shaped((HALF, HD), jnp.float32),
            shaped((8, HALF), jnp.float32),
            shaped((8,), jnp.int32),
        ),
        in_specs=[hbm] * 5,
        out_specs=(vmem,) * 4 + (smem,),
        scratch_shapes=[
            pltpu.VMEM((2, BLK, HD), jnp.bfloat16),
            pltpu.SMEM((2 * NB,), jnp.int32),
            pltpu.SMEM((2,), jnp.int32),
            pltpu.SemaphoreType.DMA((5,)),
        ],
        compiler_params=params(),
        cost_estimate=cost(2**24, 2**15, 2**21),
        name="window_fetch",
    )(
        *(far(array) for array in (block_map, window_reach, win_queries, ctx_keyvals, win_keyvals))
    )
    send = pl.pallas_call(
        window_kernel,
        out_shape=shaped((CHIPS, SEND_ROWS, HD), jnp.bfloat16),
        in_specs=[smem] + [vmem] * 3,
        out_specs=vmem,
        scratch_shapes=[pltpu.VMEM((2, BLK, HEADS * HD), jnp.float32)],
        compiler_params=params(),
        cost_estimate=cost(2**29, 2**20, 2**21),
        name="window_parts",
    )(info, queries, keyvals, other_keyvals)
    got = lax.all_to_all(send, "ctx", 0, 0, axis_index_groups=same_core, tiled=True)
    share = pl.pallas_call(
        combine_kernel,
        out_shape=shaped((CHIPS, SHARE_ROWS, HD), jnp.bfloat16),
        in_specs=[smem, vmem, vmem, vmem],
        out_specs=vmem,
        compiler_params=params(),
        cost_estimate=cost(2**20, 2**12, 2**20),
        name="window_join",
    )(info, got, own_mean, own_level)
    rows_own = lax.all_to_all(share, "ctx", 0, 0, axis_index_groups=same_core, tiled=True)
    rows_other = lax.ppermute(rows_own, "ctx", core_swap)
    shares = pl.pallas_call(
        project_kernel,
        out_shape=shaped((8, 64, BLK), jnp.bfloat16),
        in_specs=[vmem, vmem, vmem],
        out_specs=vmem,
        compiler_params=params(),
        cost_estimate=cost(2**28, 0, 2**21),
        name="project",
    )(rows_own, rows_other, out_weight)
    summands = lax.all_to_all(shares, "tp", 0, 0, tiled=True)
    context_attn = pl.pallas_call(
        block_kernel,
        out_shape=shaped((2 * BLK, HEADS * HD), jnp.bfloat16),
        grid=(2,),
        in_specs=[
            smem,
            pl.BlockSpec((BLK, HEADS * HD), lambda slot: (slot, 0)),
            pl.BlockSpec((2, BLK, HD), lambda slot: (0, slot, 0)),
            pl.BlockSpec((CHIPS, SHARE_ROWS, HD), lambda slot: (0, 0, 0)),
            pl.BlockSpec((CHIPS, SHARE_ROWS, HD), lambda slot: (0, 0, 0)),
        ],
        out_specs=pl.BlockSpec((BLK, HEADS * HD), lambda slot: (slot, 0)),
        compiler_params=params(),
        cost_estimate=cost(2**30, 2**21, 2**22),
        name="block_attention",
    )(info, ctx_queries, ctx_keyvals, rows_own, rows_other)
    window_proj = jnp.sum(summands.astype(jnp.float32), axis=0)
    return (context_attn, window_proj)


def solution(mesh):
    return jax.shard_map(
        on_device,
        mesh=mesh,
        in_specs=(
            P("ctx", "tp"),
            P(None, "ctx", "tp"),
            P(),
            P(),
            P(None, None, "tp"),
            P(None, None, None, "tp"),
            P("tp", "ctx"),
        ),
        out_specs=(P("ctx", "tp"), P("tp", "ctx")),
        check_vma=False,
    )
```

time: 68.6 us -> 68.2 us (level)
  Pallas kernels: 14.6 us -> 11.5 us
  waiting for transfers between devices: 5.82 us -> 8.35 us
    all_to_all x1, waiting for transfers between devices: 4.09 us -> 6.63 us  [on_device(): summands = lax.all_to_all(shares, 'tp', 0, 0, tiled=True)]
    pallas_call x1, Pallas kernels: 6.95 us -> 4.45 us  [on_device(): pl.pallas_call(block_kernel, out_shape=shaped((2 * BLK, HEADS * HD), jnp....]
  transfers between devices with their start and end apart: 3 -> 3, of which waited for: 2 -> 2; matrix products, arithmetic and copies ran while one was open for 0% -> 0% of each run, Pallas kernels for 15% -> 9%
where the time goes in v3:
time: 68.2 us; the launch traced here: 67.9 us
  blocking collectives  32.4 us (48%)
  starting transfers between devices  14.3 us (21%)
  Pallas kernels  11.5 us (17%)
  waiting for transfers between devices  8.35 us (12%)
    all_to_all x1, blocking collectives, on_device(): lax.all_to_all(send, 'ctx', 0, 0, axis_index_groups=same_core, tiled=True)  17.7 us
    all_to_all x1, blocking collectives, on_device(): lax.all_to_all(share, 'ctx', 0, 0, axis_index_groups=same_core, tiled=True)  14.7 us
    all_to_all x1, starting transfers between devices, on_device(): summands = lax.all_to_all(shares, 'tp', 0, 0, tiled=True)  8.32 us
    all_to_all x1, waiting for transfers between devices, on_device(): summands = lax.all_to_all(shares, 'tp', 0, 0, tiled=True)  6.63 us
    pallas_call x1, Pallas kernels, on_device(): pl.pallas_call(block_kernel, out_shape=shaped((2 * BLK, HEADS * HD), jnp....  4.45 us
    ppermute x1, starting transfers between devices, on_device(): other_keyvals = lax.ppermute(ctx_keyvals, 'ctx', core_swap)  3.33 us
    pallas_call x1, Pallas kernels, on_device(): pl.pallas_call(window_kernel, out_shape=shaped((CHIPS, SEND_ROWS, HD), jn...  2.98 us
    ppermute x1, starting transfers between devices, on_device(): rows_other = lax.ppermute(rows_own, 'ctx', core_swap)  2.61 us
  transfers between devices with their start and end apart: 3, of which 2 were waited for; matrix products, arithmetic and copies ran while one was open for 0% of the time, Pallas kernels for 9%

profile of v3, /device:TPU:1, one launch (start us, length us, event | category | flops | bytes accessed | tf_op | source)
XLA Modules:
  0.0 67.9 jit_solution(6598447477105979221)
XLA Ops:
  0.6 3.3 %collective-permute-start = (bf16[2,512,128]{2,1,0:T(8,128)(2,1)}, bf16[2,512,128]{2,1,0:T(8,128)(2,1)S(1)}, u32[]{:S(2)}, u32[]{:S(2)}) collective-permute-start(bf16[2,512,128]{2,1,0:T(8,128)(2,1)} %keyval_ref.1), channel_id=1, source_target_pairs={{0,8},{8,0},{16,24},{24,16},{32,40},{40,32},{48,56},{56,48},{64,72... | collective-permute-start | bytes 786440 | tf_op jit(solution)/shard_map/ppermute | solution.py:269
  4.0 1.8 %window_fetch.1 = (bf16[256,1024]{1,0:T(8,128)(2,1)S(1)}, bf16[2,512,128]{2,1,0:T(8,128)(2,1)S(1)}, f32[128,128]{1,0:T(8,128)S(1)}, f32[8,128]{1,0:T(8,128)S(1)}, s32[8]{0:T(128)S(1)}) custom-call(s32[64]{0:T(128)} %map_hbm.1, s32[2]{0:T(128)} %reach_hbm.1, bf16[2,256,1024]{2,1,0:T(8,128)(2,1)} %query_hbm.1, bf16[2,512,128]{2,1,0:T(8,128)(2,1)} %keyval_ref.1, ...), custom_call_target="tpu_custom_call" | custom-call | flops 16777216 | bytes 2097152 | tf_op jit(solution)/shard_map/window_fetch/pallas_call | solution.py:270
  5.8 0.0 collective-permute-done.other_ref
  5.8 3.0 %window_parts.1 = bf16[16,176,128]{2,1,0:T(8,128)(2,1)S(1)} custom-call(s32[8]{0:T(128)S(1)} %get-tuple-element.7.info_ref, bf16[256,1024]{1,0:T(8,128)(2,1)S(1)} %get-tuple-element.8.query_ref, bf16[2,512,128]{2,1,0:T(8,128)(2,1)S(1)} %get-tuple-element.9.own_ref, bf16[2,512,128]{2,1,0:T(8,128)(2,1)S(1)} %collective-permute-done.other_ref), custom_call_target="tpu_custom_call" | custom-call | flops 536870912 | bytes 2097152 | tf_op jit(solution)/shard_map/window_parts/pallas_call | solution.py:293
  8.7 17.7 %all_to_all.15.got_ref = bf16[16,176,128]{2,1,0:T(8,128)(2,1)S(1)} all-to-all(bf16[16,176,128]{2,1,0:T(8,128)(2,1)S(1)} %window_parts.1), channel_id=1, replica_groups={{0,16,32,48,64,80,96,112,128,144,160,176,192,208,224,240},{8,24,40,56,7..., dimensions={0} | all-to-all | bytes 1441792 | tf_op jit(solution)/shard_map/all_to_all | solution.py:303
  26.5 1.1 %window_join.1 = bf16[16,160,128]{2,1,0:T(8,128)(2,1)S(1)} custom-call(s32[8]{0:T(128)S(1)} %get-tuple-element.7.info_ref, bf16[16,176,128]{2,1,0:T(8,128)(2,1)S(1)} %all_to_all.15.got_ref, f32[128,128]{1,0:T(8,128)S(1)} %get-tuple-element.10.mean_ref, f32[8,128]{1,0:T(8,128)S(1)} %get-tuple-element.11.level_ref), custom_call_target="tpu_custom_call" | custom-call | flops 1048576 | bytes 1048576 | tf_op jit(solution)/shard_map/window_join/pallas_call | solution.py:304
  27.6 0.0 copy-start
  27.6 14.7 %all_to_all.16.own_ref = bf16[16,160,128]{2,1,0:T(8,128)(2,1)S(1)} all-to-all(bf16[16,160,128]{2,1,0:T(8,128)(2,1)S(1)} %window_join.1), channel_id=1, replica_groups={{0,16,32,48,64,80,96,112,128,144,160,176,192,208,224,240},{8,24,40,56,7..., dimensions={0} | all-to-all | bytes 1310720 | tf_op jit(solution)/shard_map/all_to_all | solution.py:313
  42.3 0.0 copy-start.2
  42.3 2.6 %collective-permute-start.1 = (bf16[16,160,128]{2,1,0:T(8,128)(2,1)S(1)}, bf16[16,160,128]{2,1,0:T(8,128)(2,1)S(1)}, u32[]{:S(2)}, u32[]{:S(2)}) collective-permute-start(bf16[16,160,128]{2,1,0:T(8,128)(2,1)S(1)} %all_to_all.16.own_ref), channel_id=1, source_target_pairs={{0,8},{8,0},{16,24},{24,16},{32,40},{40,32},{48,56},{56,48},{64,72... | collective-permute-start | bytes 1966088 | tf_op jit(solution)/shard_map/ppermute | solution.py:314
  44.9 1.7 %collective-permute-done.1.other_ref = bf16[16,160,128]{2,1,0:T(8,128)(2,1)S(1)} collective-permute-done((bf16[16,160,128]{2,1,0:T(8,128)(2,1)S(1)}, bf16[16,160,128]{2,1,0:T(8,128)(2,1)S(1)}, u32[]{:S(2)}, u32[]{:S(2)}) %collective-permute-start.1) | collective-permute-done | bytes 655392 | tf_op jit(solution)/shard_map/ppermute | solution.py:314
  46.7 0.0 copy-done
  46.7 1.1 %project.1 = bf16[8,64,256]{2,1,0:T(8,128)(2,1)} custom-call(bf16[16,160,128]{2,1,0:T(8,128)(2,1)S(1)} %all_to_all.16.own_ref, bf16[16,160,128]{2,1,0:T(8,128)(2,1)S(1)} %collective-permute-done.1.other_ref, bf16[1024,256]{1,0:T(8,128)(2,1)S(1)} %copy-done), custom_call_target="tpu_custom_call" | custom-call | flops 268435456 | bytes 2097152 | tf_op jit(solution)/shard_map/project/pallas_call | solution.py:315
  47.8 0.0 copy-start.1
  47.8 8.3 %all-to-all-start.2 = ((bf16[8,64,256]{2,1,0:T(8,128)(2,1)}), bf16[8,64,256]{2,1,0:T(8,128)(2,1)S(1)}, u32[]{:S(2)}, u32[]{:S(2)}) async-start(bf16[8,64,256]{2,1,0:T(8,128)(2,1)} %project.1), calls=%async_computation.2 | async-start | bytes 524288 | tf_op jit(solution)/shard_map/all_to_all | solution.py:324
  56.1 0.0 copy-done.2
  56.1 0.0 copy-done.1
  56.1 4.5 %block_attention.1 = bf16[512,1024]{1,0:T(8,128)(2,1)} custom-call(s32[8]{0:T(128)S(1)} %get-tuple-element.7.info_ref, bf16[512,1024]{1,0:T(8,128)(2,1)S(1)} %copy-done.2, bf16[2,512,128]{2,1,0:T(8,128)(2,1)S(1)} %copy-done.1, bf16[16,160,128]{2,1,0:T(8,128)(2,1)S(1)} %all_to_all.16.own_ref, bf16[16,160,128]{2,1,0:T(8,128)(2,1)S(1)} %collective-permute-done.1.other_ref), custom_call_target="tpu_custom_call" | custom-call | flops 1073741824 | bytes 4194304 | tf_op jit(solution)/shard_map/block_attention/pallas_call | solution.py:325
  60.6 6.6 %all-to-all-done.2 = bf16[8,64,256]{2,1,0:T(8,128)(2,1)S(1)} async-done(((bf16[8,64,256]{2,1,0:T(8,128)(2,1)}), bf16[8,64,256]{2,1,0:T(8,128)(2,1)S(1)}, u32[]{:S(2)}, u32[]{:S(2)}) %all-to-all-start.2) | async-done | bytes 262176 | tf_op jit(solution)/shard_map/all_to_all | solution.py:324
  67.2 0.7 convert_reduce_fusion
Async XLA Ops:
  0.6 5.1 %collective-permute-start = (bf16[2,512,128]{2,1,0:T(8,128)(2,1)}, bf16[2,512,128]{2,1,0:T(8,128)(2,1)S(1)}, u32[]{:S(2)}, u32[]{:S(2)}) collective-permute-start(bf16[2,512,128]{2,1,0:T(8,128)(2,1)} %keyval_ref.1), channel_id=1, source_target_pairs={{0,8},{8,0},{16,24},{24,16},{32,40},{40,32},{48,56},{56,48},{64,72... | collective-permute-start | bytes 786440 | tf_op jit(solution)/shard_map/ppermute | solution.py:269
  27.6 19.0 %copy-start = (bf16[1024,256]{1,0:T(8,128)(2,1)S(1)}, bf16[1024,256]{1,0:T(8,128)(2,1)}, u32[]{:S(2)}) copy-start(bf16[1024,256]{1,0:T(8,128)(2,1)} %weight_ref.1) | copy-start | bytes 1572868
  42.3 13.8 %copy-start.2 = (bf16[512,1024]{1,0:T(8,128)(2,1)S(1)}, bf16[512,1024]{1,0:T(8,128)(2,1)}, u32[]{:S(2)}) copy-start(bf16[512,1024]{1,0:T(8,128)(2,1)} %query_ref.1) | copy-start | bytes 3145732
  42.3 4.3 %collective-permute-start.1 = (bf16[16,160,128]{2,1,0:T(8,128)(2,1)S(1)}, bf16[16,160,128]{2,1,0:T(8,128)(2,1)S(1)}, u32[]{:S(2)}, u32[]{:S(2)}) collective-permute-start(bf16[16,160,128]{2,1,0:T(8,128)(2,1)S(1)} %all_to_all.16.own_ref), channel_id=1, source_target_pairs={{0,8},{8,0},{16,24},{24,16},{32,40},{40,32},{48,56},{56,48},{64,72... | collective-permute-start | bytes 1966088 | tf_op jit(solution)/shard_map/ppermute | solution.py:314
  47.8 8.3 %copy-start.1 = (bf16[2,512,128]{2,1,0:T(8,128)(2,1)S(1)}, bf16[2,512,128]{2,1,0:T(8,128)(2,1)}, u32[]{:S(2)}) copy-start(bf16[2,512,128]{2,1,0:T(8,128)(2,1)} %keyval_ref.1) | copy-start | bytes 786436
  47.8 19.4 %all-to-all-start.2 = ((bf16[8,64,256]{2,1,0:T(8,128)(2,1)}), bf16[8,64,256]{2,1,0:T(8,128)(2,1)S(1)}, u32[]{:S(2)}, u32[]{:S(2)}) async-start(bf16[8,64,256]{2,1,0:T(8,128)(2,1)} %project.1), calls=%async_computation.2 | async-start | bytes 524288 | tf_op jit(solution)/shard_map/all_to_all | solution.py:324

commit v4 on v3

v4 whole, which is shorter than its diff:
```python
import math

import jax
import jax.numpy as jnp
from jax import lax
from jax.experimental import pallas as pl
from jax.experimental.pallas import tpu as pltpu
from jax.sharding import PartitionSpec as P

HD = 128
HEADS = 8
BLK = 256
NB = 32
CHIPS = 16
HALF = 128
STAT = 16
PIECE = 32
SHARE = 32
SCALE = 1.0 / math.sqrt(HD)
SCALE2 = SCALE * math.log2(math.e)
AHEAD = 2
masked_score = -1e30

SEND_ROWS = HALF + STAT + PIECE
SHARE_ROWS = HALF + PIECE

same_core = [[chip * 2 + core for chip in range(CHIPS)] for core in range(2)]
core_swap = [(device, device ^ 1) for device in range(2 * CHIPS)]

smem = pl.BlockSpec(memory_space=pltpu.SMEM)
vmem = pl.BlockSpec(memory_space=pltpu.VMEM)
hbm = pl.BlockSpec(memory_space=pltpu.HBM)


def params(room=40):
    return pltpu.CompilerParams(vmem_limit_bytes=room * 2**20)


def cost(flops, exps, size):
    return pl.CostEstimate(flops=flops, transcendentals=exps, bytes_accessed=size)


def split_three(value):
    high = value.astype(jnp.bfloat16)
    rest = value - high.astype(jnp.float32)
    middle = rest.astype(jnp.bfloat16)
    low = (rest - middle.astype(jnp.float32)).astype(jnp.bfloat16)
    return high, middle, low


def dot_nt(left, right):
    return lax.dot_general(
        left, right, (((1,), (1,)), ((), ())), preferred_element_type=jnp.float32
    )


def row_softmax(raw):
    top = jnp.max(raw, axis=1, keepdims=True)
    weights = jnp.exp2((raw - top) * SCALE2)
    return top, jnp.sum(weights, axis=1, keepdims=True), weights


def weigh(weights, values):
    return jnp.dot(weights.astype(jnp.bfloat16), values, preferred_element_type=jnp.float32)


def each_head(query_ref, keys):
    ready = []
    for head in range(HEADS + AHEAD):
        if head < HEADS:
            ready.append(dot_nt(query_ref[:, head * HD : (head + 1) * HD], keys))
        if head >= AHEAD:
            yield head - AHEAD, ready.pop(0)


def fetch_kernel(
    map_hbm,
    reach_hbm,
    query_hbm,
    keyval_hbm,
    window_hbm,
    query_ref,
    keyval_ref,
    mean_ref,
    level_ref,
    info_ref,
    window_ref,
    map_ref,
    reach_ref,
    done,
):
    position = lax.axis_index("ctx")
    core = position % 2
    chip = position // 2
    copies = [
        pltpu.make_async_copy(source, target, done.at[number])
        for number, (source, target) in enumerate(
            (
                (map_hbm, map_ref),
                (reach_hbm, reach_ref),
                (query_hbm.at[:, :, core], query_ref),
                (window_hbm.at[chip % 2], window_ref),
                (keyval_hbm, keyval_ref),
            )
        )
    ]
    for copy in copies:
        copy.start()
    for copy in copies[:2]:
        copy.wait()
    partner = position + 1 - 2 * core
    holder = jnp.int32(0)
    for number in range(2 * NB):
        holder = jnp.where(map_ref[number] == core * NB, number // 4, holder)
    info_ref[0] = holder
    for part, device in enumerate((position, partner)):
        info_ref[1 + part] = jnp.where(map_ref[2 * device] // NB == 0, 0, 1)
        for context in range(2):
            slot = jnp.where(map_ref[2 * device] // NB == context, 0, 1)
            place = map_ref[2 * device + slot] - NB * context
            info_ref[3 + 2 * context + part] = jnp.where(place < reach_ref[context], 1, 0)
    slot = jnp.where(map_ref[2 * position] // NB == core, 0, 1)
    info_ref[7] = map_ref[2 * position + slot] - NB * core
    info_ref[8] = core
    info_ref[9] = map_ref[2 * position]
    info_ref[10] = map_ref[2 * position + 1]
    for copy in copies[2:]:
        copy.wait()
    lanes = pl.ds(pl.multiple_of(chip // 2 * HD, HD), HD)
    query = query_ref[chip % 2, :, :, lanes].reshape(HALF, HD)
    raw = dot_nt(query, window_ref[0])
    key = lax.broadcasted_iota(jnp.int32, raw.shape, 1)
    row = lax.broadcasted_iota(jnp.int32, raw.shape, 0)
    row = row // SHARE * (2 * SHARE) + core * SHARE + row % SHARE
    raw = jnp.where(key <= row, raw, masked_score)
    top, total, weights = row_softmax(raw)
    mean_ref[...] = weigh(weights, window_ref[1]) / total
    level = jnp.broadcast_to(top * SCALE + jnp.log(total), (HALF, HALF)).T
    level_ref[...] = level[:8]


def window_kernel(
    info_ref,
    query_ref,
    own_ref,
    other_ref,
    rows_hbm,
    send_ref,
    score_hbm,
    score_ref,
    rows_ref,
    done,
):
    copy = pltpu.make_async_copy(rows_hbm.at[:BLK], rows_ref, done.at[0])

    @pl.when(info_ref[8] == 0)
    def _():
        copy.start()

    def block_rows(part, context):
        slot = info_ref[1 + part]
        slot = slot if context == 0 else 1 - slot
        return pl.ds(pl.multiple_of(slot * BLK, BLK), BLK)

    sources = (own_ref, other_ref)
    lane = lax.broadcasted_iota(jnp.int32, (BLK, HD), 1)
    columns = jnp.zeros((BLK, HD), jnp.float32)
    steps = [(context, pair) for context in range(2) for pair in range(HEADS // 2)]
    keys = []
    values = []
    biases = []
    for context in range(2):
        rows = [block_rows(part, context) for part in range(2)]
        keys.append(
            jnp.concatenate([ref[0, taken, :] for ref, taken in zip(sources, rows)], axis=0)
        )
        values.append([ref[1, taken, :] for ref, taken in zip(sources, rows)])
        biases.append(
            [
                jnp.where(info_ref[3 + 2 * context + part] == 1, 0.0, masked_score)
                for part in range(2)
            ]
        )

    def score(step):
        context, pair = steps[step]
        query = jnp.concatenate(
            [
                query_ref[context, :, :, head * HD : (head + 1) * HD].reshape(HALF, HD)
                for head in (2 * pair, 2 * pair + 1)
            ],
            axis=0,
        )
        return dot_nt(query, keys[context])

    ready = [score(step) for step in range(AHEAD)]
    for step, (context, pair) in enumerate(steps):
        if step + AHEAD < len(steps):
            ready.append(score(step + AHEAD))
        raw = ready.pop(0)
        parts = []
        for part in range(2):
            top, total, weights = row_softmax(raw[:, part * BLK : (part + 1) * BLK])
            parts.append(
                (top + biases[context][part], total, weigh(weights, values[context][part]))
            )
        joined = jnp.maximum(parts[0][0], parts[1][0])
        lifts = [jnp.exp2((part[0] - joined) * SCALE2) for part in parts]
        total = parts[0][1] * lifts[0] + parts[1][1] * lifts[1]
        inverse = 1.0 / total
        mean = parts[0][2] * (lifts[0] * inverse) + parts[1][2] * (lifts[1] * inverse)
        mean = mean.astype(jnp.bfloat16)
        for half in range(2):
            target = 2 * (2 * pair + half) + context
            send_ref[target, :HALF, :] = mean[half * HALF : (half + 1) * HALF]
        columns = jnp.where(lane == step, joined, columns)
        columns = jnp.where(lane == len(steps) + step, total, columns)
    table = columns.T
    level = table[:HEADS] * SCALE + jnp.log(table[HEADS : 2 * HEADS])
    pieces = [piece.astype(jnp.float32) for piece in split_three(level)]
    row = lax.broadcasted_iota(jnp.int32, (STAT, BLK), 0)
    for step, (context, pair) in enumerate(steps):
        stats = jnp.zeros((STAT, BLK), jnp.float32)
        for number, piece in enumerate(pieces):
            stats = jnp.where(row == number, piece[step : step + 1], stats)
        stats = stats.astype(jnp.bfloat16)
        for half in range(2):
            target = 2 * (2 * pair + half) + context
            lanes = slice(half * HALF, (half + 1) * HALF)
            send_ref[target, HALF : HALF + STAT, :] = stats[:, lanes]
    first = info_ref[7] == 0
    own_rows, other_rows = [
        pl.ds(pl.multiple_of((info_ref[1 + part] ^ info_ref[8]) * BLK, BLK), BLK)
        for part in range(2)
    ]
    for member in range(2):
        block = jnp.where(first, own_ref[member, own_rows, :], other_ref[member, other_rows, :])
        send_ref[8 * member : 8 * member + 8, HALF + STAT :, :] = block.reshape(8, PIECE, HD)

    @pl.when(info_ref[8] == 0)
    def _():
        copy.wait()
        for head in range(HEADS):
            query = rows_ref[:, head * HD : (head + 1) * HD]
            score_ref[head] = dot_nt(query, own_ref[0, :BLK, :])
        copy_out = pltpu.make_async_copy(score_ref, score_hbm, done.at[1])
        copy_out.start()
        copy_out.wait()


def combine_kernel(info_ref, got_ref, mean_ref, level_ref, share_ref):
    levels = []
    for source in range(CHIPS):
        stats = got_ref[source, HALF : HALF + STAT, :].astype(jnp.float32)
        levels.append(stats[0:1] + stats[1:2] + stats[2:3])
    levels.append(level_ref[0:1, :])
    levels = jnp.concatenate(levels, axis=0)
    lifts = jnp.exp(levels - jnp.max(levels, axis=0, keepdims=True))
    lifts = lifts / jnp.sum(lifts, axis=0, keepdims=True)
    count = 3 * (CHIPS + 1)
    source_of = lax.broadcasted_iota(jnp.int32, (count, (CHIPS + 1) * HALF), 0) % (CHIPS + 1)
    column = lax.broadcasted_iota(jnp.int32, (count, (CHIPS + 1) * HALF), 1) // HALF
    spread = jnp.where(source_of == column, 1.0, 0.0).astype(jnp.bfloat16)
    wide = lax.dot_general(
        jnp.concatenate(split_three(lifts), axis=0),
        spread,
        (((0,), (0,)), ((), ())),
        preferred_element_type=jnp.float32,
    )
    joined = mean_ref[...] * wide[:, CHIPS * HALF :]
    for source in range(CHIPS):
        part = got_ref[source, :HALF, :].astype(jnp.float32)
        joined = joined + part * wide[:, source * HALF : (source + 1) * HALF]
    result = joined.astype(jnp.bfloat16)
    piece = got_ref[info_ref[0], HALF + STAT :, :]
    for target in range(CHIPS):
        share_ref[target, :HALF, :] = result
        share_ref[target, HALF:, :] = piece


def project_kernel(rows_ref, own_ref, other_ref, out_ref, anchor_ref):
    rows = jnp.concatenate(
        [
            jnp.concatenate(
                [rows_ref[2 * head + context, :HALF, :] for head in range(HEADS)], axis=1
            )
            for context in range(2)
        ],
        axis=0,
    )
    core = lax.axis_index("ctx") % 2

    def fill(weights):
        for number, ref in enumerate(weights):
            result = jnp.dot(rows, ref[...], preferred_element_type=jnp.float32)
            lanes = slice(number * BLK, (number + 1) * BLK)
            out_ref[:, :, lanes] = result.reshape(8, SHARE, BLK).astype(out_ref.dtype)

    @pl.when(core == 0)
    def _():
        fill((own_ref, other_ref))

    @pl.when(core == 1)
    def _():
        fill((other_ref, own_ref))

    anchor_ref[...] = rows_ref[:, HALF:, :].reshape(2, BLK, HD)


def total_kernel(parts_ref, mine_ref, theirs_ref):
    core = lax.axis_index("ctx") % 2
    for number in range(2):
        lanes = slice(number * BLK, (number + 1) * BLK)
        total = parts_ref[0, :, lanes].astype(jnp.float32)
        for plane in range(1, 8):
            total = total + parts_ref[plane, :, lanes].astype(jnp.float32)

        @pl.when(core == number)
        def _(total=total):
            mine_ref[...] = total

        @pl.when(core != number)
        def _(total=total):
            theirs_ref[...] = total


def block_kernel(
    info_ref, query_ref, keyval_ref, own_ref, other_ref, score_hbm, out_ref, score_ref, done
):
    step = pl.program_id(0)
    scored = (step == 1) & (info_ref[8] == 0)
    block = info_ref[10 - step]
    copy = pltpu.make_async_copy(score_hbm, score_ref, done)

    @pl.when((step == 0) & (info_ref[8] == 0))
    def _():
        copy.start()

    mine = block // NB == info_ref[8]
    bias = jnp.where(block % NB != 0, 0.0, masked_score)

    def anchor(member):
        return jnp.where(mine, own_ref[member], other_ref[member])

    values = jnp.concatenate([anchor(1), keyval_ref[1]], axis=0)
    key = lax.broadcasted_iota(jnp.int32, (BLK, BLK), 1)
    row = lax.broadcasted_iota(jnp.int32, (BLK, BLK), 0)
    live = key <= row

    def finish(head, former, latter):
        raw = jnp.concatenate([former + bias, jnp.where(live, latter, masked_score)], axis=1)
        _, total, weights = row_softmax(raw)
        result = weigh(weights, values) / total
        out_ref[:, head * HD : (head + 1) * HD] = result.astype(jnp.bfloat16)

    @pl.when(scored)
    def _():
        copy.wait()
        for head, raw in each_head(query_ref, anchor(0)):
            finish(head, raw, score_ref[head])

    @pl.when(jnp.logical_not(scored))
    def _():
        keys = jnp.concatenate([anchor(0), keyval_ref[0]], axis=0)
        for head, raw in each_head(query_ref, keys):
            finish(head, raw[:, :BLK], raw[:, BLK:])


def far(array):
    return pltpu.with_memory_space_constraint(array, pltpu.HBM)


def shaped(shape, dtype):
    return jax.ShapeDtypeStruct(shape, dtype)


def on_device(
    ctx_queries, ctx_keyvals, block_map, window_reach, win_queries, win_keyvals, out_weight
):
    other_keyvals = lax.ppermute(ctx_keyvals, "ctx", core_swap)
    halves = win_queries.reshape(2, 4, 2, SHARE, HEADS * HD)
    queries, keyvals, own_mean, own_level, info = pl.pallas_call(
        fetch_kernel,
        out_shape=(
            shaped((2, 4, SHARE, HEADS * HD), jnp.bfloat16),
            shaped((2, 2 * BLK, HD), jnp.bfloat16),
            shaped((HALF, HD), jnp.float32),
            shaped((8, HALF), jnp.float32),
            shaped((16,), jnp.int32),
        ),
        in_specs=[hbm] * 5,
        out_specs=(vmem,) * 4 + (smem,),
        scratch_shapes=[
            pltpu.VMEM((2, BLK, HD), jnp.bfloat16),
            pltpu.SMEM((2 * NB,), jnp.int32),
            pltpu.SMEM((2,), jnp.int32),
            pltpu.SemaphoreType.DMA((5,)),
        ],
        compiler_params=params(),
        cost_estimate=cost(2**24, 2**15, 2**21),
        name="window_fetch",
    )(
        *(far(array) for array in (block_map, window_reach, halves, ctx_keyvals, win_keyvals))
    )
    queries, other_keyvals, out_weight = lax.optimization_barrier(
        (queries, other_keyvals, out_weight)
    )
    other_weight = lax.ppermute(out_weight, "ctx", core_swap)
    send, scores = pl.pallas_call(
        window_kernel,
        out_shape=(
            shaped((CHIPS, SEND_ROWS, HD), jnp.bfloat16),
            pltpu.HBM((HEADS, BLK, BLK), jnp.float32),
        ),
        in_specs=[smem] + [vmem] * 3 + [hbm],
        out_specs=(vmem, hbm),
        scratch_shapes=[
            pltpu.VMEM((HEADS, BLK, BLK), jnp.float32),
            pltpu.VMEM((BLK, HEADS * HD), jnp.bfloat16),
            pltpu.SemaphoreType.DMA((2,)),
        ],
        compiler_params=params(),
        cost_estimate=cost(2**29, 2**20, 2**21),
        name="window_parts",
    )(info, queries, keyvals, other_keyvals, far(ctx_queries))
    send, other_weight = lax.optimization_barrier((send, other_weight))
    got = lax.all_to_all(send, "ctx", 0, 0, axis_index_groups=same_core, tiled=True)
    share = pl.pallas_call(
        combine_kernel,
        out_shape=shaped((CHIPS, SHARE_ROWS, HD), jnp.bfloat16),
        in_specs=[smem, vmem, vmem, vmem],
        out_specs=vmem,
        compiler_params=params(),
        cost_estimate=cost(2**20, 2**12, 2**20),
        name="window_join",
    )(info, got, own_mean, own_level)
    rows = lax.all_to_all(share, "ctx", 0, 0, axis_index_groups=same_core, tiled=True)
    shares, anchor = pl.pallas_call(
        project_kernel,
        out_shape=(
            shaped((8, SHARE, 2 * BLK), jnp.bfloat16),
            shaped((2, BLK, HD), jnp.bfloat16),
        ),
        in_specs=[vmem, vmem, vmem],
        out_specs=(vmem, vmem),
        compiler_params=params(),
        cost_estimate=cost(2**28, 0, 2**21),
        name="project",
    )(rows, out_weight, other_weight)
    summands = lax.all_to_all(shares, "tp", 0, 0, tiled=True)
    other_anchor = lax.ppermute(anchor, "ctx", core_swap)
    context_attn = pl.pallas_call(
        block_kernel,
        out_shape=shaped((2 * BLK, HEADS * HD), jnp.bfloat16),
        grid=(2,),
        in_specs=[
            smem,
            pl.BlockSpec((BLK, HEADS * HD), lambda step: (1 - step, 0)),
            pl.BlockSpec((2, BLK, HD), lambda step: (0, 1 - step, 0)),
            pl.BlockSpec((2, BLK, HD), lambda step: (0, 0, 0)),
            pl.BlockSpec((2, BLK, HD), lambda step: (0, 0, 0)),
            hbm,
        ],
        out_specs=pl.BlockSpec((BLK, HEADS * HD), lambda step: (1 - step, 0)),
        scratch_shapes=[
            pltpu.VMEM((HEADS, BLK, BLK), jnp.float32),
            pltpu.SemaphoreType.DMA,
        ],
        compiler_params=params(),
        cost_estimate=cost(2**30, 2**21, 2**22),
        name="block_attention",
    )(info, ctx_queries, ctx_keyvals, anchor, other_anchor, far(scores))
    summands, context_attn = lax.optimization_barrier((summands, context_attn))
    half_shape = shaped((SHARE, BLK), jnp.float32)
    mine, theirs = pl.pallas_call(
        total_kernel,
        out_shape=(half_shape, half_shape),
        in_specs=[vmem],
        out_specs=(vmem, vmem),
        compiler_params=params(),
        name="plane_sum",
    )(summands)
    theirs = lax.ppermute(theirs, "ctx", core_swap)
    even = lax.axis_index("ctx") % 2 == 0
    window_proj = jnp.concatenate(
        [jnp.where(even, mine, theirs), jnp.where(even, theirs, mine)], axis=0
    )
    return (context_attn, window_proj)


def solution(mesh):
    return jax.shard_map(
        on_device,
        mesh=mesh,
        in_specs=(
            P("ctx", "tp"),
            P(None, "ctx", "tp"),
            P(),
            P(),
            P(None, None, "tp"),
            P(None, None, None, "tp"),
            P("tp", "ctx"),
        ),
        out_specs=(P("ctx", "tp"), P("tp", "ctx")),
        check_vma=False,
    )
```

time: 68.2 us -> 65.2 us (0.956)
  starting transfers between devices: 14.3 us -> 22.1 us
  waiting for transfers between devices: 8.35 us -> 1.85 us
  blocking collectives: 32.4 us -> 28.4 us
    ppermute x1 -> x3, starting transfers between devices: 2.61 us -> 10.6 us  [the longest x1 5.44 us: on_device(): other_anchor = lax.ppermute(anchor, 'ctx', core_swap)]
    all_to_all x1, waiting for transfers between devices: 6.63 us -> 0.01 us  [on_device(): summands = lax.all_to_all(shares, 'tp', 0, 0, tiled=True)]
    all_to_all x1, blocking collectives: 17.7 us -> 15.1 us  [on_device(): lax.all_to_all(send, 'ctx', 0, 0, axis_index_groups=same_core, tiled=True)]
    all_to_all x1, blocking collectives: 14.7 us -> 13.3 us  [on_device(): lax.all_to_all(share, 'ctx', 0, 0, axis_index_groups=same_core, tiled=True)]
    pallas_call x3 -> x4, Pallas kernels: 5.9 us -> 5.6 us  [the longest x1 2.6 us: on_device(): pl.pallas_call(window_kernel, out_shape=(shaped((CHIPS, SEND_ROWS, HD), j...]
    ppermute x1 -> x3, waiting for transfers between devices: 1.72 us -> 1.85 us  [the longest x1 0.99 us: on_device(): other_anchor = lax.ppermute(anchor, 'ctx', core_swap)]
  transfers between devices with their start and end apart: 3 -> 5, of which waited for: 2 -> 2; matrix products, arithmetic and copies ran while one was open for 0% -> 0% of each run, Pallas kernels for 9% -> 14%
where the time goes in v4:
time: 65.2 us; the launch traced here: 64.9 us
  blocking collectives  28.4 us (44%)
  starting transfers between devices  22.1 us (34%)
  Pallas kernels  11.1 us (17%)
  waiting for transfers between devices  1.85 us (3%)
  between operations  0.73 us (1%)
    all_to_all x1, blocking collectives, on_device(): lax.all_to_all(send, 'ctx', 0, 0, axis_index_groups=same_core, tiled=True)  15.1 us
    all_to_all x1, blocking collectives, on_device(): lax.all_to_all(share, 'ctx', 0, 0, axis_index_groups=same_core, tiled=True)  13.3 us
    all_to_all x1, starting transfers between devices, on_device(): summands = lax.all_to_all(shares, 'tp', 0, 0, tiled=True)  8.18 us
    ppermute x1, starting transfers between devices, on_device(): other_anchor = lax.ppermute(anchor, 'ctx', core_swap)  5.44 us
    ppermute x1, starting transfers between devices, on_device(): theirs = lax.ppermute(theirs, 'ctx', core_swap)  5.04 us
    pallas_call x1, Pallas kernels, on_device(): pl.pallas_call(block_kernel, out_shape=shaped((2 * BLK, HEADS * HD), jnp....  4.52 us
    ppermute x1, starting transfers between devices, on_device(): other_keyvals = lax.ppermute(ctx_keyvals, 'ctx', core_swap)  3.33 us
    pallas_call x1, Pallas kernels, on_device(): pl.pallas_call(window_kernel, out_shape=(shaped((CHIPS, SEND_ROWS, HD), j...  2.6 us
  transfers between devices with their start and end apart: 5, of which 2 were waited for; matrix products, arithmetic and copies ran while one was open for 0% of the time, Pallas kernels for 14%

profile of v4, /device:TPU:1, one launch (start us, length us, event | category | flops | bytes accessed | tf_op | source)
XLA Modules:
  0.0 64.9 jit_solution(3919920810026730196)
XLA Ops:
  0.6 3.3 %collective-permute-start = (bf16[2,512,128]{2,1,0:T(8,128)(2,1)}, bf16[2,512,128]{2,1,0:T(8,128)(2,1)S(1)}, u32[]{:S(2)}, u32[]{:S(2)}) collective-permute-start(bf16[2,512,128]{2,1,0:T(8,128)(2,1)} %keyval_ref.1), channel_id=1, source_target_pairs={{0,8},{8,0},{16,24},{24,16},{32,40},{40,32},{48,56},{56,48},{64,72... | collective-permute-start | bytes 786440 | tf_op jit(solution)/shard_map/ppermute | solution.py:380
  4.0 1.8 %window_fetch.1 = (bf16[2,4,32,1024]{3,2,1,0:T(8,128)(2,1)S(1)}, bf16[2,512,128]{2,1,0:T(8,128)(2,1)S(1)}, f32[128,128]{1,0:T(8,128)S(1)}, f32[8,128]{1,0:T(8,128)S(1)}, s32[16]{0:T(128)S(1)}) custom-call(s32[64]{0:T(128)} %map_hbm.1, s32[2]{0:T(128)} %reach_hbm.1, bf16[2,4,2,32,1024]{4,3,2,1,0:T(8,128)(2,1)} %bitcast.1, bf16[2,512,128]{2,1,0:T(8,128)(2,1)} %keyval_ref.1, ...), custom_call_target="tpu_custom_call" | custom-call | flops 16777216 | bytes 2097152 | tf_op jit(solution)/shard_map/window_fetch/pallas_call | solution.py:382
  5.8 0.0 collective-permute-done.other_ref
  5.8 0.1 collective-permute-start.1
  5.9 2.6 %window_parts.1 = (bf16[16,176,128]{2,1,0:T(8,128)(2,1)S(1)}, f32[8,256,256]{2,1,0:T(8,128)}) custom-call(s32[16]{0:T(128)S(1)} %get-tuple-element.20.info_ref, bf16[2,4,32,1024]{3,2,1,0:T(8,128)(2,1)S(1)} %get-tuple-element.22.query_ref, bf16[2,512,128]{2,1,0:T(8,128)(2,1)S(1)} %get-tuple-element.23.own_ref, ...), custom_call_target="tpu_custom_call" | custom-call | flops 536870912 | bytes 2097152 | tf_op jit(solution)/shard_map/window_parts/pallas_call | solution.py:409
  8.5 0.0 collective-permute-done.1.other_ref
  8.5 0.0 copy-start.2
  8.5 15.1 %all_to_all.15.got_ref = bf16[16,176,128]{2,1,0:T(8,128)(2,1)S(1)} all-to-all(bf16[16,176,128]{2,1,0:T(8,128)(2,1)S(1)} %get-tuple-element.27), channel_id=1, replica_groups={{0,16,32,48,64,80,96,112,128,144,160,176,192,208,224,240},{8,24,40,56,7..., dimensions={0} | all-to-all | bytes 1441792 | tf_op jit(solution)/shard_map/all_to_all | solution.py:427
  23.6 1.0 %window_join.1 = bf16[16,160,128]{2,1,0:T(8,128)(2,1)S(1)} custom-call(s32[16]{0:T(128)S(1)} %get-tuple-element.20.info_ref, bf16[16,176,128]{2,1,0:T(8,128)(2,1)S(1)} %all_to_all.15.got_ref, f32[128,128]{1,0:T(8,128)S(1)} %get-tuple-element.28.mean_ref, f32[8,128]{1,0:T(8,128)S(1)} %get-tuple-element.29.level_ref), custom_call_target="tpu_custom_call" | custom-call | flops 1048576 | bytes 1048576 | tf_op jit(solution)/shard_map/window_join/pallas_call | solution.py:428
  24.6 0.0 copy-start
  24.6 0.0 copy-start.1
  24.6 13.3 %all_to_all.16.rows_ref = bf16[16,160,128]{2,1,0:T(8,128)(2,1)S(1)} all-to-all(bf16[16,160,128]{2,1,0:T(8,128)(2,1)S(1)} %window_join.1), channel_id=1, replica_groups={{0,16,32,48,64,80,96,112,128,144,160,176,192,208,224,240},{8,24,40,56,7..., dimensions={0} | all-to-all | bytes 1310720 | tf_op jit(solution)/shard_map/all_to_all | solution.py:437
  37.9 0.0 copy-done.2
  37.9 1.2 %project.1 = (bf16[8,32,512]{2,1,0:T(8,128)(2,1)}, bf16[2,256,128]{2,1,0:T(8,128)(2,1)S(1)}) custom-call(bf16[16,160,128]{2,1,0:T(8,128)(2,1)S(1)} %all_to_all.16.rows_ref, bf16[1024,256]{1,0:T(8,128)(2,1)S(1)} %copy-done.2, bf16[1024,256]{1,0:T(8,128)(2,1)S(1)} %collective-permute-done.1.other_ref), custom_call_target="tpu_custom_call" | custom-call | flops 268435456 | bytes 2097152 | tf_op jit(solution)/shard_map/project/pallas_call | solution.py:438
  39.1 8.2 %all-to-all-start.2 = ((bf16[8,32,512]{2,1,0:T(8,128)(2,1)}), bf16[8,32,512]{2,1,0:T(8,128)(2,1)S(1)}, u32[]{:S(2)}, u32[]{:S(2)}) async-start(bf16[8,32,512]{2,1,0:T(8,128)(2,1)} %get-tuple-element.31), calls=%async_computation.2 | async-start | bytes 524288 | tf_op jit(solution)/shard_map/all_to_all | solution.py:450
  47.3 5.4 %collective-permute-start.2 = (bf16[2,256,128]{2,1,0:T(8,128)(2,1)S(1)}, bf16[2,256,128]{2,1,0:T(8,128)(2,1)S(1)}, u32[]{:S(2)}, u32[]{:S(2)}) collective-permute-start(bf16[2,256,128]{2,1,0:T(8,128)(2,1)S(1)} %get-tuple-element.32.own_ref), channel_id=1, source_target_pairs={{0,8},{8,0},{16,24},{24,16},{32,40},{40,32},{48,56},{56,48},{64,72... | collective-permute-start | bytes 393224 | tf_op jit(solution)/shard_map/ppermute | solution.py:451
  52.7 1.0 %collective-permute-done.2.other_ref = bf16[2,256,128]{2,1,0:T(8,128)(2,1)S(1)} collective-permute-done((bf16[2,256,128]{2,1,0:T(8,128)(2,1)S(1)}, bf16[2,256,128]{2,1,0:T(8,128)(2,1)S(1)}, u32[]{:S(2)}, u32[]{:S(2)}) %collective-permute-start.2) | collective-permute-done | bytes 131104 | tf_op jit(solution)/shard_map/ppermute | solution.py:451
  53.7 0.0 copy-done
  53.7 0.0 copy-done.1
  53.7 4.5 %block_attention.1 = bf16[512,1024]{1,0:T(8,128)(2,1)} custom-call(s32[16]{0:T(128)S(1)} %get-tuple-element.20.info_ref, bf16[512,1024]{1,0:T(8,128)(2,1)S(1)} %copy-done, bf16[2,512,128]{2,1,0:T(8,128)(2,1)S(1)} %copy-done.1, bf16[2,256,128]{2,1,0:T(8,128)(2,1)S(1)} %get-tuple-element.32.own_ref, bf16[2,256,128]{2,1,0:T(8,128)(2,1)S(1)} %collective-permute-done.2.other_ref, ...), custom_call_target="tpu_custom_call" | custom-call | flops 1073741824 | bytes 4194304 | tf_op jit(solution)/shard_map/block_attention/pallas_call | solution.py:452
  58.3 0.0 all-to-all-done.2.parts_ref
  58.3 5.0 %collective-permute-start.3 = (f32[32,256]{1,0:T(8,128)S(1)}, f32[32,256]{1,0:T(8,128)S(1)}, u32[]{:S(2)}, u32[]{:S(2)}) collective-permute-start(f32[32,256]{1,0:T(8,128)S(1)} %get-tuple-element.37), channel_id=1, source_target_pairs={{0,8},{8,0},{16,24},{24,16},{32,40},{40,32},{48,56},{56,48},{64,72... | collective-permute-start | bytes 98312 | tf_op jit(solution)/shard_map/ppermute | solution.py:483
  63.4 0.9 %collective-permute-done.3 = f32[32,256]{1,0:T(8,128)S(1)} collective-permute-done((f32[32,256]{1,0:T(8,128)S(1)}, f32[32,256]{1,0:T(8,128)S(1)}, u32[]{:S(2)}, u32[]{:S(2)}) %collective-permute-start.3) | collective-permute-done | bytes 32800 | tf_op jit(solution)/shard_map/ppermute | solution.py:483
  64.2 0.6 pad_maximum_fusion
  (2 shorter events, 0.1 us)
Async XLA Ops:
  0.6 5.1 %collective-permute-start = (bf16[2,512,128]{2,1,0:T(8,128)(2,1)}, bf16[2,512,128]{2,1,0:T(8,128)(2,1)S(1)}, u32[]{:S(2)}, u32[]{:S(2)}) collective-permute-start(bf16[2,512,128]{2,1,0:T(8,128)(2,1)} %keyval_ref.1), channel_id=1, source_target_pairs={{0,8},{8,0},{16,24},{24,16},{32,40},{40,32},{48,56},{56,48},{64,72... | collective-permute-start | bytes 786440 | tf_op jit(solution)/shard_map/ppermute | solution.py:380
  5.8 2.7 %collective-permute-start.1 = (bf16[1024,256]{1,0:T(8,128)(2,1)}, bf16[1024,256]{1,0:T(8,128)(2,1)S(1)}, u32[]{:S(2)}, u32[]{:S(2)}) collective-permute-start(bf16[1024,256]{1,0:T(8,128)(2,1)} %own_ref), channel_id=1, source_target_pairs={{0,8},{8,0},{16,24},{24,16},{32,40},{40,32},{48,56},{56,48},{64,72... | collective-permute-start | bytes 1572872 | tf_op jit(solution)/shard_map/ppermute | solution.py:408
  8.5 29.4 %copy-start.2 = (bf16[1024,256]{1,0:T(8,128)(2,1)S(1)}, bf16[1024,256]{1,0:T(8,128)(2,1)}, u32[]{:S(2)}) copy-start(bf16[1024,256]{1,0:T(8,128)(2,1)} %own_ref) | copy-start | bytes 1572868
  24.6 29.1 %copy-start = (bf16[512,1024]{1,0:T(8,128)(2,1)S(1)}, bf16[512,1024]{1,0:T(8,128)(2,1)}, u32[]{:S(2)}) copy-start(bf16[512,1024]{1,0:T(8,128)(2,1)} %query_ref.1) | copy-start | bytes 3145732
  24.6 29.1 %copy-start.1 = (bf16[2,512,128]{2,1,0:T(8,128)(2,1)S(1)}, bf16[2,512,128]{2,1,0:T(8,128)(2,1)}, u32[]{:S(2)}) copy-start(bf16[2,512,128]{2,1,0:T(8,128)(2,1)} %keyval_ref.1) | copy-start | bytes 786436
  39.1 19.1 %all-to-all-start.2 = ((bf16[8,32,512]{2,1,0:T(8,128)(2,1)}), bf16[8,32,512]{2,1,0:T(8,128)(2,1)S(1)}, u32[]{:S(2)}, u32[]{:S(2)}) async-start(bf16[8,32,512]{2,1,0:T(8,128)(2,1)} %get-tuple-element.31), calls=%async_computation.2 | async-start | bytes 524288 | tf_op jit(solution)/shard_map/all_to_all | solution.py:450
  47.3 6.4 %collective-permute-start.2 = (bf16[2,256,128]{2,1,0:T(8,128)(2,1)S(1)}, bf16[2,256,128]{2,1,0:T(8,128)(2,1)S(1)}, u32[]{:S(2)}, u32[]{:S(2)}) collective-permute-start(bf16[2,256,128]{2,1,0:T(8,128)(2,1)S(1)} %get-tuple-element.32.own_ref), channel_id=1, source_target_pairs={{0,8},{8,0},{16,24},{24,16},{32,40},{40,32},{48,56},{56,48},{64,72... | collective-permute-start | bytes 393224 | tf_op jit(solution)/shard_map/ppermute | solution.py:451
  58.3 5.9 %collective-permute-start.3 = (f32[32,256]{1,0:T(8,128)S(1)}, f32[32,256]{1,0:T(8,128)S(1)}, u32[]{:S(2)}, u32[]{:S(2)}) collective-permute-start(f32[32,256]{1,0:T(8,128)S(1)} %get-tuple-element.37), channel_id=1, source_target_pairs={{0,8},{8,0},{16,24},{24,16},{32,40},{40,32},{48,56},{56,48},{64,72... | collective-permute-start | bytes 98312 | tf_op jit(solution)/shard_map/ppermute | solution.py:483

commit v5 on v4

--- a/solution.py
+++ b/solution.py
@@ -27,7 +27,6 @@
 same_core = [[chip * 2 + core for chip in range(CHIPS)] for core in range(2)]
 core_swap = [(device, device ^ 1) for device in range(2 * CHIPS)]
 
-smem = pl.BlockSpec(memory_space=pltpu.SMEM)
 vmem = pl.BlockSpec(memory_space=pltpu.VMEM)
 hbm = pl.BlockSpec(memory_space=pltpu.HBM)
 
@@ -71,6 +70,27 @@
             ready.append(dot_nt(query_ref[:, head * HD : (head + 1) * HD], keys))
         if head >= AHEAD:
             yield head - AHEAD, ready.pop(0)
+
+
+def read(info_ref, number):
+    return jnp.max(info_ref[number : number + 1, :]).astype(jnp.int32)
+
+
+def own_window(query_ref, window_ref):
+    position = lax.axis_index("ctx")
+    core = position % 2
+    chip = position // 2
+    lanes = pl.ds(pl.multiple_of(chip // 2 * HD, HD), HD)
+    query = query_ref[chip % 2, :, :, lanes].reshape(HALF, HD)
+    raw = dot_nt(query, window_ref[0])
+    key = lax.broadcasted_iota(jnp.int32, raw.shape, 1)
+    row = lax.broadcasted_iota(jnp.int32, raw.shape, 0)
+    row = row // SHARE * (2 * SHARE) + core * SHARE + row % SHARE
+    raw = jnp.where(key <= row, raw, masked_score)
+    top, total, weights = row_softmax(raw)
+    mean = weigh(weights, window_ref[1]) / total
+    level = jnp.broadcast_to(top * SCALE + jnp.log(total), (HALF, HALF)).T
+    return mean, level[:8]
 
 
 def fetch_kernel(
@@ -81,10 +101,8 @@
     window_hbm,
     query_ref,
     keyval_ref,
-    mean_ref,
-    level_ref,
+    window_ref,
     info_ref,
-    window_ref,
     map_ref,
     reach_ref,
     done,
@@ -99,8 +117,8 @@
                 (map_hbm, map_ref),
                 (reach_hbm, reach_ref),
                 (query_hbm.at[:, :, core], query_ref),
+                (keyval_hbm, keyval_ref),
                 (window_hbm.at[chip % 2], window_ref),
-                (keyval_hbm, keyval_ref),
             )
         )
     ]
@@ -109,34 +127,26 @@
     for copy in copies[:2]:
         copy.wait()
     partner = position + 1 - 2 * core
+
+    def put(number, value):
+        info_ref[number : number + 1, :] = jnp.full((1, HD), value.astype(jnp.float32))
+
     holder = jnp.int32(0)
     for number in range(2 * NB):
         holder = jnp.where(map_ref[number] == core * NB, number // 4, holder)
-    info_ref[0] = holder
+    put(0, holder)
     for part, device in enumerate((position, partner)):
-        info_ref[1 + part] = jnp.where(map_ref[2 * device] // NB == 0, 0, 1)
+        put(1 + part, map_ref[2 * device] // NB)
         for context in range(2):
             slot = jnp.where(map_ref[2 * device] // NB == context, 0, 1)
             place = map_ref[2 * device + slot] - NB * context
-            info_ref[3 + 2 * context + part] = jnp.where(place < reach_ref[context], 1, 0)
+            put(3 + 2 * context + part, jnp.where(place < reach_ref[context], 1, 0))
     slot = jnp.where(map_ref[2 * position] // NB == core, 0, 1)
-    info_ref[7] = map_ref[2 * position + slot] - NB * core
-    info_ref[8] = core
-    info_ref[9] = map_ref[2 * position]
-    info_ref[10] = map_ref[2 * position + 1]
+    put(7, map_ref[2 * position + slot] - NB * core)
+    put(8, map_ref[2 * position])
+    put(9, map_ref[2 * position + 1])
     for copy in copies[2:]:
         copy.wait()
-    lanes = pl.ds(pl.multiple_of(chip // 2 * HD, HD), HD)
-    query = query_ref[chip % 2, :, :, lanes].reshape(HALF, HD)
-    raw = dot_nt(query, window_ref[0])
-    key = lax.broadcasted_iota(jnp.int32, raw.shape, 1)
-    row = lax.broadcasted_iota(jnp.int32, raw.shape, 0)
-    row = row // SHARE * (2 * SHARE) + core * SHARE + row % SHARE
-    raw = jnp.where(key <= row, raw, masked_score)
-    top, total, weights = row_softmax(raw)
-    mean_ref[...] = weigh(weights, window_ref[1]) / total
-    level = jnp.broadcast_to(top * SCALE + jnp.log(total), (HALF, HALF)).T
-    level_ref[...] = level[:8]
 
 
 def window_kernel(
@@ -144,22 +154,27 @@
     query_ref,
     own_ref,
     other_ref,
+    window_ref,
     rows_hbm,
     send_ref,
+    mean_ref,
+    level_ref,
     score_hbm,
     score_ref,
     rows_ref,
     done,
 ):
+    core = lax.axis_index("ctx") % 2
     copy = pltpu.make_async_copy(rows_hbm.at[:BLK], rows_ref, done.at[0])
 
-    @pl.when(info_ref[8] == 0)
+    @pl.when(core == 0)
     def _():
         copy.start()
 
+    slots = [read(info_ref, 1 + part) for part in range(2)]
+
     def block_rows(part, context):
-        slot = info_ref[1 + part]
-        slot = slot if context == 0 else 1 - slot
+        slot = slots[part] if context == 0 else 1 - slots[part]
         return pl.ds(pl.multiple_of(slot * BLK, BLK), BLK)
 
     sources = (own_ref, other_ref)
@@ -177,8 +192,8 @@
         values.append([ref[1, taken, :] for ref, taken in zip(sources, rows)])
         biases.append(
             [
-                jnp.where(info_ref[3 + 2 * context + part] == 1, 0.0, masked_score)
-                for part in range(2)
+                jnp.where(read(info_ref, number) == 1, 0.0, masked_score)
+                for number in (3 + 2 * context, 4 + 2 * context)
             ]
         )
 
@@ -228,17 +243,17 @@
             target = 2 * (2 * pair + half) + context
             lanes = slice(half * HALF, (half + 1) * HALF)
             send_ref[target, HALF : HALF + STAT, :] = stats[:, lanes]
-    first = info_ref[7] == 0
+    first = read(info_ref, 7) == 0
     own_rows, other_rows = [
-        pl.ds(pl.multiple_of((info_ref[1 + part] ^ info_ref[8]) * BLK, BLK), BLK)
-        for part in range(2)
+        pl.ds(pl.multiple_of((slots[part] ^ core) * BLK, BLK), BLK) for part in range(2)
     ]
     for member in range(2):
         block = jnp.where(first, own_ref[member, own_rows, :], other_ref[member, other_rows, :])
         send_ref[8 * member : 8 * member + 8, HALF + STAT :, :] = block.reshape(8, PIECE, HD)
 
-    @pl.when(info_ref[8] == 0)
-    def _():
+    @pl.when(core == 0)
+    def _():
+        mean_ref[...], level_ref[...] = own_window(query_ref, window_ref)
         copy.wait()
         for head in range(HEADS):
             query = rows_ref[:, head * HD : (head + 1) * HD]
@@ -248,7 +263,20 @@
         copy_out.wait()
 
 
-def combine_kernel(info_ref, got_ref, mean_ref, level_ref, share_ref):
+def combine_kernel(
+    info_ref, got_ref, mean_in, level_in, query_ref, window_ref, share_ref, mean_ref, level_ref
+):
+    core = lax.axis_index("ctx") % 2
+
+    @pl.when(core == 0)
+    def _():
+        mean_ref[...] = mean_in[...]
+        level_ref[...] = level_in[...]
+
+    @pl.when(core == 1)
+    def _():
+        mean_ref[...], level_ref[...] = own_window(query_ref, window_ref)
+
     levels = []
     for source in range(CHIPS):
         stats = got_ref[source, HALF : HALF + STAT, :].astype(jnp.float32)
@@ -272,7 +300,7 @@
         part = got_ref[source, :HALF, :].astype(jnp.float32)
         joined = joined + part * wide[:, source * HALF : (source + 1) * HALF]
     result = joined.astype(jnp.bfloat16)
-    piece = got_ref[info_ref[0], HALF + STAT :, :]
+    piece = got_ref[read(info_ref, 0), HALF + STAT :, :]
     for target in range(CHIPS):
         share_ref[target, :HALF, :] = result
         share_ref[target, HALF:, :] = piece
@@ -328,16 +356,17 @@
     info_ref, query_ref, keyval_ref, own_ref, other_ref, score_hbm, out_ref, score_ref, done
 ):
     step = pl.program_id(0)
-    scored = (step == 1) & (info_ref[8] == 0)
-    block = info_ref[10 - step]
+    core = lax.axis_index("ctx") % 2
+    scored = (step == 1) & (core == 0)
+    block = jnp.where(step == 0, read(info_ref, 9), read(info_ref, 8))
+    mine = block // NB == core
+    bias = jnp.where(block % NB != 0, 0.0, masked_score)
     copy = pltpu.make_async_copy(score_hbm, score_ref, done)
 
-    @pl.when((step == 0) & (info_ref[8] == 0))
+    @pl.when((step == 0) & (core == 0))
     def _():
         copy.start()
 
-    mine = block // NB == info_ref[8]
-    bias = jnp.where(block % NB != 0, 0.0, masked_score)
 
     def anchor(member):
         return jnp.where(mine, own_ref[member], other_ref[member])
@@ -379,19 +408,17 @@
 ):
     other_keyvals = lax.ppermute(ctx_keyvals, "ctx", core_swap)
     halves = win_queries.reshape(2, 4, 2, SHARE, HEADS * HD)
-    queries, keyvals, own_mean, own_level, info = pl.pallas_call(
+    queries, keyvals, window, info = pl.pallas_call(
         fetch_kernel,
         out_shape=(
             shaped((2, 4, SHARE, HEADS * HD), jnp.bfloat16),
             shaped((2, 2 * BLK, HD), jnp.bfloat16),
-            shaped((HALF, HD), jnp.float32),
-            shaped((8, HALF), jnp.float32),
-            shaped((16,), jnp.int32),
+            shaped((2, BLK, HD), jnp.bfloat16),
+            shaped((16, HD), jnp.float32),
         ),
         in_specs=[hbm] * 5,
-        out_specs=(vmem,) * 4 + (smem,),
+        out_specs=(vmem,) * 4,
         scratch_shapes=[
-            pltpu.VMEM((2, BLK, HD), jnp.bfloat16),
             pltpu.SMEM((2 * NB,), jnp.int32),
             pltpu.SMEM((2,), jnp.int32),
             pltpu.SemaphoreType.DMA((5,)),
@@ -406,14 +433,16 @@
         (queries, other_keyvals, out_weight)
     )
     other_weight = lax.ppermute(out_weight, "ctx", core_swap)
-    send, scores = pl.pallas_call(
+    send, own_mean, own_level, scores = pl.pallas_call(
         window_kernel,
         out_shape=(
             shaped((CHIPS, SEND_ROWS, HD), jnp.bfloat16),
+            shaped((HALF, HD), jnp.float32),
+            shaped((8, HALF), jnp.float32),
             pltpu.HBM((HEADS, BLK, BLK), jnp.float32),
         ),
-        in_specs=[smem] + [vmem] * 3 + [hbm],
-        out_specs=(vmem, hbm),
+        in_specs=[vmem] * 5 + [hbm],
+        out_specs=(vmem, vmem, vmem, hbm),
         scratch_shapes=[
             pltpu.VMEM((HEADS, BLK, BLK), jnp.float32),
             pltpu.VMEM((BLK, HEADS * HD), jnp.bfloat16),
@@ -422,18 +451,22 @@
         compiler_params=params(),
         cost_estimate=cost(2**29, 2**20, 2**21),
         name="window_parts",
-    )(info, queries, keyvals, other_keyvals, far(ctx_queries))
+    )(info, queries, keyvals, other_keyvals, window, far(ctx_queries))
     send, other_weight = lax.optimization_barrier((send, other_weight))
     got = lax.all_to_all(send, "ctx", 0, 0, axis_index_groups=same_core, tiled=True)
     share = pl.pallas_call(
         combine_kernel,
         out_shape=shaped((CHIPS, SHARE_ROWS, HD), jnp.bfloat16),
-        in_specs=[smem, vmem, vmem, vmem],
+        in_specs=[vmem] * 6,
         out_specs=vmem,
+        scratch_shapes=[
+            pltpu.VMEM((HALF, HD), jnp.float32),
+            pltpu.VMEM((8, HALF), jnp.float32),
+        ],
         compiler_params=params(),
         cost_estimate=cost(2**20, 2**12, 2**20),
         name="window_join",
-    )(info, got, own_mean, own_level)
+    )(info, got, own_mean, own_level, queries, window)
     rows = lax.all_to_all(share, "ctx", 0, 0, axis_index_groups=same_core, tiled=True)
     shares, anchor = pl.pallas_call(
         project_kernel,
@@ -454,7 +487,7 @@
         out_shape=shaped((2 * BLK, HEADS * HD), jnp.bfloat16),
         grid=(2,),
         in_specs=[
-            smem,
+            vmem,
             pl.BlockSpec((BLK, HEADS * HD), lambda step: (1 - step, 0)),
             pl.BlockSpec((2, BLK, HD), lambda step: (0, 1 - step, 0)),
             pl.BlockSpec((2, BLK, HD), lambda step: (0, 0, 0)),

time: 65.2 us -> 64.1 us (0.983)
  Pallas kernels: 11.1 us -> 9.69 us
  transfers between devices with their start and end apart: 5 -> 5, of which waited for: 2 -> 3; matrix products, arithmetic and copies ran while one was open for 0% -> 0% of each run, Pallas kernels for 14% -> 12%
where the time goes in v5:
time: 64.1 us; the launch traced here: 63.8 us
  blocking collectives  28.4 us (44%)
  starting transfers between devices  22.3 us (35%)
  Pallas kernels  9.69 us (15%)
  waiting for transfers between devices  2.03 us (3%)
  between operations  0.71 us (1%)
    all_to_all x1, blocking collectives, on_device(): lax.all_to_all(send, 'ctx', 0, 0, axis_index_groups=same_core, tiled=True)  15 us
    all_to_all x1, blocking collectives, on_device(): lax.all_to_all(share, 'ctx', 0, 0, axis_index_groups=same_core, tiled=True)  13.3 us
    all_to_all x1, starting transfers between devices, on_device(): summands = lax.all_to_all(shares, 'tp', 0, 0, tiled=True)  8.19 us
    ppermute x1, starting transfers between devices, on_device(): theirs = lax.ppermute(theirs, 'ctx', core_swap)  5.35 us
    ppermute x1, starting transfers between devices, on_device(): other_anchor = lax.ppermute(anchor, 'ctx', core_swap)  5.08 us
    pallas_call x1, Pallas kernels, on_device(): pl.pallas_call(block_kernel, out_shape=shaped((2 * BLK, HEADS * HD), jnp....  4.2 us
    ppermute x1, starting transfers between devices, on_device(): other_keyvals = lax.ppermute(ctx_keyvals, 'ctx', core_swap)  3.33 us
    pallas_call x1, Pallas kernels, on_device(): pl.pallas_call(window_kernel, out_shape=(shaped((CHIPS, SEND_ROWS, HD), j...  2.19 us
  transfers between devices with their start and end apart: 5, of which 3 were waited for; matrix products, arithmetic and copies ran while one was open for 0% of the time, Pallas kernels for 12%

profile of v5, /device:TPU:1, one launch (start us, length us, event | category | flops | bytes accessed | tf_op | source)
XLA Modules:
  0.0 63.8 jit_solution(6698462484885668465)
XLA Ops:
  0.6 3.3 %collective-permute-start = (bf16[2,512,128]{2,1,0:T(8,128)(2,1)}, bf16[2,512,128]{2,1,0:T(8,128)(2,1)S(1)}, u32[]{:S(2)}, u32[]{:S(2)}) collective-permute-start(bf16[2,512,128]{2,1,0:T(8,128)(2,1)} %keyval_ref.1), channel_id=1, source_target_pairs={{0,8},{8,0},{16,24},{24,16},{32,40},{40,32},{48,56},{56,48},{64,72... | collective-permute-start | bytes 786440 | tf_op jit(solution)/shard_map/ppermute | solution.py:409
  4.0 1.2 %window_fetch.1 = (bf16[2,4,32,1024]{3,2,1,0:T(8,128)(2,1)S(1)}, bf16[2,512,128]{2,1,0:T(8,128)(2,1)S(1)}, bf16[2,256,128]{2,1,0:T(8,128)(2,1)S(1)}, f32[16,128]{1,0:T(8,128)S(1)}) custom-call(s32[64]{0:T(128)} %map_hbm.1, s32[2]{0:T(128)} %reach_hbm.1, bf16[2,4,2,32,1024]{4,3,2,1,0:T(8,128)(2,1)} %bitcast.1, bf16[2,512,128]{2,1,0:T(8,128)(2,1)} %keyval_ref.1, ...), custom_call_target="tpu_custom_call" | custom-call | flops 16777216 | bytes 2097152 | tf_op jit(solution)/shard_map/window_fetch/pallas_call | solution.py:411
  5.2 0.2 collective-permute-done.other_ref
  5.3 0.4 collective-permute-start.1
  5.7 2.2 %window_parts.1 = (bf16[16,176,128]{2,1,0:T(8,128)(2,1)S(1)}, f32[128,128]{1,0:T(8,128)S(1)}, f32[8,128]{1,0:T(8,128)S(1)}, f32[8,256,256]{2,1,0:T(8,128)}) custom-call(f32[16,128]{1,0:T(8,128)S(1)} %get-tuple-element.21.info_ref, bf16[2,4,32,1024]{3,2,1,0:T(8,128)(2,1)S(1)} %get-tuple-element.23.query_ref, ...), custom_call_target="tpu_custom_call" | custom-call | flops 536870912 | bytes 2097152 | tf_op jit(solution)/shard_map/window_parts/pallas_call | solution.py:436
  7.9 0.0 collective-permute-done.1.other_ref
  7.9 0.0 copy-start.2
  7.9 15.0 %all_to_all.15.got_ref = bf16[16,176,128]{2,1,0:T(8,128)(2,1)S(1)} all-to-all(bf16[16,176,128]{2,1,0:T(8,128)(2,1)S(1)} %get-tuple-element.29), channel_id=1, replica_groups={{0,16,32,48,64,80,96,112,128,144,160,176,192,208,224,240},{8,24,40,56,7..., dimensions={0} | all-to-all | bytes 1441792 | tf_op jit(solution)/shard_map/all_to_all | solution.py:456
  23.0 0.9 %window_join.1 = bf16[16,160,128]{2,1,0:T(8,128)(2,1)S(1)} custom-call(f32[16,128]{1,0:T(8,128)S(1)} %get-tuple-element.21.info_ref, bf16[16,176,128]{2,1,0:T(8,128)(2,1)S(1)} %all_to_all.15.got_ref, f32[128,128]{1,0:T(8,128)S(1)} %get-tuple-element.30.mean_in, f32[8,128]{1,0:T(8,128)S(1)} %get-tuple-element.31.level_in, ...), custom_call_target="tpu_custom_call" | custom-call | flops 1048576 | bytes 1048576 | tf_op jit(solution)/shard_map/window_join/pallas_call | solution.py:457
  23.9 0.0 copy-start
  23.9 0.0 copy-start.1
  23.9 13.3 %all_to_all.16.rows_ref = bf16[16,160,128]{2,1,0:T(8,128)(2,1)S(1)} all-to-all(bf16[16,160,128]{2,1,0:T(8,128)(2,1)S(1)} %window_join.1), channel_id=1, replica_groups={{0,16,32,48,64,80,96,112,128,144,160,176,192,208,224,240},{8,24,40,56,7..., dimensions={0} | all-to-all | bytes 1310720 | tf_op jit(solution)/shard_map/all_to_all | solution.py:470
  37.2 0.0 copy-done.2
  37.2 1.2 %project.1 = (bf16[8,32,512]{2,1,0:T(8,128)(2,1)}, bf16[2,256,128]{2,1,0:T(8,128)(2,1)S(1)}) custom-call(bf16[16,160,128]{2,1,0:T(8,128)(2,1)S(1)} %all_to_all.16.rows_ref, bf16[1024,256]{1,0:T(8,128)(2,1)S(1)} %copy-done.2, bf16[1024,256]{1,0:T(8,128)(2,1)S(1)} %collective-permute-done.1.other_ref), custom_call_target="tpu_custom_call" | custom-call | flops 268435456 | bytes 2097152 | tf_op jit(solution)/shard_map/project/pallas_call | solution.py:471
  38.4 8.2 %all-to-all-start.2 = ((bf16[8,32,512]{2,1,0:T(8,128)(2,1)}), bf16[8,32,512]{2,1,0:T(8,128)(2,1)S(1)}, u32[]{:S(2)}, u32[]{:S(2)}) async-start(bf16[8,32,512]{2,1,0:T(8,128)(2,1)} %get-tuple-element.33), calls=%async_computation.2 | async-start | bytes 524288 | tf_op jit(solution)/shard_map/all_to_all | solution.py:483
  46.6 5.1 %collective-permute-start.2 = (bf16[2,256,128]{2,1,0:T(8,128)(2,1)S(1)}, bf16[2,256,128]{2,1,0:T(8,128)(2,1)S(1)}, u32[]{:S(2)}, u32[]{:S(2)}) collective-permute-start(bf16[2,256,128]{2,1,0:T(8,128)(2,1)S(1)} %get-tuple-element.34.own_ref), channel_id=1, source_target_pairs={{0,8},{8,0},{16,24},{24,16},{32,40},{40,32},{48,56},{56,48},{64,72... | collective-permute-start | bytes 393224 | tf_op jit(solution)/shard_map/ppermute | solution.py:484
  51.6 1.0 %collective-permute-done.2.other_ref = bf16[2,256,128]{2,1,0:T(8,128)(2,1)S(1)} collective-permute-done((bf16[2,256,128]{2,1,0:T(8,128)(2,1)S(1)}, bf16[2,256,128]{2,1,0:T(8,128)(2,1)S(1)}, u32[]{:S(2)}, u32[]{:S(2)}) %collective-permute-start.2) | collective-permute-done | bytes 131104 | tf_op jit(solution)/shard_map/ppermute | solution.py:484
  52.6 0.0 copy-done
  52.6 0.0 copy-done.1
  52.6 4.2 %block_attention.1 = bf16[512,1024]{1,0:T(8,128)(2,1)} custom-call(f32[16,128]{1,0:T(8,128)S(1)} %get-tuple-element.21.info_ref, bf16[512,1024]{1,0:T(8,128)(2,1)S(1)} %copy-done, bf16[2,512,128]{2,1,0:T(8,128)(2,1)S(1)} %copy-done.1, bf16[2,256,128]{2,1,0:T(8,128)(2,1)S(1)} %get-tuple-element.34.own_ref, ...), custom_call_target="tpu_custom_call" | custom-call | flops 1073741824 | bytes 4194304 | tf_op jit(solution)/shard_map/block_attention/pallas_call | solution.py:485
  56.8 0.0 all-to-all-done.2.parts_ref
  56.9 5.3 %collective-permute-start.3 = (f32[32,256]{1,0:T(8,128)S(1)}, f32[32,256]{1,0:T(8,128)S(1)}, u32[]{:S(2)}, u32[]{:S(2)}) collective-permute-start(f32[32,256]{1,0:T(8,128)S(1)} %get-tuple-element.39), channel_id=1, source_target_pairs={{0,8},{8,0},{16,24},{24,16},{32,40},{40,32},{48,56},{56,48},{64,72... | collective-permute-start | bytes 98312 | tf_op jit(solution)/shard_map/ppermute | solution.py:516
  62.3 0.9 %collective-permute-done.3 = f32[32,256]{1,0:T(8,128)S(1)} collective-permute-done((f32[32,256]{1,0:T(8,128)S(1)}, f32[32,256]{1,0:T(8,128)S(1)}, u32[]{:S(2)}, u32[]{:S(2)}) %collective-permute-start.3) | collective-permute-done | bytes 32800 | tf_op jit(solution)/shard_map/ppermute | solution.py:516
  63.1 0.6 pad_maximum_fusion
  (2 shorter events, 0.1 us)
Async XLA Ops:
  0.6 4.7 %collective-permute-start = (bf16[2,512,128]{2,1,0:T(8,128)(2,1)}, bf16[2,512,128]{2,1,0:T(8,128)(2,1)S(1)}, u32[]{:S(2)}, u32[]{:S(2)}) collective-permute-start(bf16[2,512,128]{2,1,0:T(8,128)(2,1)} %keyval_ref.1), channel_id=1, source_target_pairs={{0,8},{8,0},{16,24},{24,16},{32,40},{40,32},{48,56},{56,48},{64,72... | collective-permute-start | bytes 786440 | tf_op jit(solution)/shard_map/ppermute | solution.py:409
  5.3 2.6 %collective-permute-start.1 = (bf16[1024,256]{1,0:T(8,128)(2,1)}, bf16[1024,256]{1,0:T(8,128)(2,1)S(1)}, u32[]{:S(2)}, u32[]{:S(2)}) collective-permute-start(bf16[1024,256]{1,0:T(8,128)(2,1)} %own_ref), channel_id=1, source_target_pairs={{0,8},{8,0},{16,24},{24,16},{32,40},{40,32},{48,56},{56,48},{64,72... | collective-permute-start | bytes 1572872 | tf_op jit(solution)/shard_map/ppermute | solution.py:435
  7.9 29.3 %copy-start.2 = (bf16[1024,256]{1,0:T(8,128)(2,1)S(1)}, bf16[1024,256]{1,0:T(8,128)(2,1)}, u32[]{:S(2)}) copy-start(bf16[1024,256]{1,0:T(8,128)(2,1)} %own_ref) | copy-start | bytes 1572868
  23.9 28.8 %copy-start = (bf16[512,1024]{1,0:T(8,128)(2,1)S(1)}, bf16[512,1024]{1,0:T(8,128)(2,1)}, u32[]{:S(2)}) copy-start(bf16[512,1024]{1,0:T(8,128)(2,1)} %query_ref.1) | copy-start | bytes 3145732
  23.9 28.8 %copy-start.1 = (bf16[2,512,128]{2,1,0:T(8,128)(2,1)S(1)}, bf16[2,512,128]{2,1,0:T(8,128)(2,1)}, u32[]{:S(2)}) copy-start(bf16[2,512,128]{2,1,0:T(8,128)(2,1)} %keyval_ref.1) | copy-start | bytes 786436
  38.4 18.5 %all-to-all-start.2 = ((bf16[8,32,512]{2,1,0:T(8,128)(2,1)}), bf16[8,32,512]{2,1,0:T(8,128)(2,1)S(1)}, u32[]{:S(2)}, u32[]{:S(2)}) async-start(bf16[8,32,512]{2,1,0:T(8,128)(2,1)} %get-tuple-element.33), calls=%async_computation.2 | async-start | bytes 524288 | tf_op jit(solution)/shard_map/all_to_all | solution.py:483
  46.6 6.1 %collective-permute-start.2 = (bf16[2,256,128]{2,1,0:T(8,128)(2,1)S(1)}, bf16[2,256,128]{2,1,0:T(8,128)(2,1)S(1)}, u32[]{:S(2)}, u32[]{:S(2)}) collective-permute-start(bf16[2,256,128]{2,1,0:T(8,128)(2,1)S(1)} %get-tuple-element.34.own_ref), channel_id=1, source_target_pairs={{0,8},{8,0},{16,24},{24,16},{32,40},{40,32},{48,56},{56,48},{64,72... | collective-permute-start | bytes 393224 | tf_op jit(solution)/shard_map/ppermute | solution.py:484
  56.9 6.2 %collective-permute-start.3 = (f32[32,256]{1,0:T(8,128)S(1)}, f32[32,256]{1,0:T(8,128)S(1)}, u32[]{:S(2)}, u32[]{:S(2)}) collective-permute-start(f32[32,256]{1,0:T(8,128)S(1)} %get-tuple-element.39), channel_id=1, source_target_pairs={{0,8},{8,0},{16,24},{24,16},{32,40},{40,32},{48,56},{56,48},{64,72... | collective-permute-start | bytes 98312 | tf_op jit(solution)/shard_map/ppermute | solution.py:516

commit v6 on v5

--- a/solution.py
+++ b/solution.py
@@ -25,6 +25,10 @@
 SHARE_ROWS = HALF + PIECE
 
 same_core = [[chip * 2 + core for chip in range(CHIPS)] for core in range(2)]
+same_chip = [
+    [(chip * 2 + core) * 8 + plane for core in range(2) for plane in range(8)]
+    for chip in range(CHIPS)
+]
 core_swap = [(device, device ^ 1) for device in range(2 * CHIPS)]
 
 vmem = pl.BlockSpec(memory_space=pltpu.VMEM)
@@ -208,6 +212,29 @@
         )
         return dot_nt(query, keys[context])
 
+    first = read(info_ref, 7) == 0
+    own_rows, other_rows = [
+        pl.ds(pl.multiple_of((slots[part] ^ core) * BLK, BLK), BLK) for part in range(2)
+    ]
+    for member in range(2):
+        block = jnp.where(first, own_ref[member, own_rows, :], other_ref[member, other_rows, :])
+        send_ref[8 * member : 8 * member + 8, HALF + STAT :, :] = block.reshape(8, PIECE, HD)
+
+    def write_stats(columns, context):
+        table = columns.T
+        level = table[:HEADS] * SCALE + jnp.log(table[HEADS : 2 * HEADS])
+        pieces = [piece.astype(jnp.float32) for piece in split_three(level)]
+        row = lax.broadcasted_iota(jnp.int32, (STAT, BLK), 0)
+        for pair in range(HEADS // 2):
+            stats = jnp.zeros((STAT, BLK), jnp.float32)
+            for number, piece in enumerate(pieces):
+                stats = jnp.where(row == number, piece[pair : pair + 1], stats)
+            stats = stats.astype(jnp.bfloat16)
+            for half in range(2):
+                target = 2 * (2 * pair + half) + context
+                lanes = slice(half * HALF, (half + 1) * HALF)
+                send_ref[target, HALF : HALF + STAT, :] = stats[:, lanes]
+
     ready = [score(step) for step in range(AHEAD)]
     for step, (context, pair) in enumerate(steps):
         if step + AHEAD < len(steps):
@@ -228,28 +255,10 @@
         for half in range(2):
             target = 2 * (2 * pair + half) + context
             send_ref[target, :HALF, :] = mean[half * HALF : (half + 1) * HALF]
-        columns = jnp.where(lane == step, joined, columns)
-        columns = jnp.where(lane == len(steps) + step, total, columns)
-    table = columns.T
-    level = table[:HEADS] * SCALE + jnp.log(table[HEADS : 2 * HEADS])
-    pieces = [piece.astype(jnp.float32) for piece in split_three(level)]
-    row = lax.broadcasted_iota(jnp.int32, (STAT, BLK), 0)
-    for step, (context, pair) in enumerate(steps):
-        stats = jnp.zeros((STAT, BLK), jnp.float32)
-        for number, piece in enumerate(pieces):
-            stats = jnp.where(row == number, piece[step : step + 1], stats)
-        stats = stats.astype(jnp.bfloat16)
-        for half in range(2):
-            target = 2 * (2 * pair + half) + context
-            lanes = slice(half * HALF, (half + 1) * HALF)
-            send_ref[target, HALF : HALF + STAT, :] = stats[:, lanes]
-    first = read(info_ref, 7) == 0
-    own_rows, other_rows = [
-        pl.ds(pl.multiple_of((slots[part] ^ core) * BLK, BLK), BLK) for part in range(2)
-    ]
-    for member in range(2):
-        block = jnp.where(first, own_ref[member, own_rows, :], other_ref[member, other_rows, :])
-        send_ref[8 * member : 8 * member + 8, HALF + STAT :, :] = block.reshape(8, PIECE, HD)
+        columns = jnp.where(lane == pair, joined, columns)
+        columns = jnp.where(lane == HEADS + pair, total, columns)
+        if pair == HEADS // 2 - 1:
+            write_stats(columns, context)
 
     @pl.when(core == 0)
     def _():
@@ -321,8 +330,8 @@
     def fill(weights):
         for number, ref in enumerate(weights):
             result = jnp.dot(rows, ref[...], preferred_element_type=jnp.float32)
-            lanes = slice(number * BLK, (number + 1) * BLK)
-            out_ref[:, :, lanes] = result.reshape(8, SHARE, BLK).astype(out_ref.dtype)
+            result = result.reshape(8, SHARE, BLK).astype(out_ref.dtype)
+            out_ref[8 * number : 8 * number + 8] = result
 
     @pl.when(core == 0)
     def _():
@@ -333,23 +342,6 @@
         fill((other_ref, own_ref))
 
     anchor_ref[...] = rows_ref[:, HALF:, :].reshape(2, BLK, HD)
-
-
-def total_kernel(parts_ref, mine_ref, theirs_ref):
-    core = lax.axis_index("ctx") % 2
-    for number in range(2):
-        lanes = slice(number * BLK, (number + 1) * BLK)
-        total = parts_ref[0, :, lanes].astype(jnp.float32)
-        for plane in range(1, 8):
-            total = total + parts_ref[plane, :, lanes].astype(jnp.float32)
-
-        @pl.when(core == number)
-        def _(total=total):
-            mine_ref[...] = total
-
-        @pl.when(core != number)
-        def _(total=total):
-            theirs_ref[...] = total
 
 
 def block_kernel(
@@ -471,7 +463,7 @@
     shares, anchor = pl.pallas_call(
         project_kernel,
         out_shape=(
-            shaped((8, SHARE, 2 * BLK), jnp.bfloat16),
+            shaped((2 * 8, SHARE, BLK), jnp.bfloat16),
             shaped((2, BLK, HD), jnp.bfloat16),
         ),
         in_specs=[vmem, vmem, vmem],
@@ -480,7 +472,9 @@
         cost_estimate=cost(2**28, 0, 2**21),
         name="project",
     )(rows, out_weight, other_weight)
-    summands = lax.all_to_all(shares, "tp", 0, 0, tiled=True)
+    summands = lax.all_to_all(
+        shares, ("ctx", "tp"), 0, 0, axis_index_groups=same_chip, tiled=True
+    )
     other_anchor = lax.ppermute(anchor, "ctx", core_swap)
     context_attn = pl.pallas_call(
         block_kernel,
@@ -504,20 +498,8 @@
         name="block_attention",
     )(info, ctx_queries, ctx_keyvals, anchor, other_anchor, far(scores))
     summands, context_attn = lax.optimization_barrier((summands, context_attn))
-    half_shape = shaped((SHARE, BLK), jnp.float32)
-    mine, theirs = pl.pallas_call(
-        total_kernel,
-        out_shape=(half_shape, half_shape),
-        in_specs=[vmem],
-        out_specs=(vmem, vmem),
-        compiler_params=params(),
-        name="plane_sum",
-    )(summands)
-    theirs = lax.ppermute(theirs, "ctx", core_swap)
-    even = lax.axis_index("ctx") % 2 == 0
-    window_proj = jnp.concatenate(
-        [jnp.where(even, mine, theirs), jnp.where(even, theirs, mine)], axis=0
-    )
+    summands = summands.reshape(2, 8, SHARE, BLK).astype(jnp.float32)
+    window_proj = jnp.sum(summands, axis=1).reshape(2 * SHARE, BLK)
     return (context_attn, window_proj)
 
 

time: 64.1 us -> 62.2 us (0.970)
  starting transfers between devices: 22.3 us -> 17.1 us
  waiting for transfers between devices: 2.03 us -> 5.17 us
    ppermute x1 -> x0, starting transfers between devices: 5.35 us -> none  [on_device(): theirs = lax.ppermute(theirs, 'ctx', core_swap)]
    all_to_all x1, starting transfers between devices: 8.19 us -> 13.2 us  [on_device(): lax.all_to_all(shares, ('ctx', 'tp'), 0, 0, axis_index_groups=same_chip,...]
    ppermute x1, starting transfers between devices: 5.08 us -> 0.18 us  [on_device(): other_anchor = lax.ppermute(anchor, 'ctx', core_swap)]
    all_to_all x1, waiting for transfers between devices: 0.01 us -> 3.82 us  [on_device(): lax.all_to_all(shares, ('ctx', 'tp'), 0, 0, axis_index_groups=same_chip,...]
    ppermute x1 -> x0, waiting for transfers between devices: 0.86 us -> none  [on_device(): theirs = lax.ppermute(theirs, 'ctx', core_swap)]
    reduce_sum x0 -> x1, other arithmetic: none -> 0.67 us  [on_device(): window_proj = jnp.sum(summands, axis=1).reshape(2 * SHARE, BLK)]
  transfers between devices with their start and end apart: 5 -> 4, of which waited for: 3 -> 3; matrix products, arithmetic and copies ran while one was open for 0% -> 0% of each run, Pallas kernels for 12% -> 12%
where the time goes in v6:
time: 62.2 us; the launch traced here: 61.8 us
  blocking collectives  28.5 us (46%)
  starting transfers between devices  17.1 us (27%)
  Pallas kernels  9.7 us (16%)
  waiting for transfers between devices  5.17 us (8%)
  between operations  0.7 us (1%)
  other arithmetic  0.67 us (1%)
    all_to_all x1, blocking collectives, on_device(): lax.all_to_all(send, 'ctx', 0, 0, axis_index_groups=same_core, tiled=True)  15.2 us
    all_to_all x1, blocking collectives, on_device(): lax.all_to_all(share, 'ctx', 0, 0, axis_index_groups=same_core, tiled=True)  13.3 us
    all_to_all x1, starting transfers between devices, on_device(): lax.all_to_all(shares, ('ctx', 'tp'), 0, 0, axis_index_groups=same_chip,...  13.2 us
    pallas_call x1, Pallas kernels, on_device(): pl.pallas_call(block_kernel, out_shape=shaped((2 * BLK, HEADS * HD), jnp....  4.2 us
    all_to_all x1, waiting for transfers between devices, on_device(): lax.all_to_all(shares, ('ctx', 'tp'), 0, 0, axis_index_groups=same_chip,...  3.82 us
    ppermute x1, starting transfers between devices, on_device(): other_keyvals = lax.ppermute(ctx_keyvals, 'ctx', core_swap)  3.33 us
    pallas_call x1, Pallas kernels, on_device(): pl.pallas_call(window_kernel, out_shape=(shaped((CHIPS, SEND_ROWS, HD), j...  2.23 us
  transfers between devices with their start and end apart: 4, of which 3 were waited for; matrix products, arithmetic and copies ran while one was open for 0% of the time, Pallas kernels for 12%

profile of v6, /device:TPU:1, one launch (start us, length us, event | category | flops | bytes accessed | tf_op | source)
XLA Modules:
  0.0 61.8 jit_solution(5461593902816564241)
XLA Ops:
  0.6 3.3 %collective-permute-start = (bf16[2,512,128]{2,1,0:T(8,128)(2,1)}, bf16[2,512,128]{2,1,0:T(8,128)(2,1)S(1)}, u32[]{:S(2)}, u32[]{:S(2)}) collective-permute-start(bf16[2,512,128]{2,1,0:T(8,128)(2,1)} %keyval_ref.1), channel_id=1, source_target_pairs={{0,8},{8,0},{16,24},{24,16},{32,40},{40,32},{48,56},{56,48},{64,72... | collective-permute-start | bytes 786440 | tf_op jit(solution)/shard_map/ppermute | solution.py:401
  4.0 1.2 %window_fetch.1 = (bf16[2,4,32,1024]{3,2,1,0:T(8,128)(2,1)S(1)}, bf16[2,512,128]{2,1,0:T(8,128)(2,1)S(1)}, bf16[2,256,128]{2,1,0:T(8,128)(2,1)S(1)}, f32[16,128]{1,0:T(8,128)S(1)}) custom-call(s32[64]{0:T(128)} %map_hbm.1, s32[2]{0:T(128)} %reach_hbm.1, bf16[2,4,2,32,1024]{4,3,2,1,0:T(8,128)(2,1)} %bitcast.5, bf16[2,512,128]{2,1,0:T(8,128)(2,1)} %keyval_ref.1, ...), custom_call_target="tpu_custom_call" | custom-call | flops 16777216 | bytes 2097152 | tf_op jit(solution)/shard_map/window_fetch/pallas_call | solution.py:403
  5.2 0.2 collective-permute-done.other_ref
  5.3 0.4 collective-permute-start.1
  5.7 2.2 %window_parts.1 = (bf16[16,176,128]{2,1,0:T(8,128)(2,1)S(1)}, f32[128,128]{1,0:T(8,128)S(1)}, f32[8,128]{1,0:T(8,128)S(1)}, f32[8,256,256]{2,1,0:T(8,128)}) custom-call(f32[16,128]{1,0:T(8,128)S(1)} %get-tuple-element.19.info_ref, bf16[2,4,32,1024]{3,2,1,0:T(8,128)(2,1)S(1)} %get-tuple-element.21.query_ref, ...), custom_call_target="tpu_custom_call" | custom-call | flops 536870912 | bytes 2097152 | tf_op jit(solution)/shard_map/window_parts/pallas_call | solution.py:428
  7.9 0.0 collective-permute-done.1.other_ref
  8.0 0.0 copy-start.2
  8.0 15.2 %all_to_all.15.got_ref = bf16[16,176,128]{2,1,0:T(8,128)(2,1)S(1)} all-to-all(bf16[16,176,128]{2,1,0:T(8,128)(2,1)S(1)} %get-tuple-element.27), channel_id=1, replica_groups={{0,16,32,48,64,80,96,112,128,144,160,176,192,208,224,240},{8,24,40,56,7..., dimensions={0} | all-to-all | bytes 1441792 | tf_op jit(solution)/shard_map/all_to_all | solution.py:448
  23.2 0.9 %window_join.1 = bf16[16,160,128]{2,1,0:T(8,128)(2,1)S(1)} custom-call(f32[16,128]{1,0:T(8,128)S(1)} %get-tuple-element.19.info_ref, bf16[16,176,128]{2,1,0:T(8,128)(2,1)S(1)} %all_to_all.15.got_ref, f32[128,128]{1,0:T(8,128)S(1)} %get-tuple-element.28.mean_in, f32[8,128]{1,0:T(8,128)S(1)} %get-tuple-element.29.level_in, ...), custom_call_target="tpu_custom_call" | custom-call | flops 1048576 | bytes 1048576 | tf_op jit(solution)/shard_map/window_join/pallas_call | solution.py:449
  24.1 0.0 copy-start
  24.1 0.0 copy-start.1
  24.1 13.3 %all_to_all.16.rows_ref = bf16[16,160,128]{2,1,0:T(8,128)(2,1)S(1)} all-to-all(bf16[16,160,128]{2,1,0:T(8,128)(2,1)S(1)} %window_join.1), channel_id=1, replica_groups={{0,16,32,48,64,80,96,112,128,144,160,176,192,208,224,240},{8,24,40,56,7..., dimensions={0} | all-to-all | bytes 1310720 | tf_op jit(solution)/shard_map/all_to_all | solution.py:462
  37.4 0.0 copy-done.2
  37.4 1.2 %project.1 = (bf16[16,32,256]{2,1,0:T(8,128)(2,1)}, bf16[2,256,128]{2,1,0:T(8,128)(2,1)S(1)}) custom-call(bf16[16,160,128]{2,1,0:T(8,128)(2,1)S(1)} %all_to_all.16.rows_ref, bf16[1024,256]{1,0:T(8,128)(2,1)S(1)} %copy-done.2, bf16[1024,256]{1,0:T(8,128)(2,1)S(1)} %collective-permute-done.1.other_ref), custom_call_target="tpu_custom_call" | custom-call | flops 268435456 | bytes 2097152 | tf_op jit(solution)/shard_map/project/pallas_call | solution.py:463
  38.5 13.2 %all-to-all-start.2 = ((bf16[16,32,256]{2,1,0:T(8,128)(2,1)}), bf16[16,32,256]{2,1,0:T(8,128)(2,1)S(1)}, u32[]{:S(2)}, u32[]{:S(2)}) async-start(bf16[16,32,256]{2,1,0:T(8,128)(2,1)} %get-tuple-element.31), calls=%async_computation.2 | async-start | bytes 524288 | tf_op jit(solution)/shard_map/all_to_all | solution.py:475
  51.7 0.2 collective-permute-start.2
  51.9 1.2 %collective-permute-done.2.other_ref = bf16[2,256,128]{2,1,0:T(8,128)(2,1)S(1)} collective-permute-done((bf16[2,256,128]{2,1,0:T(8,128)(2,1)S(1)}, bf16[2,256,128]{2,1,0:T(8,128)(2,1)S(1)}, u32[]{:S(2)}, u32[]{:S(2)}) %collective-permute-start.2) | collective-permute-done | bytes 131104 | tf_op jit(solution)/shard_map/ppermute | solution.py:478
  53.1 0.0 copy-done
  53.1 0.0 copy-done.1
  53.1 4.2 %block_attention.1 = bf16[512,1024]{1,0:T(8,128)(2,1)} custom-call(f32[16,128]{1,0:T(8,128)S(1)} %get-tuple-element.19.info_ref, bf16[512,1024]{1,0:T(8,128)(2,1)S(1)} %copy-done, bf16[2,512,128]{2,1,0:T(8,128)(2,1)S(1)} %copy-done.1, bf16[2,256,128]{2,1,0:T(8,128)(2,1)S(1)} %get-tuple-element.32.own_ref, ...), custom_call_target="tpu_custom_call" | custom-call | flops 1073741824 | bytes 4194304 | tf_op jit(solution)/shard_map/block_attention/pallas_call | solution.py:479
  57.3 3.8 %all-to-all-done.2 = bf16[16,32,256]{2,1,0:T(8,128)(2,1)S(1)} async-done(((bf16[16,32,256]{2,1,0:T(8,128)(2,1)}), bf16[16,32,256]{2,1,0:T(8,128)(2,1)S(1)}, u32[]{:S(2)}, u32[]{:S(2)}) %all-to-all-start.2) | async-done | bytes 262176 | tf_op jit(solution)/shard_map/all_to_all | solution.py:475
  61.1 0.7 %convert_reduce_fusion = f32[2,32,256]{2,1,0:T(8,128)} fusion(bf16[16,32,256]{2,1,0:T(8,128)(2,1)S(1)} %all-to-all-done.2), kind=kLoop, calls=%fused_computation | loop fusion | flops 245760 | bytes 327680 | tf_op jit(solution)/shard_map/reduce_sum | solution.py:502
Async XLA Ops:
  0.6 4.7 %collective-permute-start = (bf16[2,512,128]{2,1,0:T(8,128)(2,1)}, bf16[2,512,128]{2,1,0:T(8,128)(2,1)S(1)}, u32[]{:S(2)}, u32[]{:S(2)}) collective-permute-start(bf16[2,512,128]{2,1,0:T(8,128)(2,1)} %keyval_ref.1), channel_id=1, source_target_pairs={{0,8},{8,0},{16,24},{24,16},{32,40},{40,32},{48,56},{56,48},{64,72... | collective-permute-start | bytes 786440 | tf_op jit(solution)/shard_map/ppermute | solution.py:401
  5.3 2.6 %collective-permute-start.1 = (bf16[1024,256]{1,0:T(8,128)(2,1)}, bf16[1024,256]{1,0:T(8,128)(2,1)S(1)}, u32[]{:S(2)}, u32[]{:S(2)}) collective-permute-start(bf16[1024,256]{1,0:T(8,128)(2,1)} %own_ref), channel_id=1, source_target_pairs={{0,8},{8,0},{16,24},{24,16},{32,40},{40,32},{48,56},{56,48},{64,72... | collective-permute-start | bytes 1572872 | tf_op jit(solution)/shard_map/ppermute | solution.py:427
  8.0 29.4 %copy-start.2 = (bf16[1024,256]{1,0:T(8,128)(2,1)S(1)}, bf16[1024,256]{1,0:T(8,128)(2,1)}, u32[]{:S(2)}) copy-start(bf16[1024,256]{1,0:T(8,128)(2,1)} %own_ref) | copy-start | bytes 1572868
  24.1 29.0 %copy-start = (bf16[512,1024]{1,0:T(8,128)(2,1)S(1)}, bf16[512,1024]{1,0:T(8,128)(2,1)}, u32[]{:S(2)}) copy-start(bf16[512,1024]{1,0:T(8,128)(2,1)} %query_ref.1) | copy-start | bytes 3145732
  24.1 29.0 %copy-start.1 = (bf16[2,512,128]{2,1,0:T(8,128)(2,1)S(1)}, bf16[2,512,128]{2,1,0:T(8,128)(2,1)}, u32[]{:S(2)}) copy-start(bf16[2,512,128]{2,1,0:T(8,128)(2,1)} %keyval_ref.1) | copy-start | bytes 786436
  38.5 22.6 %all-to-all-start.2 = ((bf16[16,32,256]{2,1,0:T(8,128)(2,1)}), bf16[16,32,256]{2,1,0:T(8,128)(2,1)S(1)}, u32[]{:S(2)}, u32[]{:S(2)}) async-start(bf16[16,32,256]{2,1,0:T(8,128)(2,1)} %get-tuple-element.31), calls=%async_computation.2 | async-start | bytes 524288 | tf_op jit(solution)/shard_map/all_to_all | solution.py:475
  51.7 1.3 %collective-permute-start.2 = (bf16[2,256,128]{2,1,0:T(8,128)(2,1)S(1)}, bf16[2,256,128]{2,1,0:T(8,128)(2,1)S(1)}, u32[]{:S(2)}, u32[]{:S(2)}) collective-permute-start(bf16[2,256,128]{2,1,0:T(8,128)(2,1)S(1)} %get-tuple-element.32.own_ref), channel_id=1, source_target_pairs={{0,8},{8,0},{16,24},{24,16},{32,40},{40,32},{48,56},{56,48},{64,72... | collective-permute-start | bytes 393224 | tf_op jit(solution)/shard_map/ppermute | solution.py:478

commit v7 on v6

--- a/solution.py
+++ b/solution.py
@@ -19,6 +19,7 @@
 SCALE = 1.0 / math.sqrt(HD)
 SCALE2 = SCALE * math.log2(math.e)
 AHEAD = 2
+EARLY = 4
 masked_score = -1e30
 
 SEND_ROWS = HALF + STAT + PIECE
@@ -74,6 +75,29 @@
             ready.append(dot_nt(query_ref[:, head * HD : (head + 1) * HD], keys))
         if head >= AHEAD:
             yield head - AHEAD, ready.pop(0)
+
+
+def staged(score, count):
+    ready = []
+    for step in range(count + AHEAD):
+        if step < count:
+            ready.append(score(step))
+        if step >= AHEAD:
+            yield step - AHEAD, ready.pop(0)
+
+
+steps = [(context, pair) for context in range(2) for pair in range(HEADS // 2)]
+
+
+def pair_query(query_ref, step):
+    context, pair = steps[step]
+    return jnp.concatenate(
+        [
+            query_ref[context, :, :, head * HD : (head + 1) * HD].reshape(HALF, HD)
+            for head in (2 * pair, 2 * pair + 1)
+        ],
+        axis=0,
+    )
 
 
 def read(info_ref, number):
@@ -107,6 +131,7 @@
     keyval_ref,
     window_ref,
     info_ref,
+    table_ref,
     map_ref,
     reach_ref,
     done,
@@ -152,6 +177,16 @@
     for copy in copies[2:]:
         copy.wait()
 
+    @pl.when(core == 1)
+    def _():
+        taken = pl.ds(pl.multiple_of(map_ref[2 * position] // NB * BLK, BLK), BLK)
+        keys, values = keyval_ref[0, taken, :], keyval_ref[1, taken, :]
+        for step, raw in staged(lambda step: dot_nt(pair_query(query_ref, step), keys), EARLY):
+            top, total, weights = row_softmax(raw)
+            table_ref[0, step] = jnp.broadcast_to(top, (BLK, HD))
+            table_ref[1, step] = jnp.broadcast_to(total, (BLK, HD))
+            table_ref[2, step] = weigh(weights, values)
+
 
 def window_kernel(
     info_ref,
@@ -159,6 +194,7 @@
     own_ref,
     other_ref,
     window_ref,
+    table_ref,
     rows_hbm,
     send_ref,
     mean_ref,
@@ -183,16 +219,12 @@
 
     sources = (own_ref, other_ref)
     lane = lax.broadcasted_iota(jnp.int32, (BLK, HD), 1)
-    columns = jnp.zeros((BLK, HD), jnp.float32)
-    steps = [(context, pair) for context in range(2) for pair in range(HEADS // 2)]
     keys = []
     values = []
     biases = []
     for context in range(2):
         rows = [block_rows(part, context) for part in range(2)]
-        keys.append(
-            jnp.concatenate([ref[0, taken, :] for ref, taken in zip(sources, rows)], axis=0)
-        )
+        keys.append([ref[0, taken, :] for ref, taken in zip(sources, rows)])
         values.append([ref[1, taken, :] for ref, taken in zip(sources, rows)])
         biases.append(
             [
@@ -200,17 +232,6 @@
                 for number in (3 + 2 * context, 4 + 2 * context)
             ]
         )
-
-    def score(step):
-        context, pair = steps[step]
-        query = jnp.concatenate(
-            [
-                query_ref[context, :, :, head * HD : (head + 1) * HD].reshape(HALF, HD)
-                for head in (2 * pair, 2 * pair + 1)
-            ],
-            axis=0,
-        )
-        return dot_nt(query, keys[context])
 
     first = read(info_ref, 7) == 0
     own_rows, other_rows = [
@@ -235,19 +256,15 @@
                 lanes = slice(half * HALF, (half + 1) * HALF)
                 send_ref[target, HALF : HALF + STAT, :] = stats[:, lanes]
 
-    ready = [score(step) for step in range(AHEAD)]
-    for step, (context, pair) in enumerate(steps):
-        if step + AHEAD < len(steps):
-            ready.append(score(step + AHEAD))
-        raw = ready.pop(0)
-        parts = []
-        for part in range(2):
-            top, total, weights = row_softmax(raw[:, part * BLK : (part + 1) * BLK])
-            parts.append(
-                (top + biases[context][part], total, weigh(weights, values[context][part]))
-            )
-        joined = jnp.maximum(parts[0][0], parts[1][0])
-        lifts = [jnp.exp2((part[0] - joined) * SCALE2) for part in parts]
+    def part_of(raw, step, part):
+        top, total, weights = row_softmax(raw)
+        return top, total, weigh(weights, values[steps[step][0]][part])
+
+    def merge(step, parts, columns):
+        context, pair = steps[step]
+        tops = [part[0] + bias for part, bias in zip(parts, biases[context])]
+        joined = jnp.maximum(tops[0], tops[1])
+        lifts = [jnp.exp2((top - joined) * SCALE2) for top in tops]
         total = parts[0][1] * lifts[0] + parts[1][1] * lifts[1]
         inverse = 1.0 / total
         mean = parts[0][2] * (lifts[0] * inverse) + parts[1][2] * (lifts[1] * inverse)
@@ -255,10 +272,42 @@
         for half in range(2):
             target = 2 * (2 * pair + half) + context
             send_ref[target, :HALF, :] = mean[half * HALF : (half + 1) * HALF]
+        if pair == 0:
+            columns = jnp.zeros((BLK, HD), jnp.float32)
         columns = jnp.where(lane == pair, joined, columns)
         columns = jnp.where(lane == HEADS + pair, total, columns)
         if pair == HEADS // 2 - 1:
             write_stats(columns, context)
+        return columns
+
+    both = [jnp.concatenate(pair, axis=0) for pair in keys]
+
+    def run(early):
+        columns = None
+
+        def score(step):
+            context = steps[step][0]
+            return dot_nt(
+                pair_query(query_ref, step), keys[context][1] if step < early else both[context]
+            )
+
+        for step, raw in staged(score, len(steps)):
+            if step < early:
+                parts = [[table_ref[number, step] for number in range(3)], part_of(raw, step, 1)]
+            else:
+                parts = [
+                    part_of(raw[:, part * BLK : (part + 1) * BLK], step, part)
+                    for part in range(2)
+                ]
+            columns = merge(step, parts, columns)
+
+    @pl.when(core == 0)
+    def _():
+        run(0)
+
+    @pl.when(core == 1)
+    def _():
+        run(EARLY)
 
     @pl.when(core == 0)
     def _():
@@ -400,16 +449,17 @@
 ):
     other_keyvals = lax.ppermute(ctx_keyvals, "ctx", core_swap)
     halves = win_queries.reshape(2, 4, 2, SHARE, HEADS * HD)
-    queries, keyvals, window, info = pl.pallas_call(
+    queries, keyvals, window, info, table = pl.pallas_call(
         fetch_kernel,
         out_shape=(
             shaped((2, 4, SHARE, HEADS * HD), jnp.bfloat16),
             shaped((2, 2 * BLK, HD), jnp.bfloat16),
             shaped((2, BLK, HD), jnp.bfloat16),
             shaped((16, HD), jnp.float32),
+            shaped((3, EARLY, BLK, HD), jnp.float32),
         ),
         in_specs=[hbm] * 5,
-        out_specs=(vmem,) * 4,
+        out_specs=(vmem,) * 5,
         scratch_shapes=[
             pltpu.SMEM((2 * NB,), jnp.int32),
             pltpu.SMEM((2,), jnp.int32),
@@ -433,7 +483,7 @@
             shaped((8, HALF), jnp.float32),
             pltpu.HBM((HEADS, BLK, BLK), jnp.float32),
         ),
-        in_specs=[vmem] * 5 + [hbm],
+        in_specs=[vmem] * 6 + [hbm],
         out_specs=(vmem, vmem, vmem, hbm),
         scratch_shapes=[
             pltpu.VMEM((HEADS, BLK, BLK), jnp.float32),
@@ -443,7 +493,7 @@
         compiler_params=params(),
         cost_estimate=cost(2**29, 2**20, 2**21),
         name="window_parts",
-    )(info, queries, keyvals, other_keyvals, window, far(ctx_queries))
+    )(info, queries, keyvals, other_keyvals, window, table, far(ctx_queries))
     send, other_weight = lax.optimization_barrier((send, other_weight))
     got = lax.all_to_all(send, "ctx", 0, 0, axis_index_groups=same_core, tiled=True)
     share = pl.pallas_call(

time: 62.2 us -> 62.2 us (level)
  transfers between devices with their start and end apart: 4 -> 4, of which waited for: 3 -> 2; matrix products, arithmetic and copies ran while one was open for 0% -> 0% of each run, Pallas kernels for 12% -> 13%
where the time goes in v7:
time: 62.2 us; the launch traced here: 61.7 us
  blocking collectives  28.1 us (45%)
  starting transfers between devices  17.3 us (28%)
  Pallas kernels  10.1 us (16%)
  waiting for transfers between devices  4.85 us (8%)
  between operations  0.7 us (1%)
  other arithmetic  0.67 us (1%)
    all_to_all x1, blocking collectives, on_device(): lax.all_to_all(send, 'ctx', 0, 0, axis_index_groups=same_core, tiled=True)  14.9 us
    all_to_all x1, starting transfers between devices, on_device(): lax.all_to_all(shares, ('ctx', 'tp'), 0, 0, axis_index_groups=same_chip,...  13.5 us
    all_to_all x1, blocking collectives, on_device(): lax.all_to_all(share, 'ctx', 0, 0, axis_index_groups=same_core, tiled=True)  13.2 us
    pallas_call x1, Pallas kernels, on_device(): pl.pallas_call(block_kernel, out_shape=shaped((2 * BLK, HEADS * HD), jnp....  4.2 us
    all_to_all x1, waiting for transfers between devices, on_device(): lax.all_to_all(shares, ('ctx', 'tp'), 0, 0, axis_index_groups=same_chip,...  3.82 us
    ppermute x1, starting transfers between devices, on_device(): other_keyvals = lax.ppermute(ctx_keyvals, 'ctx', core_swap)  3.33 us
    pallas_call x1, Pallas kernels, on_device(): pl.pallas_call(window_kernel, out_shape=(shaped((CHIPS, SEND_ROWS, HD), j...  2.06 us
    pallas_call x1, Pallas kernels, on_device(): pl.pallas_call(fetch_kernel, out_shape=(shaped((2, 4, SHARE, HEADS * HD),...  1.78 us
  transfers between devices with their start and end apart: 4, of which 2 were waited for; matrix products, arithmetic and copies ran while one was open for 0% of the time, Pallas kernels for 13%

profile of v7, /device:TPU:1, one launch (start us, length us, event | category | flops | bytes accessed | tf_op | source)
XLA Modules:
  0.0 61.7 jit_solution(18065149825099116089)
XLA Ops:
  0.6 3.3 %collective-permute-start = (bf16[2,512,128]{2,1,0:T(8,128)(2,1)}, bf16[2,512,128]{2,1,0:T(8,128)(2,1)S(1)}, u32[]{:S(2)}, u32[]{:S(2)}) collective-permute-start(bf16[2,512,128]{2,1,0:T(8,128)(2,1)} %keyval_ref.1), channel_id=1, source_target_pairs={{0,8},{8,0},{16,24},{24,16},{32,40},{40,32},{48,56},{56,48},{64,72... | collective-permute-start | bytes 786440 | tf_op jit(solution)/shard_map/ppermute | solution.py:450
  4.0 1.8 %window_fetch.1 = (bf16[2,4,32,1024]{3,2,1,0:T(8,128)(2,1)S(1)}, bf16[2,512,128]{2,1,0:T(8,128)(2,1)S(1)}, bf16[2,256,128]{2,1,0:T(8,128)(2,1)S(1)}, f32[16,128]{1,0:T(8,128)S(1)}, f32[3,4,256,128]{3,2,1,0:T(8,128)S(1)}) custom-call(s32[64]{0:T(128)} %map_hbm.1, s32[2]{0:T(128)} %reach_hbm.1, bf16[2,4,2,32,1024]{4,3,2,1,0:T(8,128)(2,1)} %bitcast.5, ...), custom_call_target="tpu_custom_call" | custom-call | flops 16777216 | bytes 2097152 | tf_op jit(solution)/shard_map/window_fetch/pallas_call | solution.py:452
  5.7 0.0 collective-permute-done.other_ref
  5.8 0.1 collective-permute-start.1
  5.9 2.1 %window_parts.1 = (bf16[16,176,128]{2,1,0:T(8,128)(2,1)S(1)}, f32[128,128]{1,0:T(8,128)S(1)}, f32[8,128]{1,0:T(8,128)S(1)}, f32[8,256,256]{2,1,0:T(8,128)}) custom-call(f32[16,128]{1,0:T(8,128)S(1)} %get-tuple-element.20.info_ref, bf16[2,4,32,1024]{3,2,1,0:T(8,128)(2,1)S(1)} %get-tuple-element.22.query_ref, ...), custom_call_target="tpu_custom_call" | custom-call | flops 536870912 | bytes 2097152 | tf_op jit(solution)/shard_map/window_parts/pallas_call | solution.py:478
  7.9 0.0 collective-permute-done.1.other_ref
  8.0 0.0 copy-start.2
  8.0 14.9 %all_to_all.15.got_ref = bf16[16,176,128]{2,1,0:T(8,128)(2,1)S(1)} all-to-all(bf16[16,176,128]{2,1,0:T(8,128)(2,1)S(1)} %get-tuple-element.29), channel_id=1, replica_groups={{0,16,32,48,64,80,96,112,128,144,160,176,192,208,224,240},{8,24,40,56,7..., dimensions={0} | all-to-all | bytes 1441792 | tf_op jit(solution)/shard_map/all_to_all | solution.py:498
  22.9 0.9 %window_join.1 = bf16[16,160,128]{2,1,0:T(8,128)(2,1)S(1)} custom-call(f32[16,128]{1,0:T(8,128)S(1)} %get-tuple-element.20.info_ref, bf16[16,176,128]{2,1,0:T(8,128)(2,1)S(1)} %all_to_all.15.got_ref, f32[128,128]{1,0:T(8,128)S(1)} %get-tuple-element.30.mean_in, f32[8,128]{1,0:T(8,128)S(1)} %get-tuple-element.31.level_in, ...), custom_call_target="tpu_custom_call" | custom-call | flops 1048576 | bytes 1048576 | tf_op jit(solution)/shard_map/window_join/pallas_call | solution.py:499
  23.8 0.0 copy-start
  23.8 0.0 copy-start.1
  23.8 13.2 %all_to_all.16.rows_ref = bf16[16,160,128]{2,1,0:T(8,128)(2,1)S(1)} all-to-all(bf16[16,160,128]{2,1,0:T(8,128)(2,1)S(1)} %window_join.1), channel_id=1, replica_groups={{0,16,32,48,64,80,96,112,128,144,160,176,192,208,224,240},{8,24,40,56,7..., dimensions={0} | all-to-all | bytes 1310720 | tf_op jit(solution)/shard_map/all_to_all | solution.py:512
  37.0 0.0 copy-done.2
  37.0 1.2 %project.1 = (bf16[16,32,256]{2,1,0:T(8,128)(2,1)}, bf16[2,256,128]{2,1,0:T(8,128)(2,1)S(1)}) custom-call(bf16[16,160,128]{2,1,0:T(8,128)(2,1)S(1)} %all_to_all.16.rows_ref, bf16[1024,256]{1,0:T(8,128)(2,1)S(1)} %copy-done.2, bf16[1024,256]{1,0:T(8,128)(2,1)S(1)} %collective-permute-done.1.other_ref), custom_call_target="tpu_custom_call" | custom-call | flops 268435456 | bytes 2097152 | tf_op jit(solution)/shard_map/project/pallas_call | solution.py:513
  38.2 13.5 %all-to-all-start.2 = ((bf16[16,32,256]{2,1,0:T(8,128)(2,1)}), bf16[16,32,256]{2,1,0:T(8,128)(2,1)S(1)}, u32[]{:S(2)}, u32[]{:S(2)}) async-start(bf16[16,32,256]{2,1,0:T(8,128)(2,1)} %get-tuple-element.33), calls=%async_computation.2 | async-start | bytes 524288 | tf_op jit(solution)/shard_map/all_to_all | solution.py:525
  51.7 0.4 collective-permute-start.2
  52.1 1.0 %collective-permute-done.2.other_ref = bf16[2,256,128]{2,1,0:T(8,128)(2,1)S(1)} collective-permute-done((bf16[2,256,128]{2,1,0:T(8,128)(2,1)S(1)}, bf16[2,256,128]{2,1,0:T(8,128)(2,1)S(1)}, u32[]{:S(2)}, u32[]{:S(2)}) %collective-permute-start.2) | collective-permute-done | bytes 131104 | tf_op jit(solution)/shard_map/ppermute | solution.py:528
  53.0 0.0 copy-done
  53.0 0.0 copy-done.1
  53.0 4.2 %block_attention.1 = bf16[512,1024]{1,0:T(8,128)(2,1)} custom-call(f32[16,128]{1,0:T(8,128)S(1)} %get-tuple-element.20.info_ref, bf16[512,1024]{1,0:T(8,128)(2,1)S(1)} %copy-done, bf16[2,512,128]{2,1,0:T(8,128)(2,1)S(1)} %copy-done.1, bf16[2,256,128]{2,1,0:T(8,128)(2,1)S(1)} %get-tuple-element.34.own_ref, ...), custom_call_target="tpu_custom_call" | custom-call | flops 1073741824 | bytes 4194304 | tf_op jit(solution)/shard_map/block_attention/pallas_call | solution.py:529
  57.3 3.8 %all-to-all-done.2 = bf16[16,32,256]{2,1,0:T(8,128)(2,1)S(1)} async-done(((bf16[16,32,256]{2,1,0:T(8,128)(2,1)}), bf16[16,32,256]{2,1,0:T(8,128)(2,1)S(1)}, u32[]{:S(2)}, u32[]{:S(2)}) %all-to-all-start.2) | async-done | bytes 262176 | tf_op jit(solution)/shard_map/all_to_all | solution.py:525
  61.1 0.7 %convert_reduce_fusion = f32[2,32,256]{2,1,0:T(8,128)} fusion(bf16[16,32,256]{2,1,0:T(8,128)(2,1)S(1)} %all-to-all-done.2), kind=kLoop, calls=%fused_computation | loop fusion | flops 245760 | bytes 327680 | tf_op jit(solution)/shard_map/reduce_sum | solution.py:552
Async XLA Ops:
  0.6 5.1 %collective-permute-start = (bf16[2,512,128]{2,1,0:T(8,128)(2,1)}, bf16[2,512,128]{2,1,0:T(8,128)(2,1)S(1)}, u32[]{:S(2)}, u32[]{:S(2)}) collective-permute-start(bf16[2,512,128]{2,1,0:T(8,128)(2,1)} %keyval_ref.1), channel_id=1, source_target_pairs={{0,8},{8,0},{16,24},{24,16},{32,40},{40,32},{48,56},{56,48},{64,72... | collective-permute-start | bytes 786440 | tf_op jit(solution)/shard_map/ppermute | solution.py:450
  5.8 2.2 %collective-permute-start.1 = (bf16[1024,256]{1,0:T(8,128)(2,1)}, bf16[1024,256]{1,0:T(8,128)(2,1)S(1)}, u32[]{:S(2)}, u32[]{:S(2)}) collective-permute-start(bf16[1024,256]{1,0:T(8,128)(2,1)} %own_ref), channel_id=1, source_target_pairs={{0,8},{8,0},{16,24},{24,16},{32,40},{40,32},{48,56},{56,48},{64,72... | collective-permute-start | bytes 1572872 | tf_op jit(solution)/shard_map/ppermute | solution.py:477
  8.0 29.0 %copy-start.2 = (bf16[1024,256]{1,0:T(8,128)(2,1)S(1)}, bf16[1024,256]{1,0:T(8,128)(2,1)}, u32[]{:S(2)}) copy-start(bf16[1024,256]{1,0:T(8,128)(2,1)} %own_ref) | copy-start | bytes 1572868
  23.8 29.3 %copy-start = (bf16[512,1024]{1,0:T(8,128)(2,1)S(1)}, bf16[512,1024]{1,0:T(8,128)(2,1)}, u32[]{:S(2)}) copy-start(bf16[512,1024]{1,0:T(8,128)(2,1)} %query_ref.1) | copy-start | bytes 3145732
  23.8 29.2 %copy-start.1 = (bf16[2,512,128]{2,1,0:T(8,128)(2,1)S(1)}, bf16[2,512,128]{2,1,0:T(8,128)(2,1)}, u32[]{:S(2)}) copy-start(bf16[2,512,128]{2,1,0:T(8,128)(2,1)} %keyval_ref.1) | copy-start | bytes 786436
  38.2 22.9 %all-to-all-start.2 = ((bf16[16,32,256]{2,1,0:T(8,128)(2,1)}), bf16[16,32,256]{2,1,0:T(8,128)(2,1)S(1)}, u32[]{:S(2)}, u32[]{:S(2)}) async-start(bf16[16,32,256]{2,1,0:T(8,128)(2,1)} %get-tuple-element.33), calls=%async_computation.2 | async-start | bytes 524288 | tf_op jit(solution)/shard_map/all_to_all | solution.py:525
  51.7 1.4 %collective-permute-start.2 = (bf16[2,256,128]{2,1,0:T(8,128)(2,1)S(1)}, bf16[2,256,128]{2,1,0:T(8,128)(2,1)S(1)}, u32[]{:S(2)}, u32[]{:S(2)}) collective-permute-start(bf16[2,256,128]{2,1,0:T(8,128)(2,1)S(1)} %get-tuple-element.34.own_ref), channel_id=1, source_target_pairs={{0,8},{8,0},{16,24},{24,16},{32,40},{40,32},{48,56},{56,48},{64,72... | collective-permute-start | bytes 393224 | tf_op jit(solution)/shard_map/ppermute | solution.py:528

commit v8 on v6

--- a/solution.py
+++ b/solution.py
@@ -24,7 +24,10 @@
 SEND_ROWS = HALF + STAT + PIECE
 SHARE_ROWS = HALF + PIECE
 
-same_core = [[chip * 2 + core for chip in range(CHIPS)] for core in range(2)]
+same_core = [
+    [(place + core * CHIPS // 2) % CHIPS * 2 + core for place in range(CHIPS)]
+    for core in range(2)
+]
 same_chip = [
     [(chip * 2 + core) * 8 + plane for core in range(2) for plane in range(8)]
     for chip in range(CHIPS)
@@ -83,7 +86,7 @@
 def own_window(query_ref, window_ref):
     position = lax.axis_index("ctx")
     core = position % 2
-    chip = position // 2
+    chip = (position // 2 + core * (CHIPS // 2)) % CHIPS
     lanes = pl.ds(pl.multiple_of(chip // 2 * HD, HD), HD)
     query = query_ref[chip % 2, :, :, lanes].reshape(HALF, HD)
     raw = dot_nt(query, window_ref[0])
@@ -113,7 +116,7 @@
 ):
     position = lax.axis_index("ctx")
     core = position % 2
-    chip = position // 2
+    chip = (position // 2 + core * (CHIPS // 2)) % CHIPS
     copies = [
         pltpu.make_async_copy(source, target, done.at[number])
         for number, (source, target) in enumerate(
@@ -138,7 +141,7 @@
     holder = jnp.int32(0)
     for number in range(2 * NB):
         holder = jnp.where(map_ref[number] == core * NB, number // 4, holder)
-    put(0, holder)
+    put(0, (holder + core * (CHIPS // 2)) % CHIPS)
     for part, device in enumerate((position, partner)):
         put(1 + part, map_ref[2 * device] // NB)
         for context in range(2):

time: 62.2 us -> 62.1 us (level)
  blocking collectives: 28.5 us -> 26.8 us
  starting transfers between devices: 17.1 us -> 18.6 us
    all_to_all x1, blocking collectives: 15.2 us -> 13.5 us  [on_device(): lax.all_to_all(send, 'ctx', 0, 0, axis_index_groups=same_core, tiled=True)]
    all_to_all x1, starting transfers between devices: 13.2 us -> 14.8 us  [on_device(): lax.all_to_all(shares, ('ctx', 'tp'), 0, 0, axis_index_groups=same_chip,...]
where the time goes in v8:
time: 62.1 us; the launch traced here: 61.7 us
  blocking collectives  26.8 us (43%)
  starting transfers between devices  18.6 us (30%)
  Pallas kernels  9.7 us (16%)
  waiting for transfers between devices  5.16 us (8%)
  between operations  0.7 us (1%)
  other arithmetic  0.67 us (1%)
    all_to_all x1, starting transfers between devices, on_device(): lax.all_to_all(shares, ('ctx', 'tp'), 0, 0, axis_index_groups=same_chip,...  14.8 us
    all_to_all x1, blocking collectives, on_device(): lax.all_to_all(send, 'ctx', 0, 0, axis_index_groups=same_core, tiled=True)  13.5 us
    all_to_all x1, blocking collectives, on_device(): lax.all_to_all(share, 'ctx', 0, 0, axis_index_groups=same_core, tiled=True)  13.3 us
    pallas_call x1, Pallas kernels, on_device(): pl.pallas_call(block_kernel, out_shape=shaped((2 * BLK, HEADS * HD), jnp....  4.2 us
    all_to_all x1, waiting for transfers between devices, on_device(): lax.all_to_all(shares, ('ctx', 'tp'), 0, 0, axis_index_groups=same_chip,...  3.82 us
    ppermute x1, starting transfers between devices, on_device(): other_keyvals = lax.ppermute(ctx_keyvals, 'ctx', core_swap)  3.33 us
    pallas_call x1, Pallas kernels, on_device(): pl.pallas_call(window_kernel, out_shape=(shaped((CHIPS, SEND_ROWS, HD), j...  2.23 us
  transfers between devices with their start and end apart: 4, of which 3 were waited for; matrix products, arithmetic and copies ran while one was open for 0% of the time, Pallas kernels for 12%

profile of v8, /device:TPU:1, one launch (start us, length us, event | category | flops | bytes accessed | tf_op | source)
XLA Modules:
  0.0 61.7 jit_solution(6504215617814989454)
XLA Ops:
  0.6 3.3 %collective-permute-start = (bf16[2,512,128]{2,1,0:T(8,128)(2,1)}, bf16[2,512,128]{2,1,0:T(8,128)(2,1)S(1)}, u32[]{:S(2)}, u32[]{:S(2)}) collective-permute-start(bf16[2,512,128]{2,1,0:T(8,128)(2,1)} %keyval_ref.1), channel_id=1, source_target_pairs={{0,8},{8,0},{16,24},{24,16},{32,40},{40,32},{48,56},{56,48},{64,72... | collective-permute-start | bytes 786440 | tf_op jit(solution)/shard_map/ppermute | solution.py:404
  4.0 1.2 %window_fetch.1 = (bf16[2,4,32,1024]{3,2,1,0:T(8,128)(2,1)S(1)}, bf16[2,512,128]{2,1,0:T(8,128)(2,1)S(1)}, bf16[2,256,128]{2,1,0:T(8,128)(2,1)S(1)}, f32[16,128]{1,0:T(8,128)S(1)}) custom-call(s32[64]{0:T(128)} %map_hbm.1, s32[2]{0:T(128)} %reach_hbm.1, bf16[2,4,2,32,1024]{4,3,2,1,0:T(8,128)(2,1)} %bitcast.5, bf16[2,512,128]{2,1,0:T(8,128)(2,1)} %keyval_ref.1, ...), custom_call_target="tpu_custom_call" | custom-call | flops 16777216 | bytes 2097152 | tf_op jit(solution)/shard_map/window_fetch/pallas_call | solution.py:406
  5.2 0.2 collective-permute-done.other_ref
  5.3 0.4 collective-permute-start.1
  5.7 2.2 %window_parts.1 = (bf16[16,176,128]{2,1,0:T(8,128)(2,1)S(1)}, f32[128,128]{1,0:T(8,128)S(1)}, f32[8,128]{1,0:T(8,128)S(1)}, f32[8,256,256]{2,1,0:T(8,128)}) custom-call(f32[16,128]{1,0:T(8,128)S(1)} %get-tuple-element.19.info_ref, bf16[2,4,32,1024]{3,2,1,0:T(8,128)(2,1)S(1)} %get-tuple-element.21.query_ref, ...), custom_call_target="tpu_custom_call" | custom-call | flops 536870912 | bytes 2097152 | tf_op jit(solution)/shard_map/window_parts/pallas_call | solution.py:431
  7.9 0.0 collective-permute-done.1.other_ref
  8.0 0.0 copy-start.2
  8.0 13.5 %all_to_all.15.got_ref = bf16[16,176,128]{2,1,0:T(8,128)(2,1)S(1)} all-to-all(bf16[16,176,128]{2,1,0:T(8,128)(2,1)S(1)} %get-tuple-element.27), channel_id=1, replica_groups={{0,16,32,48,64,80,96,112,128,144,160,176,192,208,224,240},{136,152,168,..., dimensions={0} | all-to-all | bytes 1441792 | tf_op jit(solution)/shard_map/all_to_all | solution.py:451
  21.5 0.9 %window_join.1 = bf16[16,160,128]{2,1,0:T(8,128)(2,1)S(1)} custom-call(f32[16,128]{1,0:T(8,128)S(1)} %get-tuple-element.19.info_ref, bf16[16,176,128]{2,1,0:T(8,128)(2,1)S(1)} %all_to_all.15.got_ref, f32[128,128]{1,0:T(8,128)S(1)} %get-tuple-element.28.mean_in, f32[8,128]{1,0:T(8,128)S(1)} %get-tuple-element.29.level_in, ...), custom_call_target="tpu_custom_call" | custom-call | flops 1048576 | bytes 1048576 | tf_op jit(solution)/shard_map/window_join/pallas_call | solution.py:452
  22.4 0.0 copy-start
  22.4 0.0 copy-start.1
  22.4 13.3 %all_to_all.16.rows_ref = bf16[16,160,128]{2,1,0:T(8,128)(2,1)S(1)} all-to-all(bf16[16,160,128]{2,1,0:T(8,128)(2,1)S(1)} %window_join.1), channel_id=1, replica_groups={{0,16,32,48,64,80,96,112,128,144,160,176,192,208,224,240},{136,152,168,..., dimensions={0} | all-to-all | bytes 1310720 | tf_op jit(solution)/shard_map/all_to_all | solution.py:465
  35.7 0.0 copy-done.2
  35.7 1.2 %project.1 = (bf16[16,32,256]{2,1,0:T(8,128)(2,1)}, bf16[2,256,128]{2,1,0:T(8,128)(2,1)S(1)}) custom-call(bf16[16,160,128]{2,1,0:T(8,128)(2,1)S(1)} %all_to_all.16.rows_ref, bf16[1024,256]{1,0:T(8,128)(2,1)S(1)} %copy-done.2, bf16[1024,256]{1,0:T(8,128)(2,1)S(1)} %collective-permute-done.1.other_ref), custom_call_target="tpu_custom_call" | custom-call | flops 268435456 | bytes 2097152 | tf_op jit(solution)/shard_map/project/pallas_call | solution.py:466
  36.9 14.8 %all-to-all-start.2 = ((bf16[16,32,256]{2,1,0:T(8,128)(2,1)}), bf16[16,32,256]{2,1,0:T(8,128)(2,1)S(1)}, u32[]{:S(2)}, u32[]{:S(2)}) async-start(bf16[16,32,256]{2,1,0:T(8,128)(2,1)} %get-tuple-element.31), calls=%async_computation.2 | async-start | bytes 524288 | tf_op jit(solution)/shard_map/all_to_all | solution.py:478
  51.6 0.2 collective-permute-start.2
  51.8 1.2 %collective-permute-done.2.other_ref = bf16[2,256,128]{2,1,0:T(8,128)(2,1)S(1)} collective-permute-done((bf16[2,256,128]{2,1,0:T(8,128)(2,1)S(1)}, bf16[2,256,128]{2,1,0:T(8,128)(2,1)S(1)}, u32[]{:S(2)}, u32[]{:S(2)}) %collective-permute-start.2) | collective-permute-done | bytes 131104 | tf_op jit(solution)/shard_map/ppermute | solution.py:481
  53.0 0.0 copy-done
  53.0 0.0 copy-done.1
  53.0 4.2 %block_attention.1 = bf16[512,1024]{1,0:T(8,128)(2,1)} custom-call(f32[16,128]{1,0:T(8,128)S(1)} %get-tuple-element.19.info_ref, bf16[512,1024]{1,0:T(8,128)(2,1)S(1)} %copy-done, bf16[2,512,128]{2,1,0:T(8,128)(2,1)S(1)} %copy-done.1, bf16[2,256,128]{2,1,0:T(8,128)(2,1)S(1)} %get-tuple-element.32.own_ref, ...), custom_call_target="tpu_custom_call" | custom-call | flops 1073741824 | bytes 4194304 | tf_op jit(solution)/shard_map/block_attention/pallas_call | solution.py:482
  57.2 3.8 %all-to-all-done.2 = bf16[16,32,256]{2,1,0:T(8,128)(2,1)S(1)} async-done(((bf16[16,32,256]{2,1,0:T(8,128)(2,1)}), bf16[16,32,256]{2,1,0:T(8,128)(2,1)S(1)}, u32[]{:S(2)}, u32[]{:S(2)}) %all-to-all-start.2) | async-done | bytes 262176 | tf_op jit(solution)/shard_map/all_to_all | solution.py:478
  61.0 0.7 %convert_reduce_fusion = f32[2,32,256]{2,1,0:T(8,128)} fusion(bf16[16,32,256]{2,1,0:T(8,128)(2,1)S(1)} %all-to-all-done.2), kind=kLoop, calls=%fused_computation | loop fusion | flops 245760 | bytes 327680 | tf_op jit(solution)/shard_map/reduce_sum | solution.py:505
Async XLA Ops:
  0.6 4.7 %collective-permute-start = (bf16[2,512,128]{2,1,0:T(8,128)(2,1)}, bf16[2,512,128]{2,1,0:T(8,128)(2,1)S(1)}, u32[]{:S(2)}, u32[]{:S(2)}) collective-permute-start(bf16[2,512,128]{2,1,0:T(8,128)(2,1)} %keyval_ref.1), channel_id=1, source_target_pairs={{0,8},{8,0},{16,24},{24,16},{32,40},{40,32},{48,56},{56,48},{64,72... | collective-permute-start | bytes 786440 | tf_op jit(solution)/shard_map/ppermute | solution.py:404
  5.3 2.6 %collective-permute-start.1 = (bf16[1024,256]{1,0:T(8,128)(2,1)}, bf16[1024,256]{1,0:T(8,128)(2,1)S(1)}, u32[]{:S(2)}, u32[]{:S(2)}) collective-permute-start(bf16[1024,256]{1,0:T(8,128)(2,1)} %own_ref), channel_id=1, source_target_pairs={{0,8},{8,0},{16,24},{24,16},{32,40},{40,32},{48,56},{56,48},{64,72... | collective-permute-start | bytes 1572872 | tf_op jit(solution)/shard_map/ppermute | solution.py:430
  8.0 27.7 %copy-start.2 = (bf16[1024,256]{1,0:T(8,128)(2,1)S(1)}, bf16[1024,256]{1,0:T(8,128)(2,1)}, u32[]{:S(2)}) copy-start(bf16[1024,256]{1,0:T(8,128)(2,1)} %own_ref) | copy-start | bytes 1572868
  22.4 30.6 %copy-start = (bf16[512,1024]{1,0:T(8,128)(2,1)S(1)}, bf16[512,1024]{1,0:T(8,128)(2,1)}, u32[]{:S(2)}) copy-start(bf16[512,1024]{1,0:T(8,128)(2,1)} %query_ref.1) | copy-start | bytes 3145732
  22.4 30.6 %copy-start.1 = (bf16[2,512,128]{2,1,0:T(8,128)(2,1)S(1)}, bf16[2,512,128]{2,1,0:T(8,128)(2,1)}, u32[]{:S(2)}) copy-start(bf16[2,512,128]{2,1,0:T(8,128)(2,1)} %keyval_ref.1) | copy-start | bytes 786436
  36.9 24.1 %all-to-all-start.2 = ((bf16[16,32,256]{2,1,0:T(8,128)(2,1)}), bf16[16,32,256]{2,1,0:T(8,128)(2,1)S(1)}, u32[]{:S(2)}, u32[]{:S(2)}) async-start(bf16[16,32,256]{2,1,0:T(8,128)(2,1)} %get-tuple-element.31), calls=%async_computation.2 | async-start | bytes 524288 | tf_op jit(solution)/shard_map/all_to_all | solution.py:478
  51.6 1.3 %collective-permute-start.2 = (bf16[2,256,128]{2,1,0:T(8,128)(2,1)S(1)}, bf16[2,256,128]{2,1,0:T(8,128)(2,1)S(1)}, u32[]{:S(2)}, u32[]{:S(2)}) collective-permute-start(bf16[2,256,128]{2,1,0:T(8,128)(2,1)S(1)} %get-tuple-element.32.own_ref), channel_id=1, source_target_pairs={{0,8},{8,0},{16,24},{24,16},{32,40},{40,32},{48,56},{56,48},{64,72... | collective-permute-start | bytes 393224 | tf_op jit(solution)/shard_map/ppermute | solution.py:481

commit v9 on v8

--- a/solution.py
+++ b/solution.py
@@ -18,7 +18,7 @@
 SHARE = 32
 SCALE = 1.0 / math.sqrt(HD)
 SCALE2 = SCALE * math.log2(math.e)
-AHEAD = 2
+AHEAD = 1
 masked_score = -1e30
 
 SEND_ROWS = HALF + STAT + PIECE

time: 62.1 us -> 62.1 us (level)
  transfers between devices with their start and end apart: 4 -> 4, of which waited for: 3 -> 3; matrix products, arithmetic and copies ran while one was open for 0% -> 0% of each run, Pallas kernels for 12% -> 13%
where the time goes in v9:
time: 62.1 us; the launch traced here: 61.6 us
  blocking collectives  26.8 us (43%)
  starting transfers between devices  18.6 us (30%)
  Pallas kernels  9.86 us (16%)
  waiting for transfers between devices  4.97 us (8%)
  between operations  0.7 us (1%)
  other arithmetic  0.67 us (1%)
    all_to_all x1, starting transfers between devices, on_device(): lax.all_to_all(shares, ('ctx', 'tp'), 0, 0, axis_index_groups=same_chip,...  14.8 us
    all_to_all x1, blocking collectives, on_device(): lax.all_to_all(send, 'ctx', 0, 0, axis_index_groups=same_core, tiled=True)  13.5 us
    all_to_all x1, blocking collectives, on_device(): lax.all_to_all(share, 'ctx', 0, 0, axis_index_groups=same_core, tiled=True)  13.3 us
    pallas_call x1, Pallas kernels, on_device(): pl.pallas_call(block_kernel, out_shape=shaped((2 * BLK, HEADS * HD), jnp....  4.4 us
    all_to_all x1, waiting for transfers between devices, on_device(): lax.all_to_all(shares, ('ctx', 'tp'), 0, 0, axis_index_groups=same_chip,...  3.62 us
    ppermute x1, starting transfers between devices, on_device(): other_keyvals = lax.ppermute(ctx_keyvals, 'ctx', core_swap)  3.33 us
    pallas_call x1, Pallas kernels, on_device(): pl.pallas_call(window_kernel, out_shape=(shaped((CHIPS, SEND_ROWS, HD), j...  2.2 us
  transfers between devices with their start and end apart: 4, of which 3 were waited for; matrix products, arithmetic and copies ran while one was open for 0% of the time, Pallas kernels for 13%

profile of v9, /device:TPU:1, one launch (start us, length us, event | category | flops | bytes accessed | tf_op | source)
XLA Modules:
  0.0 61.6 jit_solution(7898753358705685706)
XLA Ops:
  0.6 3.3 %collective-permute-start = (bf16[2,512,128]{2,1,0:T(8,128)(2,1)}, bf16[2,512,128]{2,1,0:T(8,128)(2,1)S(1)}, u32[]{:S(2)}, u32[]{:S(2)}) collective-permute-start(bf16[2,512,128]{2,1,0:T(8,128)(2,1)} %keyval_ref.1), channel_id=1, source_target_pairs={{0,8},{8,0},{16,24},{24,16},{32,40},{40,32},{48,56},{56,48},{64,72... | collective-permute-start | bytes 786440 | tf_op jit(solution)/shard_map/ppermute | solution.py:404
  4.0 1.2 %window_fetch.1 = (bf16[2,4,32,1024]{3,2,1,0:T(8,128)(2,1)S(1)}, bf16[2,512,128]{2,1,0:T(8,128)(2,1)S(1)}, bf16[2,256,128]{2,1,0:T(8,128)(2,1)S(1)}, f32[16,128]{1,0:T(8,128)S(1)}) custom-call(s32[64]{0:T(128)} %map_hbm.1, s32[2]{0:T(128)} %reach_hbm.1, bf16[2,4,2,32,1024]{4,3,2,1,0:T(8,128)(2,1)} %bitcast.5, bf16[2,512,128]{2,1,0:T(8,128)(2,1)} %keyval_ref.1, ...), custom_call_target="tpu_custom_call" | custom-call | flops 16777216 | bytes 2097152 | tf_op jit(solution)/shard_map/window_fetch/pallas_call | solution.py:406
  5.2 0.2 collective-permute-done.other_ref
  5.3 0.4 collective-permute-start.1
  5.7 2.2 %window_parts.1 = (bf16[16,176,128]{2,1,0:T(8,128)(2,1)S(1)}, f32[128,128]{1,0:T(8,128)S(1)}, f32[8,128]{1,0:T(8,128)S(1)}, f32[8,256,256]{2,1,0:T(8,128)}) custom-call(f32[16,128]{1,0:T(8,128)S(1)} %get-tuple-element.19.info_ref, bf16[2,4,32,1024]{3,2,1,0:T(8,128)(2,1)S(1)} %get-tuple-element.21.query_ref, ...), custom_call_target="tpu_custom_call" | custom-call | flops 536870912 | bytes 2097152 | tf_op jit(solution)/shard_map/window_parts/pallas_call | solution.py:431
  7.9 0.0 collective-permute-done.1.other_ref
  7.9 0.0 copy-start.2
  7.9 13.5 %all_to_all.15.got_ref = bf16[16,176,128]{2,1,0:T(8,128)(2,1)S(1)} all-to-all(bf16[16,176,128]{2,1,0:T(8,128)(2,1)S(1)} %get-tuple-element.27), channel_id=1, replica_groups={{0,16,32,48,64,80,96,112,128,144,160,176,192,208,224,240},{136,152,168,..., dimensions={0} | all-to-all | bytes 1441792 | tf_op jit(solution)/shard_map/all_to_all | solution.py:451
  21.4 0.9 %window_join.1 = bf16[16,160,128]{2,1,0:T(8,128)(2,1)S(1)} custom-call(f32[16,128]{1,0:T(8,128)S(1)} %get-tuple-element.19.info_ref, bf16[16,176,128]{2,1,0:T(8,128)(2,1)S(1)} %all_to_all.15.got_ref, f32[128,128]{1,0:T(8,128)S(1)} %get-tuple-element.28.mean_in, f32[8,128]{1,0:T(8,128)S(1)} %get-tuple-element.29.level_in, ...), custom_call_target="tpu_custom_call" | custom-call | flops 1048576 | bytes 1048576 | tf_op jit(solution)/shard_map/window_join/pallas_call | solution.py:452
  22.3 0.0 copy-start
  22.4 0.0 copy-start.1
  22.4 13.3 %all_to_all.16.rows_ref = bf16[16,160,128]{2,1,0:T(8,128)(2,1)S(1)} all-to-all(bf16[16,160,128]{2,1,0:T(8,128)(2,1)S(1)} %window_join.1), channel_id=1, replica_groups={{0,16,32,48,64,80,96,112,128,144,160,176,192,208,224,240},{136,152,168,..., dimensions={0} | all-to-all | bytes 1310720 | tf_op jit(solution)/shard_map/all_to_all | solution.py:465
  35.6 0.0 copy-done.2
  35.6 1.2 %project.1 = (bf16[16,32,256]{2,1,0:T(8,128)(2,1)}, bf16[2,256,128]{2,1,0:T(8,128)(2,1)S(1)}) custom-call(bf16[16,160,128]{2,1,0:T(8,128)(2,1)S(1)} %all_to_all.16.rows_ref, bf16[1024,256]{1,0:T(8,128)(2,1)S(1)} %copy-done.2, bf16[1024,256]{1,0:T(8,128)(2,1)S(1)} %collective-permute-done.1.other_ref), custom_call_target="tpu_custom_call" | custom-call | flops 268435456 | bytes 2097152 | tf_op jit(solution)/shard_map/project/pallas_call | solution.py:466
  36.8 14.8 %all-to-all-start.2 = ((bf16[16,32,256]{2,1,0:T(8,128)(2,1)}), bf16[16,32,256]{2,1,0:T(8,128)(2,1)S(1)}, u32[]{:S(2)}, u32[]{:S(2)}) async-start(bf16[16,32,256]{2,1,0:T(8,128)(2,1)} %get-tuple-element.31), calls=%async_computation.2 | async-start | bytes 524288 | tf_op jit(solution)/shard_map/all_to_all | solution.py:478
  51.6 0.2 collective-permute-start.2
  51.8 1.2 %collective-permute-done.2.other_ref = bf16[2,256,128]{2,1,0:T(8,128)(2,1)S(1)} collective-permute-done((bf16[2,256,128]{2,1,0:T(8,128)(2,1)S(1)}, bf16[2,256,128]{2,1,0:T(8,128)(2,1)S(1)}, u32[]{:S(2)}, u32[]{:S(2)}) %collective-permute-start.2) | collective-permute-done | bytes 131104 | tf_op jit(solution)/shard_map/ppermute | solution.py:481
  52.9 0.0 copy-done
  52.9 0.0 copy-done.1
  52.9 4.4 %block_attention.1 = bf16[512,1024]{1,0:T(8,128)(2,1)} custom-call(f32[16,128]{1,0:T(8,128)S(1)} %get-tuple-element.19.info_ref, bf16[512,1024]{1,0:T(8,128)(2,1)S(1)} %copy-done, bf16[2,512,128]{2,1,0:T(8,128)(2,1)S(1)} %copy-done.1, bf16[2,256,128]{2,1,0:T(8,128)(2,1)S(1)} %get-tuple-element.32.own_ref, ...), custom_call_target="tpu_custom_call" | custom-call | flops 1073741824 | bytes 4194304 | tf_op jit(solution)/shard_map/block_attention/pallas_call | solution.py:482
  57.3 3.6 %all-to-all-done.2 = bf16[16,32,256]{2,1,0:T(8,128)(2,1)S(1)} async-done(((bf16[16,32,256]{2,1,0:T(8,128)(2,1)}), bf16[16,32,256]{2,1,0:T(8,128)(2,1)S(1)}, u32[]{:S(2)}, u32[]{:S(2)}) %all-to-all-start.2) | async-done | bytes 262176 | tf_op jit(solution)/shard_map/all_to_all | solution.py:478
  61.0 0.7 %convert_reduce_fusion = f32[2,32,256]{2,1,0:T(8,128)} fusion(bf16[16,32,256]{2,1,0:T(8,128)(2,1)S(1)} %all-to-all-done.2), kind=kLoop, calls=%fused_computation | loop fusion | flops 245760 | bytes 327680 | tf_op jit(solution)/shard_map/reduce_sum | solution.py:505
Async XLA Ops:
  0.6 4.7 %collective-permute-start = (bf16[2,512,128]{2,1,0:T(8,128)(2,1)}, bf16[2,512,128]{2,1,0:T(8,128)(2,1)S(1)}, u32[]{:S(2)}, u32[]{:S(2)}) collective-permute-start(bf16[2,512,128]{2,1,0:T(8,128)(2,1)} %keyval_ref.1), channel_id=1, source_target_pairs={{0,8},{8,0},{16,24},{24,16},{32,40},{40,32},{48,56},{56,48},{64,72... | collective-permute-start | bytes 786440 | tf_op jit(solution)/shard_map/ppermute | solution.py:404
  5.3 2.6 %collective-permute-start.1 = (bf16[1024,256]{1,0:T(8,128)(2,1)}, bf16[1024,256]{1,0:T(8,128)(2,1)S(1)}, u32[]{:S(2)}, u32[]{:S(2)}) collective-permute-start(bf16[1024,256]{1,0:T(8,128)(2,1)} %own_ref), channel_id=1, source_target_pairs={{0,8},{8,0},{16,24},{24,16},{32,40},{40,32},{48,56},{56,48},{64,72... | collective-permute-start | bytes 1572872 | tf_op jit(solution)/shard_map/ppermute | solution.py:430
  7.9 27.7 %copy-start.2 = (bf16[1024,256]{1,0:T(8,128)(2,1)S(1)}, bf16[1024,256]{1,0:T(8,128)(2,1)}, u32[]{:S(2)}) copy-start(bf16[1024,256]{1,0:T(8,128)(2,1)} %own_ref) | copy-start | bytes 1572868
  22.3 30.6 %copy-start = (bf16[512,1024]{1,0:T(8,128)(2,1)S(1)}, bf16[512,1024]{1,0:T(8,128)(2,1)}, u32[]{:S(2)}) copy-start(bf16[512,1024]{1,0:T(8,128)(2,1)} %query_ref.1) | copy-start | bytes 3145732
  22.4 30.6 %copy-start.1 = (bf16[2,512,128]{2,1,0:T(8,128)(2,1)S(1)}, bf16[2,512,128]{2,1,0:T(8,128)(2,1)}, u32[]{:S(2)}) copy-start(bf16[2,512,128]{2,1,0:T(8,128)(2,1)} %keyval_ref.1) | copy-start | bytes 786436
  36.8 24.1 %all-to-all-start.2 = ((bf16[16,32,256]{2,1,0:T(8,128)(2,1)}), bf16[16,32,256]{2,1,0:T(8,128)(2,1)S(1)}, u32[]{:S(2)}, u32[]{:S(2)}) async-start(bf16[16,32,256]{2,1,0:T(8,128)(2,1)} %get-tuple-element.31), calls=%async_computation.2 | async-start | bytes 524288 | tf_op jit(solution)/shard_map/all_to_all | solution.py:478
  51.6 1.3 %collective-permute-start.2 = (bf16[2,256,128]{2,1,0:T(8,128)(2,1)S(1)}, bf16[2,256,128]{2,1,0:T(8,128)(2,1)S(1)}, u32[]{:S(2)}, u32[]{:S(2)}) collective-permute-start(bf16[2,256,128]{2,1,0:T(8,128)(2,1)S(1)} %get-tuple-element.32.own_ref), channel_id=1, source_target_pairs={{0,8},{8,0},{16,24},{24,16},{32,40},{40,32},{48,56},{56,48},{64,72... | collective-permute-start | bytes 393224 | tf_op jit(solution)/shard_map/ppermute | solution.py:481
